TPU v7x, 512 devices: a whole 4x4x16 slice. The times are simulated.
512 devices in a mesh: dp: 64 (over x_hi, z, core), mp: 8 (over x_lo, y).
Axes of the slice: x: 4 (x_hi: 2, x_lo: 2; x = x_hi * 2 + x_lo), y: 4, z: 16, core: 2. Of those that a mesh axis runs over, the one named last changes fastest.
Arguments:
- layer_input: bfloat16 [256, 256, 1536], P('dp', 'mp'), may hold values from -6 to 6
- in_weight: bfloat16 [1536, 4096], P('dp', 'mp'), may hold values from -0.15625 to 0.15625
- out_weight: bfloat16 [4096, 1536], P('mp'), may hold values from -0.09375 to 0.09375
- image_rest: bfloat16 [1792, 1536], P('dp'), may hold values from -2 to 2
- text_embed: bfloat16 [2048, 1536], P(('dp', 'mp')), may hold values from -2 to 2
- log_scale: float32 [1], replicated, may hold values from 3.4 to 4.6
- logit_bias: float32 [1], replicated, may hold values from -6 to -2
- loss_scale: float32 [1], replicated, may hold values from 2048 to 8192
Outputs:
- input_grad: bfloat16 [256, 256, 1536], P('dp', 'mp')
- in_weight_grad: bfloat16 [1536, 4096], P(None, 'mp')
- out_weight_grad: bfloat16 [4096, 1536], P('mp', 'dp')
- rest_grad: float32 [1792, 1536], P('dp')
- text_grad: float32 [2048, 1536], P(('dp', 'mp'))
All inputs are finite; a program needn't handle non-finite values.
Results may differ from a plain program's by a relative error of at most 0.025.
Values may be sent and summed in bfloat16 or wider, within the bound.
No kernel may reach another device: no remote copies, remote signals or barrier semaphores. Data moves between devices by JAX's collectives and lax.ppermute only.
A program may use at most 64 MiB of HBM per device.

v0:
```python
import math

import jax
import jax.numpy as jnp
from jax import lax
from jax.sharding import PartitionSpec as P

epsilon = 1e-06


def shifted(shard, axis, by):
    devices = lax.axis_size(axis)
    return lax.ppermute(shard, axis, [(i, (i + by) % devices) for i in range(devices)])


def gelu_slope(values):
    root = math.sqrt(2.0 / math.pi)
    inner = root * (values + 0.044715 * values * values * values)
    tangent = jnp.tanh(inner)
    return 0.5 * (1.0 + tangent) + 0.5 * values * (1.0 - tangent * tangent) * root * (
        1.0 + 3.0 * 0.044715 * values * values
    )


def unit_rows(values):
    norm_inv = lax.rsqrt(jnp.sum(values * values, -1, keepdims=True) + epsilon)
    return (values * norm_inv, norm_inv)


def unit_backward(grad_dir, unit_vals, norm_inv):
    return (grad_dir - unit_vals * jnp.sum(unit_vals * grad_dir, -1, keepdims=True)) * norm_inv


def body(
    layer_input, in_weight, out_weight, image_rest, text_embed, log_scale, logit_bias, loss_scale
):
    dp_count = lax.axis_size("dp")
    local_rows = layer_input.shape[0]
    width_model = layer_input.shape[2]
    full_in = lax.all_gather(in_weight, "dp", axis=0, tiled=True)
    inputs_f = layer_input.astype(jnp.float32)
    centered = inputs_f - jnp.mean(inputs_f, -1, keepdims=True)
    inv_std = lax.rsqrt(jnp.mean(centered * centered, -1, keepdims=True) + epsilon)
    standard = centered * inv_std
    gathered = lax.all_gather(standard.astype(jnp.bfloat16), "mp", axis=1, tiled=True)
    patches = gathered.shape[1]
    flat = gathered.reshape(-1, width_model)
    hidden = jnp.dot(flat, full_in, preferred_element_type=jnp.float32)
    hidden_width = hidden.shape[1]
    act_mean = jnp.mean(
        jax.nn.gelu(hidden, approximate=True).reshape(local_rows, patches, hidden_width), 1
    ).astype(jnp.bfloat16)
    part_pool = (
        jnp.dot(act_mean, out_weight, preferred_element_type=jnp.float32)
        + jnp.sum(inputs_f, 1) / patches
    )
    pooled = lax.psum(part_pool, "mp")
    images = jnp.concatenate([pooled, image_rest.astype(jnp.float32)], 0)
    image_count = images.shape[0]
    text_count = text_embed.shape[0]
    image_unit, image_inv = unit_rows(images)
    image_low = image_unit.astype(jnp.bfloat16)
    text_unit, text_inv = unit_rows(text_embed.astype(jnp.float32))
    text_low = text_unit.astype(jnp.bfloat16)
    scale_value = jnp.exp(log_scale[0])
    weight_coef = loss_scale[0] / (image_count * dp_count)

    def pair_terms(text_block):
        logits = (
            scale_value
            * jnp.einsum("id,jd->ij", image_low, text_block, preferred_element_type=jnp.float32)
            + logit_bias[0]
        )
        pair_weights = (weight_coef * jax.nn.sigmoid(logits)).astype(jnp.bfloat16)
        image_term = jnp.dot(pair_weights, text_block, preferred_element_type=jnp.float32)
        text_term = jnp.einsum(
            "ij,id->jd", pair_weights, image_low, preferred_element_type=jnp.float32
        )
        return (image_term, text_term)

    own_image, own_text = pair_terms(text_low)

    def forward_step(step_index, loop_state):
        text_block, partials, image_acc = loop_state
        text_block = shifted(text_block, "dp", 1)
        partials = shifted(partials, "dp", 1)
        image_term, text_term = pair_terms(text_block)
        return (text_block, partials + text_term, image_acc + image_term)

    _, partials, image_acc = lax.fori_loop(
        0, dp_count - 1, forward_step, (text_low, own_text, own_image)
    )
    text_acc = shifted(partials, "dp", 1)
    first_row = lax.axis_index("mp") * text_count
    zero_index = jnp.zeros((), jnp.int32)
    paired_texts = lax.dynamic_update_slice(
        jnp.zeros_like(images), text_low.astype(jnp.float32), (first_row, zero_index)
    )
    image_dir = scale_value * lax.psum(
        (image_acc - weight_coef * paired_texts).astype(jnp.bfloat16), "mp"
    ).astype(jnp.float32)
    paired_images = lax.dynamic_slice_in_dim(image_low, first_row, text_count, 0).astype(
        jnp.float32
    )
    text_dir = scale_value * (text_acc - weight_coef * paired_images)
    image_grad = unit_backward(image_dir, image_unit, image_inv)
    text_grad = unit_backward(text_dir, text_unit, text_inv)
    pool_grad = image_grad[:local_rows]
    rest_grad = image_grad[local_rows:]
    pool_low = pool_grad.astype(jnp.bfloat16)
    row_grad = (
        jnp.einsum("bd,fd->bf", pool_low, out_weight, preferred_element_type=jnp.float32) / patches
    )
    hidden_grad = (
        row_grad.reshape(local_rows, 1, hidden_width)
        * gelu_slope(hidden).reshape(local_rows, patches, hidden_width)
    ).astype(jnp.bfloat16)
    in_part = jnp.einsum(
        "rd,rf->df", flat, hidden_grad.reshape(-1, hidden_width), preferred_element_type=jnp.float32
    )
    in_weight_grad = lax.psum(in_part, "dp").astype(jnp.bfloat16)
    normed_grad = jnp.transpose(
        lax.psum_scatter(
            jnp.einsum(
                "bpf,df->pbd", hidden_grad, full_in, preferred_element_type=jnp.float32
            ).astype(jnp.bfloat16),
            "mp",
            scatter_dimension=0,
            tiled=True,
        ).astype(jnp.float32),
        (1, 0, 2),
    )
    input_grad = inv_std * (
        normed_grad
        - jnp.mean(normed_grad, -1, keepdims=True)
        - standard * jnp.mean(normed_grad * standard, -1, keepdims=True)
    )
    input_grad = (input_grad + pool_grad[:, None, :] / patches).astype(jnp.bfloat16)
    column_width = width_model // dp_count
    all_means, all_pools = (
        lax.all_gather(act_mean, "dp", axis=0, tiled=True),
        lax.all_gather(pool_low, "dp", axis=0, tiled=True),
    )
    first_col = lax.axis_index("dp") * column_width
    columns = lax.dynamic_slice_in_dim(all_pools, first_col, column_width, 1)
    out_weight_grad = jnp.einsum(
        "bf,bc->fc", all_means, columns, preferred_element_type=jnp.float32
    ).astype(jnp.bfloat16)
    return (input_grad, in_weight_grad, out_weight_grad, rest_grad, text_grad)


def solution(mesh):
    in_specs = (
        P("dp", "mp", None),
        P("dp", "mp"),
        P("mp", None),
        P("dp", None),
        P(("dp", "mp"), None),
        P(),
        P(),
        P(),
    )
    out_specs = (
        P("dp", "mp", None),
        P(None, "mp"),
        P("mp", "dp"),
        P("dp", None),
        P(("dp", "mp"), None),
    )
    return jax.shard_map(body, mesh=mesh, in_specs=in_specs, out_specs=out_specs, check_vma=False)
```

profile of v0, /device:TPU:1, one launch (start us, length us, event | category | flops | bytes accessed | tf_op | source)
XLA Modules:
  0.0 1473.0 jit_solution(14271402259236358683)
XLA Ops:
  14.8 144.3 %all-gather.7.cloned.1.call-done = bf16[1536,512]{1,0:T(8,128)(2,1)} async-done(((bf16[24,512]{1,0:T(8,128)(2,1)}), bf16[1536,512]{1,0:T(8,128)(2,1)}) %all-gather.7.cloned.1.call-update) | async-done | bytes 1572880 | tf_op jit(solution)/shard_map/all_gather | solution.py:40
  159.1 45.9 %all-gather.5.cloned.1.call-done = bf16[4,256,1536]{2,1,0:T(8,128)(2,1)} async-done(((bf16[4,32,1536]{2,1,0:T(8,128)(2,1)}), bf16[4,256,1536]{2,1,0:T(8,128)(2,1)}) %all-gather.5.cloned.1.call-update) | async-done | bytes 3145744 | tf_op jit(solution)/shard_map/all_gather | solution.py:45
  205.0 6.4 fusion.19
  212.4 25.7 %psum.21 = f32[4,1536]{1,0:T(4,128)S(1)} all-reduce(f32[4,1536]{1,0:T(4,128)S(1)} %convolution_add_fusion.2), channel_id=1, replica_groups=mesh['dp'=64,'mp'=8] {'mp'}, use_global_device_ids=true, to_apply=%region_5.0 | all-reduce | flops 6144 | bytes 49152 | tf_op jit(solution)/shard_map/psum | solution.py:57
  238.8 684.8 %while.14 = (s32[]{:T(128)}, bf16[4,1536]{1,0:T(4,128)(2,1)S(1)}, f32[4,1536]{1,0:T(4,128)S(1)}, f32[32,1536]{1,0:T(8,128)S(1)}, f32[]{:T(128)}, /*index=5*/f32[...) while((s32[]{:T(128)}, bf16[4,1536]{1,0:T(4,128)(2,1)S(1)}, f32[4,1536]{1,0:T(4,128)S(1)}, ...), condition=%wide.region_8.0_spmd, body=%wide.region_7.0_spmd.sunk | while | flops 1235842 | bytes 836537 | solution.py:90
  238.8 13.2 collective-permute-start
  279.1 4.9 collective-permute-done
  289.9 4.9 collective-permute-done
  300.7 4.9 collective-permute-done
  311.5 4.9 collective-permute-done
  322.3 4.9 collective-permute-done
  333.1 4.9 collective-permute-done
  343.9 4.9 collective-permute-done
  354.7 4.9 collective-permute-done
  365.5 4.9 collective-permute-done
  376.4 4.9 collective-permute-done
  387.2 4.9 collective-permute-done
  398.0 4.9 collective-permute-done
  408.8 4.9 collective-permute-done
  419.6 4.9 collective-permute-done
  430.4 4.9 collective-permute-done
  441.2 4.9 collective-permute-done
  452.0 4.9 collective-permute-done
  462.8 4.9 collective-permute-done
  473.6 4.9 collective-permute-done
  484.4 4.9 collective-permute-done
  495.2 4.9 collective-permute-done
  506.0 4.9 collective-permute-done
  516.8 4.9 collective-permute-done
  527.6 4.9 collective-permute-done
  538.4 4.9 collective-permute-done
  549.2 4.9 collective-permute-done
  560.1 4.9 collective-permute-done
  570.9 4.9 collective-permute-done
  581.7 4.9 collective-permute-done
  592.5 4.9 collective-permute-done
  603.3 4.9 collective-permute-done
  614.1 4.9 collective-permute-done
  776.2 4.9 collective-permute-done
  797.8 4.9 collective-permute-done
  819.4 4.9 collective-permute-done
  924.3 75.5 %all-reduce.3.cloned.1.call-done = bf16[32,1536]{1,0:T(8,128)(2,1)} async-done(((bf16[32,1536]{1,0:T(8,128)(2,1)}), bf16[32,1536]{1,0:T(8,128)(2,1)}) %all-reduce.3.cloned.1.call-update) | async-done | bytes 98320 | tf_op jit(solution)/shard_map/psum | solution.py:99
  1002.6 5.1 fusion.7
  1007.8 8.7 collective-permute-start.2
  1016.5 77.9 %all-gather = bf16[64,4,512]{2,1,0:T(4,128)(2,1)S(1)} all-gather(bf16[1,4,512]{2,1,0:T(4,128)(2,1)S(1)} %fusion.48), channel_id=1, replica_groups=mesh['dp'=64,'mp'=8] {'dp'}, dimensions={0}, use_global_device_ids=true | all-gather | bytes 266240 | tf_op jit(solution)/shard_map/all_gather | solution.py:141
  1096.0 6.1 convolution_bitcast_fusion
  1102.1 73.7 %all-gather.1 = bf16[64,4,1536]{2,1,0:T(4,128)(2,1)S(1)} all-gather(bf16[1,4,1536]{2,1,0:T(4,128)(2,1)S(1)} %fusion.47), channel_id=1, replica_groups=mesh['dp'=64,'mp'=8] {'dp'}, dimensions={0}, use_global_device_ids=true | all-gather | bytes 798720 | tf_op jit(solution)/shard_map/all_gather | solution.py:142
  1178.6 284.3 %all-reduce.4 = bf16[1536,512]{1,0:T(8,128)(2,1)} all-reduce(f32[1536,512]{1,0:T(8,128)} %convolution_bitcast_fusion), channel_id=1, replica_groups=mesh['dp'=64,'mp'=8] {'dp'}, use_global_device_ids=true, to_apply=%region_14.0 | all-reduce | flops 786432 | bytes 4718592 | tf_op jit(solution)/shard_map/psum | solution.py:121
  (522 shorter events, 517.1 us)
Async XLA Ops:
  7.2 151.9 %all-gather.7.cloned.1.call-start = ((), (), s32[]{:S(2)}) async-start(), calls=%async_computation.2 | async-start | bytes 1597440 | tf_op jit(solution)/shard_map/all_gather | solution.py:40
  7.9 197.0 %all-gather.5.cloned.1.call-start = ((), (), s32[]{:S(2)}) async-start(), calls=%async_computation.1 | async-start | bytes 3538944 | tf_op jit(solution)/shard_map/all_gather | solution.py:45
  12.5 987.4 %all-reduce.3.cloned.1.call-start = ((), (), s32[]{:S(2)}) async-start(), calls=%async_computation.3 | async-start | bytes 196608 | tf_op jit(solution)/shard_map/psum | solution.py:99
  238.8 15.2 %collective-permute-start = (bf16[4,1536]{1,0:T(4,128)(2,1)S(1)}, bf16[4,1536]{1,0:T(4,128)(2,1)S(1)}, u32[]{:S(2)}, u32[]{:S(2)}) collective-permute-start(bf16[4,1536]{1,0:T(4,128)(2,1)S(1)} %get-tuple-element.135), channel_id=1, source_target_pairs={{0,8},{8,16},{16,24},{24,32},{32,40},{40,48},{48,56},{56,64},{64,7... | collective-permute-start | bytes 36872 | tf_op jit(solution)/shard_map/while/body/eval_jaxpr/ppermute | solution.py:13
  277.2 8.8 collective-permute-start.1
  288.0 8.8 collective-permute-start.1
  298.8 8.8 collective-permute-start.1
  309.6 8.8 collective-permute-start.1
  331.2 8.8 collective-permute-start.1
  342.0 8.8 collective-permute-start.1
  352.8 8.8 collective-permute-start.1
  363.6 8.8 collective-permute-start.1
  374.4 8.8 collective-permute-start.1
  385.2 8.8 collective-permute-start.1
  396.0 8.8 collective-permute-start.1
  406.8 8.8 collective-permute-start.1
  428.5 8.8 collective-permute-start.1
  450.1 8.8 collective-permute-start.1
  471.7 8.8 collective-permute-start.1
  493.3 8.8 collective-permute-start.1
  514.9 8.8 collective-permute-start.1
  536.5 8.8 collective-permute-start.1
  547.3 8.8 collective-permute-start.1
  558.1 8.8 collective-permute-start.1
  568.9 8.8 collective-permute-start.1
  579.7 8.8 collective-permute-start.1
  590.5 8.8 collective-permute-start.1
  601.3 8.8 collective-permute-start.1
  612.2 8.8 collective-permute-start.1
  633.8 8.8 collective-permute-start.1
  655.4 8.8 collective-permute-start.1
  677.0 8.8 collective-permute-start.1
  698.6 8.8 collective-permute-start.1
  720.2 8.8 collective-permute-start.1
  741.8 8.8 collective-permute-start.1
  752.6 8.8 collective-permute-start.1
  763.4 8.8 collective-permute-start.1
  774.2 8.8 collective-permute-start.1
  785.0 8.8 collective-permute-start.1
  795.8 8.8 collective-permute-start.1
  806.7 8.8 collective-permute-start.1
  817.5 8.8 collective-permute-start.1
  839.1 8.8 collective-permute-start.1
  860.7 8.8 collective-permute-start.1
  882.3 8.8 collective-permute-start.1
  903.9 8.8 collective-permute-start.1
  924.3 538.7 %reduce-scatter.2.cloned.1.call-start = ((), (), s32[]{:S(2)}) async-start(), calls=%async_computation.4 | async-start | bytes 3538944 | tf_op jit(solution)/shard_map/reduce_scatter | solution.py:123
  1007.8 86.7 %collective-permute-start.2 = (f32[4,1536]{1,0:T(4,128)S(1)}, f32[4,1536]{1,0:T(4,128)S(1)}, u32[]{:S(2)}, u32[]{:S(2)}) collective-permute-start(f32[4,1536]{1,0:T(4,128)S(1)} %get-tuple-element.49), channel_id=1, source_target_pairs={{0,8},{8,16},{16,24},{24,32},{32,40},{40,48},{48,56},{56,64},{64,7... | collective-permute-start | bytes 73736 | tf_op jit(solution)/shard_map/ppermute | solution.py:13
  (88 other events, 1219.0 us)
Sparse Core Ops, SparseCore 0:
  11.3 147.6 all-gather.6
  161.7 43.1 all-gather.4
  924.4 75.4 all-reduce.2
  1007.9 55.5 reduce-scatter.1
where the time goes:
time: 1480 us; the launch traced here: 1470 us
  waiting for transfers between devices  621 us (42%)
  blocking collectives  462 us (31%)
  starting transfers between devices  264 us (18%)
  matrix products  93.9 us (6%)
  between operations  15.9 us (1%)
    ppermute x127, waiting for transfers between devices, shifted(): lax.ppermute(shard, axis, [(i, (i + by) % devices) for i in range(devices)])  354 us
    psum x1, blocking collectives, body(): in_weight_grad = lax.psum(in_part, 'dp').astype(jnp.bfloat16)  284 us
    ppermute x127, starting transfers between devices, shifted(): lax.ppermute(shard, axis, [(i, (i + by) % devices) for i in range(devices)])  264 us
    all_gather x1, waiting for transfers between devices, body(): full_in = lax.all_gather(in_weight, 'dp', axis=0, tiled=True)  144 us
    all_gather x1, blocking collectives, body(): lax.all_gather(act_mean, 'dp', axis=0, tiled=True)  77.9 us
    psum x1, waiting for transfers between devices, body(): lax.psum((image_acc - weight_coef * paired_texts).astype(jnp.bfloat16), '...  75.5 us
    all_gather x1, blocking collectives, body(): lax.all_gather(pool_low, 'dp', axis=0, tiled=True)  73.7 us
    dot_general x64, matrix products, pair_terms(): jnp.einsum('id,jd->ij', image_low, text_block, preferred_element_type=jnp...  49.3 us
  transfers between devices with their start and end apart: 131, of which 128 were waited for; matrix products, arithmetic and copies ran while one was open for 6% of the time, Pallas kernels for 0%

commit v1 on v0

v1 whole, which is shorter than its diff:
```python
import math

import jax
import jax.numpy as jnp
from jax import lax
from jax.sharding import PartitionSpec as P

epsilon = 1e-06
GROUPS = {
    "core": [[2 * k, 2 * k + 1] for k in range(32)],
    "x_hi": [[k, 32 + k] for k in range(32)],
    "z": [[32 * high + 2 * z + core for z in range(16)] for high in range(2) for core in range(2)],
}


def gelu_slope(values):
    root = math.sqrt(2.0 / math.pi)
    inner = root * (values + 0.044715 * values * values * values)
    tangent = jnp.tanh(inner)
    return 0.5 * (1.0 + tangent) + 0.5 * values * (1.0 - tangent * tangent) * root * (
        1.0 + 3.0 * 0.044715 * values * values
    )


def unit_rows(values):
    norm_inv = lax.rsqrt(jnp.sum(values * values, -1, keepdims=True) + epsilon)
    return (values * norm_inv, norm_inv)


def unit_backward(grad_dir, unit_vals, norm_inv):
    return (grad_dir - unit_vals * jnp.sum(unit_vals * grad_dir, -1, keepdims=True)) * norm_inv


def exchange(blocks, axis):
    if axis in GROUPS:
        return lax.all_to_all(blocks, "dp", 0, 0, axis_index_groups=GROUPS[axis], tiled=True)
    return lax.all_to_all(blocks, axis, 0, 0, tiled=True)


def spread(block, axis):
    count = len(GROUPS[axis][0]) if axis in GROUPS else lax.axis_size(axis)
    return exchange(jnp.broadcast_to(block[None], (count,) + block.shape), axis)


def sum_over(block, axis):
    return jnp.sum(spread(block, axis).astype(jnp.float32), 0)


def gather_dp(block):
    rows, width = block.shape
    block = lax.all_gather(block, "dp", axis=0, axis_index_groups=GROUPS["z"], tiled=True)
    block = spread(block, "x_hi")
    block = spread(block.reshape(-1, width), "core")
    return block.reshape(2, 2, 16, rows, width)


def scatter_sum_dp(parts):
    rows, width = parts.shape[-2:]
    for axis in ("core", "x_hi"):
        got = exchange(parts, axis)
        parts = jnp.sum(got.astype(jnp.float32), 0).astype(jnp.bfloat16)
    return jnp.sum(exchange(parts, "z").astype(jnp.float32), 0).reshape(rows, width)


def body(
    layer_input, in_weight, out_weight, image_rest, text_embed, log_scale, logit_bias, loss_scale
):
    local_rows, local_patches, width_model = layer_input.shape
    hidden_width = in_weight.shape[1]
    patches = local_patches * 8
    dp_count = 64
    in_rows = in_weight.shape[0]
    text_count = text_embed.shape[0]
    text_rows = text_count * width_model // hidden_width

    inputs_f = layer_input.astype(jnp.float32)
    centered = inputs_f - jnp.mean(inputs_f, -1, keepdims=True)
    inv_std = lax.rsqrt(jnp.mean(centered * centered, -1, keepdims=True) + epsilon)
    standard = centered * inv_std
    flat = lax.all_gather(
        standard.astype(jnp.bfloat16).reshape(-1, width_model), "mp", axis=0, tiled=True
    )
    token_shape = (8, local_rows, local_patches, hidden_width)

    text_unit, text_inv = unit_rows(text_embed.astype(jnp.float32))
    text_low = text_unit.astype(jnp.bfloat16)
    both = gather_dp(jnp.concatenate([in_weight, text_low.reshape(text_rows, hidden_width)], 0))
    full_in = jnp.transpose(both[:, :, :, :in_rows], (1, 2, 0, 3, 4)).reshape(
        width_model, hidden_width
    )
    texts = both[:, :, :, in_rows:].reshape(dp_count * text_count, width_model)

    hidden = jnp.dot(flat, full_in, preferred_element_type=jnp.float32)
    act_mean = jnp.mean(
        jax.nn.gelu(hidden, approximate=True).reshape(token_shape), (0, 2)
    ).astype(jnp.bfloat16)
    part_pool = (
        jnp.dot(act_mean, out_weight, preferred_element_type=jnp.float32)
        + jnp.sum(inputs_f, 1) / patches
    )
    pooled = sum_over(part_pool, "mp")
    images = jnp.concatenate([pooled, image_rest.astype(jnp.float32)], 0)
    image_count = images.shape[0]
    image_unit, image_inv = unit_rows(images)
    image_low = image_unit.astype(jnp.bfloat16)
    scale_value = jnp.exp(log_scale[0])
    weight_coef = loss_scale[0] / (image_count * dp_count)

    logits = (
        scale_value * jnp.einsum("id,jd->ij", image_low, texts, preferred_element_type=jnp.float32)
        + logit_bias[0]
    )
    pair_weights = (weight_coef * jax.nn.sigmoid(logits)).astype(jnp.bfloat16)
    image_acc = jnp.dot(pair_weights, texts, preferred_element_type=jnp.float32)
    text_part = jnp.einsum("ij,id->jd", pair_weights, image_low, preferred_element_type=jnp.float32)

    first_row = lax.axis_index("mp") * text_count
    zero_index = jnp.zeros((), jnp.int32)
    paired_texts = lax.dynamic_update_slice(
        jnp.zeros_like(images), text_low.astype(jnp.float32), (first_row, zero_index)
    )
    image_dir = scale_value * sum_over(
        (image_acc - weight_coef * paired_texts).astype(jnp.bfloat16), "mp"
    )
    image_grad = unit_backward(image_dir, image_unit, image_inv)
    pool_grad = image_grad[:local_rows]
    rest_grad = image_grad[local_rows:]
    pool_low = pool_grad.astype(jnp.bfloat16)
    row_grad = (
        jnp.einsum("bd,fd->bf", pool_low, out_weight, preferred_element_type=jnp.float32) / patches
    )
    hidden_grad = (
        row_grad.reshape(1, local_rows, 1, hidden_width) * gelu_slope(hidden).reshape(token_shape)
    ).astype(jnp.bfloat16).reshape(-1, hidden_width)
    normed_part = jnp.einsum(
        "rf,df->rd", hidden_grad, full_in, preferred_element_type=jnp.float32
    ).astype(jnp.bfloat16)
    normed_grad = (
        lax.psum_scatter(normed_part, "mp", scatter_dimension=0, tiled=True)
        .astype(jnp.float32)
        .reshape(layer_input.shape)
    )

    in_part = jnp.einsum(
        "rd,rf->df", flat, hidden_grad, preferred_element_type=jnp.float32
    ).astype(jnp.bfloat16)
    summed = scatter_sum_dp(
        jnp.concatenate(
            [
                in_part.reshape(2, 2, 16, in_rows, hidden_width),
                text_part.astype(jnp.bfloat16).reshape(2, 2, 16, text_rows, hidden_width),
            ],
            3,
        )
    )
    text_acc = summed[in_rows:].reshape(text_count, width_model)
    paired_images = lax.dynamic_slice_in_dim(image_low, first_row, text_count, 0).astype(
        jnp.float32
    )
    text_dir = scale_value * (text_acc - weight_coef * paired_images)
    text_grad = unit_backward(text_dir, text_unit, text_inv)

    column_width = width_model // dp_count
    columns = exchange(
        jnp.transpose(pool_low.reshape(local_rows, dp_count, column_width), (1, 0, 2)), "dp"
    )
    columns = jnp.transpose(
        columns.reshape(2, 16, 2, local_rows, column_width), (2, 0, 1, 3, 4)
    ).reshape(dp_count * local_rows, column_width)

    back = gather_dp(jnp.concatenate([summed[:in_rows].astype(jnp.bfloat16), act_mean], 0))
    in_weight_grad = back[:, :, :, :in_rows].reshape(width_model, hidden_width)
    all_means = back[:, :, :, in_rows:].reshape(dp_count * local_rows, hidden_width)
    out_weight_grad = jnp.einsum(
        "bf,bc->fc", all_means, columns, preferred_element_type=jnp.float32
    ).astype(jnp.bfloat16)

    input_grad = inv_std * (
        normed_grad
        - jnp.mean(normed_grad, -1, keepdims=True)
        - standard * jnp.mean(normed_grad * standard, -1, keepdims=True)
    )
    input_grad = (input_grad + pool_grad[:, None, :] / patches).astype(jnp.bfloat16)
    return (input_grad, in_weight_grad, out_weight_grad, rest_grad, text_grad)


def solution(mesh):
    in_specs = (
        P("dp", "mp", None),
        P("dp", "mp"),
        P("mp", None),
        P("dp", None),
        P(("dp", "mp"), None),
        P(),
        P(),
        P(),
    )
    out_specs = (
        P("dp", "mp", None),
        P(None, "mp"),
        P("mp", "dp"),
        P("dp", None),
        P(("dp", "mp"), None),
    )
    return jax.shard_map(body, mesh=mesh, in_specs=in_specs, out_specs=out_specs, check_vma=False)
```

time: 1480 us -> 330 us (0.22)
  waiting for transfers between devices: 621 us -> 43.3 us
  blocking collectives: 462 us -> 178 us
  starting transfers between devices: 264 us -> 23.4 us
  matrix products: 93.9 us -> 16.7 us
  local copies, waits for them, and re-layouts: 2.33 us -> 30.6 us
    ppermute x127 -> x0, waiting for transfers between devices: 354 us -> none  [shifted(): lax.ppermute(shard, axis, [(i, (i + by) % devices) for i in range(devices)])]
    psum x2 -> x0, blocking collectives: 310 us -> none  [the longest x1 284 us: body(): in_weight_grad = lax.psum(in_part, 'dp').astype(jnp.bfloat16)]
    ppermute x127 -> x0, starting transfers between devices: 264 us -> none  [shifted(): lax.ppermute(shard, axis, [(i, (i + by) % devices) for i in range(devices)])]
    all_gather x2 -> x1, waiting for transfers between devices: 190 us -> 0.02 us  [body(): lax.all_gather(standard.astype(jnp.bfloat16).reshape(-1, width_model), 'm...]
    all_to_all x0 -> x6, blocking collectives: none -> 116 us  [the longest x5 99.8 us: exchange(): lax.all_to_all(blocks, 'dp', 0, 0, axis_index_groups=GROUPS[axis], tiled=...]
    all_gather x2, blocking collectives: 152 us -> 62.1 us  [gather_dp(): lax.all_gather(block, 'dp', axis=0, axis_index_groups=GROUPS['z'], tiled=...]
    dot_general x194 -> x5, matrix products: 84.9 us -> 8.5 us  [the longest x1 4 us: body(): jnp.einsum('rd,rf->df', flat, hidden_grad, preferred_element_type=jnp.flo...]
    psum x1 -> x0, waiting for transfers between devices: 75.5 us -> none  [body(): lax.psum((image_acc - weight_coef * paired_texts).astype(jnp.bfloat16), '...]
  transfers between devices with their start and end apart: 131 -> 6, of which waited for: 128 -> 3; matrix products, arithmetic and copies ran while one was open for 6% -> 12% of each run, Pallas kernels for 0% -> 0%
where the time goes in v1:
time: 330 us; the launch traced here: 329 us
  blocking collectives  178 us (54%)
  waiting for transfers between devices  43.3 us (13%)
  local copies, waits for them, and re-layouts  30.6 us (9%)
  starting transfers between devices  23.4 us (7%)
  other arithmetic  20.2 us (6%)
  matrix products  16.7 us (5%)
  between operations  16.6 us (5%)
    all_to_all x5, blocking collectives, exchange(): lax.all_to_all(blocks, 'dp', 0, 0, axis_index_groups=GROUPS[axis], tiled=...  99.8 us
    all_gather x2, blocking collectives, gather_dp(): lax.all_gather(block, 'dp', axis=0, axis_index_groups=GROUPS['z'], tiled=...  62.1 us
    all_to_all x2, waiting for transfers between devices, exchange(): lax.all_to_all(blocks, 'dp', 0, 0, axis_index_groups=GROUPS[axis], tiled=...  33.7 us
    all_to_all x1, blocking collectives, exchange(): return lax.all_to_all(blocks, axis, 0, 0, tiled=True)  16.3 us
    all_to_all x2, starting transfers between devices, exchange(): lax.all_to_all(blocks, 'dp', 0, 0, axis_index_groups=GROUPS[axis], tiled=...  13.9 us
    all_to_all x2, local copies, waits for them, and re-layouts, exchange(): lax.all_to_all(blocks, 'dp', 0, 0, axis_index_groups=GROUPS[axis], tiled=...  11.1 us
    all_to_all x2, waiting for transfers between devices, exchange(): return lax.all_to_all(blocks, axis, 0, 0, tiled=True)  9.49 us
    all_to_all x2, starting transfers between devices, exchange(): return lax.all_to_all(blocks, axis, 0, 0, tiled=True)  9.42 us
  transfers between devices with their start and end apart: 6, of which 3 were waited for; matrix products, arithmetic and copies ran while one was open for 12% of the time, Pallas kernels for 0%

profile of v1, /device:TPU:1, one launch (start us, length us, event | category | flops | bytes accessed | tf_op | source)
XLA Modules:
  0.0 328.9 jit_solution(9024220834922010104)
XLA Ops:
  7.2 1.2 convert_reduce_fusion.3
  8.5 1.3 convert_reduce_fusion.2
  9.8 2.0 fusion.27
  11.8 0.8 fusion.43
  12.9 34.1 %all-gather = bf16[16,36,512]{2,1,0:T(8,128)(2,1)S(1)} all-gather(bf16[1,36,512]{2,1,0:T(8,128)(2,1)S(1)} %maximum_bitcast_fusion), channel_id=1, replica_groups={{0,16,32,48,64,80,96,112,128,144,160,176,192,208,224,240},{8,24,40,56,7..., dimensions={0}, use_global_device_ids=true | all-gather | bytes 626688 | tf_op jit(solution)/shard_map/all_gather | solution.py:51
  47.2 30.6 %all_to_all.50 = bf16[2,576,512]{2,1,0:T(8,128)(2,1)S(1)} all-to-all(bf16[2,576,512]{2,1,0:T(8,128)(2,1)S(1)} %broadcast_in_dim.18), channel_id=1, replica_groups={{0,256},{8,264},{16,272},{24,280},{32,288},{40,296},{48,304},{56,312},{..., dimensions={0} | all-to-all | bytes 2359296 | tf_op jit(solution)/shard_map/all_to_all | solution.py:36
  77.9 9.1 %all_to_all.51 = bf16[2,1152,512]{2,1,0:T(8,128)(2,1)S(1)} all-to-all(bf16[2,1152,512]{2,1,0:T(8,128)(2,1)S(1)} %broadcast_in_dim.20), channel_id=1, replica_groups={{0,8},{16,24},{32,40},{48,56},{64,72},{80,88},{96,104},{112,120},{128,1..., dimensions={0} | all-to-all | bytes 4718592 | tf_op jit(solution)/shard_map/all_to_all | solution.py:36
  87.0 9.2 %copy.64 = bf16[2,1152,512]{2,0,1:T(2,128)(2,1)S(1)} copy(bf16[2,1152,512]{2,1,0:T(8,128)(2,1)S(1)} %all_to_all.51) | data formatting | bytes 4718592 | tf_op jit(solution)/shard_map/all_to_all | solution.py:36
  96.2 1.4 copy-done.2
  97.7 1.6 slice_bitcast_fusion
  99.7 6.5 %fusion.7 = (f32[1024,512]{1,0:T(8,128)}, f32[1024,512]{1,0:T(8,128)}) fusion(bf16[1024,1536]{1,0:T(8,128)(2,1)} %all-gather.4.cloned.1.call-done, bf16[1536,512]{1,0:T(8,128)(2,1)S(1)} %bitcast.57), kind=kOutput, calls=%fused_computation.16 | convolution fusion | flops 1614807040 | bytes 8912896 | tf_op jit(solution)/shard_map/dot_general | solution.py:93
  106.2 1.8 reduce_sum.144
  108.3 0.7 broadcast_in_dim.21
  109.0 3.4 %all-to-all-start.2 = ((f32[8,4,1536]{2,1,0:T(4,128)}), f32[8,4,1536]{2,1,0:T(4,128)S(1)}, u32[]{:S(2)}, u32[]{:S(2)}) async-start(f32[8,4,1536]{2,1,0:T(4,128)} %broadcast_in_dim.21), calls=%async_computation.2 | async-start | bytes 393216 | tf_op jit(solution)/shard_map/all_to_all | solution.py:37
  114.5 1.7 slice.34
  116.2 1.2 copy.67
  117.4 1.6 reshape.115
  120.0 16.3 %all_to_all.52 = bf16[8,32,1536]{2,1,0:T(8,128)(2,1)S(1)} all-to-all(bf16[8,32,1536]{2,1,0:T(8,128)(2,1)S(1)} %broadcast_in_dim.23), channel_id=1, replica_groups=mesh['dp'=64,'mp'=8] {'mp'}, dimensions={0} | all-to-all | bytes 1572864 | tf_op jit(solution)/shard_map/all_to_all | solution.py:37
  136.8 0.7 copy-done.7
  138.0 1.3 fusion.14
  139.3 1.0 copy-done.9
  140.3 3.5 %convolution_convert_fusion = bf16[1024,1536]{1,0:T(8,128)(2,1)} fusion(bf16[1024,512]{1,0:T(8,128)(2,1)S(1)} %fusion.14, bf16[1536,512]{1,0:T(8,128)(2,1)S(1)} %bitcast.58), kind=kOutput, calls=%fused_computation | convolution fusion | flops 1612185600 | bytes 5767168 | tf_op jit(solution)/shard_map/rf,df->rd/dot_general | solution.py:135
  145.2 4.0 %convolution_convert_fusion.1 = bf16[1536,512]{1,0:T(8,128)(2,1)S(1)} fusion(bf16[1024,1536]{1,0:T(8,128)(2,1)} %all-gather.4.cloned.1.call-done, bf16[1024,512]{1,0:T(8,128)(2,1)} %copy-done.9), kind=kOutput, calls=%fused_computation.4 | convolution fusion | flops 1611399168 | bytes 5767168 | tf_op jit(solution)/shard_map/rd,rf->df/dot_general | solution.py:144
  149.9 8.5 %all_to_all.53 = bf16[2,2,16,36,512]{4,2,3,1,0:T(8,128)(2,1)} all-to-all(bf16[2,2,16,36,512]{4,2,3,1,0:T(8,128)(2,1)S(1)} %pad_maximum_fusion), channel_id=1, replica_groups={{0,8},{16,24},{32,40},{48,56},{64,72},{80,88},{96,104},{112,120},{128,1..., dimensions={0} | all-to-all | bytes 4718592 | tf_op jit(solution)/shard_map/all_to_all | solution.py:36
  158.5 3.5 %reduce_sum.152 = bf16[2,16,36,512]{3,1,2,0:T(8,128)(2,1)} reduce(bf16[2,2,16,36,512]{4,2,3,1,0:T(8,128)(2,1)} %all_to_all.53, bf16[]{:T(256)} %constant.48.clone.1), dimensions={0}, to_apply=%region_12.0 | reduce | flops 589824 | bytes 3538946 | tf_op jit(solution)/shard_map/reduce_sum | solution.py:61
  162.0 33.0 %all_to_all.54 = bf16[2,16,36,512]{3,1,2,0:T(8,128)(2,1)S(1)} all-to-all(bf16[2,16,36,512]{3,1,2,0:T(8,128)(2,1)} %reduce_sum.152), channel_id=1, replica_groups={{0,256},{8,264},{16,272},{24,280},{32,288},{40,296},{48,304},{56,312},{..., dimensions={0} | all-to-all | bytes 2359296 | tf_op jit(solution)/shard_map/all_to_all | solution.py:36
  195.3 1.2 copy.70
  196.5 10.3 %all-to-all-start.6 = ((bf16[16,36,512]{2,1,0:T(8,128)(2,1)}), bf16[16,36,512]{2,1,0:T(8,128)(2,1)S(1)}, u32[]{:S(2)}, u32[]{:S(2)}) async-start(bf16[16,36,512]{2,1,0:T(8,128)(2,1)} %copy.70), calls=%async_computation.7 | async-start | bytes 1310720 | tf_op jit(solution)/shard_map/all_to_all | solution.py:36
  206.8 0.7 slice.39
  207.7 0.7 copy.74
  208.3 26.3 %all-to-all-done.6 = bf16[16,36,512]{2,1,0:T(8,128)(2,1)S(1)} async-done(((bf16[16,36,512]{2,1,0:T(8,128)(2,1)}), bf16[16,36,512]{2,1,0:T(8,128)(2,1)S(1)}, u32[]{:S(2)}, u32[]{:S(2)}) %all-to-all-start.6) | async-done | bytes 589856 | tf_op jit(solution)/shard_map/all_to_all | solution.py:36
  234.8 28.1 %all-gather.1 = bf16[16,28,512]{2,1,0:T(8,128)(2,1)S(1)} all-gather(bf16[1,28,512]{2,1,0:T(8,128)(2,1)S(1)} %maximum_bitcast_fusion.1), channel_id=1, replica_groups={{0,16,32,48,64,80,96,112,128,144,160,176,192,208,224,240},{8,24,40,56,7..., dimensions={0}, use_global_device_ids=true | all-gather | bytes 487424 | tf_op jit(solution)/shard_map/all_gather | solution.py:51
  262.9 1.0 broadcast_in_dim.24
  263.9 3.6 %all-to-all-start.7 = ((bf16[2,448,512]{2,1,0:T(8,128)(2,1)}), bf16[2,448,512]{2,1,0:T(8,128)(2,1)S(1)}, u32[]{:S(2)}, u32[]{:S(2)}) async-start(bf16[2,448,512]{2,1,0:T(8,128)(2,1)} %broadcast_in_dim.24), calls=%async_computation.8 | async-start | bytes 1835008 | tf_op jit(solution)/shard_map/all_to_all | solution.py:36
  267.5 0.6 slice_multiply_fusion
  268.1 0.9 fusion.40
  269.1 7.4 %all-to-all-done.7 = bf16[2,448,512]{2,1,0:T(8,128)(2,1)S(1)} async-done(((bf16[2,448,512]{2,1,0:T(8,128)(2,1)}), bf16[2,448,512]{2,1,0:T(8,128)(2,1)S(1)}, u32[]{:S(2)}, u32[]{:S(2)}) %all-to-all-start.7) | async-done | bytes 917536 | tf_op jit(solution)/shard_map/all_to_all | solution.py:36
  276.6 18.6 %all_to_all.55 = bf16[2,896,512]{2,1,0:T(8,128)(2,1)S(1)} all-to-all(bf16[2,896,512]{2,1,0:T(8,128)(2,1)S(1)} %broadcast_in_dim.26), channel_id=1, replica_groups={{0,8},{16,24},{32,40},{48,56},{64,72},{80,88},{96,104},{112,120},{128,1..., dimensions={0} | all-to-all | bytes 3670016 | tf_op jit(solution)/shard_map/all_to_all | solution.py:36
  295.3 6.0 %all-to-all-start.9 = ((bf16[64,4,24]{2,1,0:T(4,128)(2,1)}), bf16[64,4,24]{2,1,0:T(4,128)(2,1)S(1)}, u32[]{:S(2)}, u32[]{:S(2)}) async-start(bf16[64,4,24]{2,1,0:T(4,128)(2,1)} %copy.74), calls=%async_computation.10 | async-start | bytes 131072 | tf_op jit(solution)/shard_map/all_to_all | solution.py:37
  301.3 1.4 fusion.42
  302.7 1.9 copy.71
  304.8 1.6 slice.37
  306.5 1.4 copy.72
  307.9 9.5 %all-to-all-done.9 = bf16[64,4,24]{2,1,0:T(4,128)(2,1)S(1)} async-done(((bf16[64,4,24]{2,1,0:T(4,128)(2,1)}), bf16[64,4,24]{2,1,0:T(4,128)(2,1)S(1)}, u32[]{:S(2)}, u32[]{:S(2)}) %all-to-all-start.9) | async-done | bytes 12320 | tf_op jit(solution)/shard_map/all_to_all | solution.py:37
  317.4 0.9 fusion.15
  318.2 1.2 convert_reduce_fusion.4
  319.5 1.1 convert_element_type.83
  321.0 1.1 fusion.32
  (93 shorter events, 6.7 us)
Async XLA Ops:
  7.2 100.9 %copy-start = (bf16[512,1536]{1,0:T(8,128)(2,1)S(1)}, bf16[512,1536]{1,0:T(8,128)(2,1)}, u32[]{:S(2)}) copy-start(bf16[512,1536]{1,0:T(8,128)(2,1)} %param.10) | copy-start | bytes 4718596
  7.2 5.5 %copy-start.11 = (bf16[4,1536]{1,0:T(4,128)(2,1)S(1)}, bf16[4,1536]{1,0:T(4,128)(2,1)}, u32[]{:S(2)}) copy-start(bf16[4,1536]{1,0:T(4,128)(2,1)} %param.12) | copy-start | bytes 36868
  7.2 5.6 %copy-start.18 = (bf16[24,512]{1,0:T(8,128)(2,1)S(1)}, bf16[24,512]{1,0:T(8,128)(2,1)}, u32[]{:S(2)}) copy-start(bf16[24,512]{1,0:T(8,128)(2,1)} %param.9) | copy-start | bytes 73732
  7.2 92.5 %all-gather.4.cloned.1.call-start = ((), (), s32[]{:S(2)}) async-start(), calls=%async_computation.11 | async-start | bytes 3538944 | tf_op jit(solution)/shard_map/all_gather | solution.py:80
  9.8 37.3 %copy-start.16 = (f32[4,32]{1,0:T(4,128)}, f32[4,32]{1,0:T(4,128)S(1)}, u32[]{:S(2)}) copy-start(f32[4,32]{1,0:T(4,128)S(1)} %add_rsqrt_fusion) | copy-start | bytes 1540
  12.7 65.1 %copy-start.19 = (f32[4]{0:T(128)}, f32[4]{0:T(128)S(1)}, u32[]{:S(2)}) copy-start(f32[4]{0:T(128)S(1)} %add_rsqrt_fusion.2) | copy-start | bytes 52
  96.2 1.4 copy-start.2
  99.6 6.6 %copy-start.5 = (bf16[2,16,2,24,512]{4,3,2,1,0:T(8,128)(2,1)}, bf16[2,16,2,24,512]{4,3,2,1,0:T(8,128)(2,1)S(1)}, u32[]{:S(2)}) copy-start(bf16[2,16,2,24,512]{4,3,2,1,0:T(8,128)(2,1)S(1)} %copy.65) | copy-start | bytes 4718596
  106.2 8.3 %copy-start.12 = (bf16[28,1536]{1,0:T(8,128)(2,1)S(1)}, bf16[28,1536]{1,0:T(8,128)(2,1)}, u32[]{:S(2)}) copy-start(bf16[28,1536]{1,0:T(8,128)(2,1)} %param.11) | copy-start | bytes 258052
  108.0 9.4 %copy-start.14 = (bf16[4,512]{1,0:T(4,128)(2,1)}, bf16[4,512]{1,0:T(4,128)(2,1)S(1)}, u32[]{:S(2)}) copy-start(bf16[4,512]{1,0:T(4,128)(2,1)S(1)} %multiply_convert_fusion.1) | copy-start | bytes 12292
  109.0 10.0 %all-to-all-start.2 = ((f32[8,4,1536]{2,1,0:T(4,128)}), f32[8,4,1536]{2,1,0:T(4,128)S(1)}, u32[]{:S(2)}, u32[]{:S(2)}) async-start(f32[8,4,1536]{2,1,0:T(4,128)} %broadcast_in_dim.21), calls=%async_computation.2 | async-start | bytes 393216 | tf_op jit(solution)/shard_map/all_to_all | solution.py:37
  112.4 205.8 %reduce-scatter.2.cloned.1.call-start = ((), (), s32[]{:S(2)}) async-start(), calls=%async_computation.12 | async-start | bytes 3538944 | tf_op jit(solution)/shard_map/reduce_scatter | solution.py:139
  119.3 24.6 %copy-start.10 = (bf16[32,1536]{1,0:T(8,128)(2,1)}, bf16[32,1536]{1,0:T(8,128)(2,1)S(1)}, u32[]{:S(2)}) copy-start(bf16[32,1536]{1,0:T(8,128)(2,1)S(1)} %multiply_convert_fusion) | copy-start | bytes 294916
  136.3 1.7 copy-start.4
  136.7 0.7 copy-start.7
  137.4 2.9 copy-start.6
  139.3 1.0 copy-start.9
  195.0 11.8 %copy-start.8 = (f32[32,1536]{1,0:T(8,128)S(1)}, f32[32,1536]{1,0:T(8,128)}, u32[]{:S(2)}) copy-start(f32[32,1536]{1,0:T(8,128)} %copy-done.7) | copy-start | bytes 589828
  195.3 39.4 %copy-start.15 = (bf16[4,512]{1,0:T(4,128)(2,1)S(1)}, bf16[4,512]{1,0:T(4,128)(2,1)}, u32[]{:S(2)}) copy-start(bf16[4,512]{1,0:T(4,128)(2,1)} %copy-done.14) | copy-start | bytes 12292
  196.5 38.1 %all-to-all-start.6 = ((bf16[16,36,512]{2,1,0:T(8,128)(2,1)}), bf16[16,36,512]{2,1,0:T(8,128)(2,1)S(1)}, u32[]{:S(2)}, u32[]{:S(2)}) async-start(bf16[16,36,512]{2,1,0:T(8,128)(2,1)} %copy.70), calls=%async_computation.7 | async-start | bytes 1310720 | tf_op jit(solution)/shard_map/all_to_all | solution.py:36
  262.8 5.3 %copy-start.20 = (f32[4]{0:T(128)S(1)}, f32[4]{0:T(128)}, u32[]{:S(2)}) copy-start(f32[4]{0:T(128)} %copy-done.19) | copy-start | bytes 52
  263.9 12.6 %all-to-all-start.7 = ((bf16[2,448,512]{2,1,0:T(8,128)(2,1)}), bf16[2,448,512]{2,1,0:T(8,128)(2,1)S(1)}, u32[]{:S(2)}, u32[]{:S(2)}) async-start(bf16[2,448,512]{2,1,0:T(8,128)(2,1)} %broadcast_in_dim.24), calls=%async_computation.8 | async-start | bytes 1835008 | tf_op jit(solution)/shard_map/all_to_all | solution.py:36
  276.6 24.7 %copy-start.21 = (f32[4]{0:T(128)S(1)}, f32[4]{0:T(128)}, u32[]{:S(2)}) copy-start(f32[4]{0:T(128)} %copy-done.19) | copy-start | bytes 52
  295.3 22.1 %all-to-all-start.9 = ((bf16[64,4,24]{2,1,0:T(4,128)(2,1)}), bf16[64,4,24]{2,1,0:T(4,128)(2,1)S(1)}, u32[]{:S(2)}, u32[]{:S(2)}) async-start(bf16[64,4,24]{2,1,0:T(4,128)(2,1)} %copy.74), calls=%async_computation.10 | async-start | bytes 131072 | tf_op jit(solution)/shard_map/all_to_all | solution.py:37
  306.4 14.2 %copy-start.1 = (bf16[4,32,1536]{2,1,0:T(8,128)(2,1)S(1)}, bf16[4,32,1536]{2,1,0:T(8,128)(2,1)}, u32[]{:S(2)}) copy-start(bf16[4,32,1536]{2,1,0:T(8,128)(2,1)} %param.8) | copy-start | bytes 1179652
  306.5 14.2 %copy-start.17 = (f32[4,32]{1,0:T(4,128)S(1)}, f32[4,32]{1,0:T(4,128)}, u32[]{:S(2)}) copy-start(f32[4,32]{1,0:T(4,128)} %copy-done.16) | copy-start | bytes 1540
  307.9 13.1 %copy-start.13 = (f32[4,1536]{1,0:T(4,128)S(1)}, f32[4,1536]{1,0:T(4,128)}, u32[]{:S(2)}) copy-start(f32[4,1536]{1,0:T(4,128)} %slice_multiply_fusion) | copy-start | bytes 73732
  318.2 2.7 copy-start.3
Sparse Core Ops, SparseCore 0:
  12.0 64.9 all-gather.3
  144.0 61.0 reduce-scatter.1

commit v2 on v1

v2 whole, which is shorter than its diff:
```python
import math

import jax
import jax.numpy as jnp
from jax import lax
from jax.sharding import PartitionSpec as P

epsilon = 1e-06


def dp_index(x_hi, z_hi, z_lo, core):
    return 32 * x_hi + 4 * z_hi + 2 * z_lo + core


TWO, EIGHT = range(2), range(8)
GROUPS = {
    "core": [[dp_index(x, h, l, c) for c in TWO] for x in TWO for h in EIGHT for l in TWO],
    "x_hi": [[dp_index(x, h, l, c) for x in TWO] for h in EIGHT for l in TWO for c in TWO],
    "z": [[dp_index(x, h, l, c) for h in EIGHT for l in TWO] for x in TWO for c in TWO],
    "z_hi": [[dp_index(x, h, l, c) for h in EIGHT] for x in TWO for l in TWO for c in TWO],
    "x_hi z_lo": [[dp_index(x, h, l, c) for x in TWO for l in TWO] for h in EIGHT for c in TWO],
    "core x_hi": [[dp_index(x, h, l, c) for c in TWO for x in TWO] for h in EIGHT for l in TWO],
}


def gelu_slope(values):
    root = math.sqrt(2.0 / math.pi)
    inner = root * (values + 0.044715 * values * values * values)
    tangent = jnp.tanh(inner)
    return 0.5 * (1.0 + tangent) + 0.5 * values * (1.0 - tangent * tangent) * root * (
        1.0 + 3.0 * 0.044715 * values * values
    )


def unit_rows(values):
    norm_inv = lax.rsqrt(jnp.sum(values * values, -1, keepdims=True) + epsilon)
    return (values * norm_inv, norm_inv)


def unit_backward(grad_dir, unit_vals, norm_inv):
    return (grad_dir - unit_vals * jnp.sum(unit_vals * grad_dir, -1, keepdims=True)) * norm_inv


def exchange(blocks, axis):
    if axis in GROUPS:
        return lax.all_to_all(blocks, "dp", 0, 0, axis_index_groups=GROUPS[axis], tiled=True)
    return lax.all_to_all(blocks, axis, 0, 0, tiled=True)


def spread(block, axis):
    count = len(GROUPS[axis][0]) if axis in GROUPS else lax.axis_size(axis)
    return exchange(jnp.broadcast_to(block[None], (count,) + block.shape), axis)


def sum_over(block, axis):
    return jnp.sum(spread(block, axis).astype(jnp.float32), 0)


def gather_z(block):
    return lax.all_gather(block, "dp", axis=0, axis_index_groups=GROUPS["z"], tiled=False)


def pad_rows(block, rows):
    return jnp.pad(block, [(0, 0)] * (block.ndim - 2) + [(0, rows - block.shape[-2]), (0, 0)])


def body(
    layer_input, in_weight, out_weight, image_rest, text_embed, log_scale, logit_bias, loss_scale
):
    local_rows, local_patches, width_model = layer_input.shape
    hidden_width = in_weight.shape[1]
    patches = local_patches * 8
    dp_count = 64
    in_rows = in_weight.shape[0]
    text_count = text_embed.shape[0]
    text_rows = text_count * width_model // hidden_width
    scale_value = jnp.exp(log_scale[0])
    image_count = local_rows + image_rest.shape[0]
    weight_coef = loss_scale[0] / (image_count * dp_count)

    inputs_f = layer_input.astype(jnp.float32)
    centered = inputs_f - jnp.mean(inputs_f, -1, keepdims=True)
    inv_std = lax.rsqrt(jnp.mean(centered * centered, -1, keepdims=True) + epsilon)
    standard = centered * inv_std
    normed = standard.astype(jnp.bfloat16).reshape(-1, width_model)
    in_weight, normed = lax.optimization_barrier((in_weight, normed))
    flat = lax.all_gather(normed, "mp", axis=0, tiled=True)
    token_shape = (8, local_rows, local_patches, hidden_width)

    text_unit, text_inv = unit_rows(text_embed.astype(jnp.float32))
    text_low = text_unit.astype(jnp.bfloat16)
    pair = spread(in_weight, "x_hi").reshape(2 * in_rows, hidden_width)
    both = gather_z(jnp.concatenate([pair, text_low.reshape(text_rows, hidden_width)], 0))
    full_in = spread(both[:, : 2 * in_rows], "core").reshape(2, 16, 2, in_rows, hidden_width)
    full_in = jnp.transpose(full_in, (2, 1, 0, 3, 4)).reshape(width_model, hidden_width)
    flat, late = lax.optimization_barrier((flat, both[:, 2 * in_rows :]))
    texts = spread(late, "core x_hi")

    first_row = lax.axis_index("mp") * text_count
    zero_index = jnp.zeros((), jnp.int32)
    paired_texts = lax.dynamic_update_slice(
        jnp.zeros((image_count, width_model), jnp.float32),
        text_low.astype(jnp.float32),
        (first_row, zero_index),
    )
    hidden = jnp.dot(flat, full_in, preferred_element_type=jnp.float32)
    act_mean = jnp.mean(
        jax.nn.gelu(hidden, approximate=True).reshape(token_shape), (0, 2)
    ).astype(jnp.bfloat16)
    act_mean, texts = lax.optimization_barrier((act_mean, texts))
    texts = jnp.transpose(texts.reshape(4, 8, 2, text_rows, hidden_width), (0, 2, 1, 3, 4))
    texts = texts.reshape(dp_count * text_count, width_model)
    part_pool = (
        jnp.dot(act_mean, out_weight, preferred_element_type=jnp.float32)
        + jnp.sum(inputs_f, 1) / patches
    )
    pooled = sum_over(part_pool, "mp")
    images = jnp.concatenate([pooled, image_rest.astype(jnp.float32)], 0)
    image_unit, image_inv = unit_rows(images)
    image_low = image_unit.astype(jnp.bfloat16)
    logits = (
        scale_value * jnp.einsum("id,jd->ij", image_low, texts, preferred_element_type=jnp.float32)
        + logit_bias[0]
    )
    pair_weights = (weight_coef * jax.nn.sigmoid(logits)).astype(jnp.bfloat16)
    image_acc = jnp.dot(pair_weights, texts, preferred_element_type=jnp.float32)
    image_dir = scale_value * sum_over(
        (image_acc - weight_coef * paired_texts).astype(jnp.bfloat16), "mp"
    )
    image_grad = unit_backward(image_dir, image_unit, image_inv)
    pool_grad = image_grad[:local_rows]
    rest_grad = image_grad[local_rows:]
    pool_low = pool_grad.astype(jnp.bfloat16)
    row_grad = (
        jnp.einsum("bd,fd->bf", pool_low, out_weight, preferred_element_type=jnp.float32) / patches
    )
    hidden_grad = (
        (row_grad.reshape(1, local_rows, 1, hidden_width) * gelu_slope(hidden).reshape(token_shape))
        .astype(jnp.bfloat16)
        .reshape(-1, hidden_width)
    )

    text_part = jnp.einsum("ij,id->jd", pair_weights, image_low, preferred_element_type=jnp.float32)
    in_part = jnp.einsum("rd,rf->df", flat, hidden_grad, preferred_element_type=jnp.float32)
    index = lax.axis_index("dp")
    place = index % 2 * 4 + index // 32 * 2 + index // 2 % 2
    column_width = width_model // dp_count
    columns = pool_low.reshape(local_rows, 2, 8, 2, 2, column_width)
    columns = jnp.transpose(columns, (4, 1, 3, 2, 0, 5)).reshape(2, 4, 8, local_rows, column_width)
    columns = jnp.concatenate([columns] * 8, -1)
    columns = jnp.where(jnp.arange(8 * column_width) // column_width == place, columns, 0)
    columns = jnp.pad(columns, [(0, 0)] * 4 + [(0, hidden_width - columns.shape[-1])])
    parts = jnp.concatenate(
        [
            in_part.astype(jnp.bfloat16).reshape(2, 4, 8, in_rows, hidden_width),
            text_part.astype(jnp.bfloat16).reshape(2, 4, 8, text_rows, hidden_width),
            columns,
        ],
        3,
    )
    for axis in ("core", "x_hi z_lo"):
        got = exchange(parts, axis).astype(jnp.float32)
        parts = sum(got[k] for k in range(got.shape[0])).astype(jnp.bfloat16)
    hidden_grad, parts = lax.optimization_barrier((hidden_grad, parts))
    normed_part = jnp.einsum(
        "rf,df->rd", hidden_grad, full_in, preferred_element_type=jnp.float32
    ).astype(jnp.bfloat16)
    normed_grad = (
        lax.psum_scatter(normed_part, "mp", scatter_dimension=0, tiled=True)
        .astype(jnp.float32)
        .reshape(layer_input.shape)
    )
    got = exchange(parts, "z_hi")
    summed = jnp.sum(got[:, : in_rows + text_rows].astype(jnp.float32), 0)
    back = jnp.concatenate([summed[:in_rows].astype(jnp.bfloat16), act_mean], 0)
    back = spread(spread(spread(pad_rows(back, 32), "z_hi"), "x_hi z_lo"), "core")
    back = back.reshape(dp_count, 32, hidden_width)
    in_weight_grad = back[:, :in_rows].reshape(width_model, hidden_width)
    all_means = back[:, in_rows : in_rows + local_rows].reshape(-1, hidden_width)
    columns = got[:, in_rows + text_rows :, : 8 * column_width]
    columns = columns.reshape(8, local_rows, 8, column_width)
    columns = jnp.transpose(columns, (2, 0, 1, 3)).reshape(-1, column_width)
    out_weight_grad = jnp.einsum(
        "bf,bc->fc", all_means, columns, preferred_element_type=jnp.float32
    ).astype(jnp.bfloat16)

    text_acc = summed[in_rows:].reshape(text_count, width_model)
    paired_images = lax.dynamic_slice_in_dim(image_low, first_row, text_count, 0).astype(
        jnp.float32
    )
    text_dir = scale_value * (text_acc - weight_coef * paired_images)
    text_grad = unit_backward(text_dir, text_unit, text_inv)

    input_grad = inv_std * (
        normed_grad
        - jnp.mean(normed_grad, -1, keepdims=True)
        - standard * jnp.mean(normed_grad * standard, -1, keepdims=True)
    )
    input_grad = (input_grad + pool_grad[:, None, :] / patches).astype(jnp.bfloat16)
    return (input_grad, in_weight_grad, out_weight_grad, rest_grad, text_grad)


def solution(mesh):
    in_specs = (
        P("dp", "mp", None),
        P("dp", "mp"),
        P("mp", None),
        P("dp", None),
        P(("dp", "mp"), None),
        P(),
        P(),
        P(),
    )
    out_specs = (
        P("dp", "mp", None),
        P(None, "mp"),
        P("mp", "dp"),
        P("dp", None),
        P(("dp", "mp"), None),
    )
    return jax.shard_map(body, mesh=mesh, in_specs=in_specs, out_specs=out_specs, check_vma=False)
```

time: 330 us -> 255 us (0.77)
  blocking collectives: 178 us -> 136 us
  waiting for transfers between devices: 43.3 us -> 25.2 us
  local copies, waits for them, and re-layouts: 30.6 us -> 18.1 us
    all_gather x2 -> x1, blocking collectives: 62.1 us -> 37.7 us  [gather_z(): lax.all_gather(block, 'dp', axis=0, axis_index_groups=GROUPS['z'], tiled=...]
    all_to_all x1 -> x0, blocking collectives: 16.3 us -> none  [exchange(): return lax.all_to_all(blocks, axis, 0, 0, tiled=True)]
    all_to_all x2 -> x3, waiting for transfers between devices: 33.7 us -> 18.5 us  [exchange(): lax.all_to_all(blocks, 'dp', 0, 0, axis_index_groups=GROUPS[axis], tiled=...]
    all_to_all x2 -> x0, local copies, waits for them, and re-layouts: 11.1 us -> none  [exchange(): lax.all_to_all(blocks, 'dp', 0, 0, axis_index_groups=GROUPS[axis], tiled=...]
    slice x6 -> x8, local copies, waits for them, and re-layouts: 6.1 us -> 1.43 us  [the longest x1 1.25 us: body(): in_weight_grad = back[:, :in_rows].reshape(width_model, hidden_width)]
    reduce_sum x3 -> x1, other arithmetic: 3.94 us -> 0.05 us  [body(): summed = jnp.sum(got[:, :in_rows + text_rows].astype(jnp.float32), 0)]
    broadcast_in_dim x6 -> x8, local copies, waits for them, and re-layouts: 2.13 us -> 5.56 us  [spread(): return exchange(jnp.broadcast_to(block[None], (count,) + block.shape), axis)]
    all_to_all x5 -> x6, blocking collectives: 99.8 us -> 98.7 us  [exchange(): lax.all_to_all(blocks, 'dp', 0, 0, axis_index_groups=GROUPS[axis], tiled=...]
  transfers between devices with their start and end apart: 6 -> 7, of which waited for: 3 -> 5; matrix products, arithmetic and copies ran while one was open for 12% -> 9% of each run, Pallas kernels for 0% -> 0%
where the time goes in v2:
time: 255 us; the launch traced here: 254 us
  blocking collectives  136 us (53%)
  waiting for transfers between devices  25.2 us (10%)
  starting transfers between devices  24.1 us (9%)
  local copies, waits for them, and re-layouts  18.1 us (7%)
  other arithmetic  17.1 us (7%)
  between operations  16.5 us (6%)
  matrix products  16.4 us (6%)
    all_to_all x6, blocking collectives, exchange(): lax.all_to_all(blocks, 'dp', 0, 0, axis_index_groups=GROUPS[axis], tiled=...  98.7 us
    all_gather x1, blocking collectives, gather_z(): lax.all_gather(block, 'dp', axis=0, axis_index_groups=GROUPS['z'], tiled=...  37.7 us
    all_to_all x3, waiting for transfers between devices, exchange(): lax.all_to_all(blocks, 'dp', 0, 0, axis_index_groups=GROUPS[axis], tiled=...  18.5 us
    all_to_all x3, starting transfers between devices, exchange(): lax.all_to_all(blocks, 'dp', 0, 0, axis_index_groups=GROUPS[axis], tiled=...  14.2 us
    all_to_all x2, starting transfers between devices, exchange(): return lax.all_to_all(blocks, axis, 0, 0, tiled=True)  9.82 us
    all_to_all x2, waiting for transfers between devices, exchange(): return lax.all_to_all(blocks, axis, 0, 0, tiled=True)  6.7 us
    dot_general x1, matrix products, body(): hidden = jnp.dot(flat, full_in, preferred_element_type=jnp.float32)  6.41 us
    broadcast_in_dim x8, local copies, waits for them, and re-layouts, spread(): return exchange(jnp.broadcast_to(block[None], (count,) + block.shape), axis)  5.56 us
  transfers between devices with their start and end apart: 7, of which 5 were waited for; matrix products, arithmetic and copies ran while one was open for 9% of the time, Pallas kernels for 0%

profile of v2, /device:TPU:1, one launch (start us, length us, event | category | flops | bytes accessed | tf_op | source)
XLA Modules:
  0.0 253.8 jit_solution(2598011455758539525)
XLA Ops:
  7.2 1.2 convert_reduce_fusion.2
  8.5 1.3 convert_reduce_fusion.1
  9.8 2.0 fusion.30
  11.8 1.4 broadcast_in_dim.24
  13.2 4.8 %all-to-all-start = ((bf16[2,24,512]{2,1,0:T(8,128)(2,1)}), bf16[2,24,512]{2,1,0:T(8,128)(2,1)S(1)}, u32[]{:S(2)}, u32[]{:S(2)}) async-start(bf16[2,24,512]{2,1,0:T(8,128)(2,1)} %broadcast_in_dim.24), calls=%async_computation | async-start | bytes 98304 | tf_op jit(solution)/shard_map/all_to_all | solution.py:46
  18.3 4.1 %all-to-all-done = bf16[2,24,512]{2,1,0:T(8,128)(2,1)S(1)} async-done(((bf16[2,24,512]{2,1,0:T(8,128)(2,1)}), bf16[2,24,512]{2,1,0:T(8,128)(2,1)S(1)}, u32[]{:S(2)}, u32[]{:S(2)}) %all-to-all-start) | async-done | bytes 49184 | tf_op jit(solution)/shard_map/all_to_all | solution.py:46
  22.4 37.7 %all-gather.1 = bf16[16,60,512]{2,1,0:T(8,128)(2,1)S(1)} all-gather(bf16[1,60,512]{2,1,0:T(8,128)(2,1)S(1)} %maximum_bitcast_fusion), channel_id=2, replica_groups={{0,16,32,48,64,80,96,112,128,144,160,176,192,208,224,240},{8,24,40,56,7..., dimensions={0}, use_global_device_ids=true | all-gather | bytes 1044480 | tf_op jit(solution)/shard_map/all_gather | solution.py:60
  60.4 0.7 copy-done.2
  61.1 10.5 %all_to_all.55 = bf16[2,16,48,512]{3,2,1,0:T(8,128)(2,1)S(1)} all-to-all(bf16[2,16,48,512]{3,2,1,0:T(8,128)(2,1)S(1)} %broadcast_in_dim.25), channel_id=1, replica_groups={{0,8},{16,24},{32,40},{48,56},{64,72},{80,88},{96,104},{112,120},{128,1..., dimensions={0} | all-to-all | bytes 3145728 | tf_op jit(solution)/shard_map/all_to_all | solution.py:46
  71.6 1.3 copy.44
  73.1 1.0 broadcast_in_dim.26
  74.0 3.8 %all-to-all-start.2 = ((bf16[4,16,12,512]{3,1,2,0:T(8,128)(2,1)}), bf16[4,16,12,512]{3,1,2,0:T(8,128)(2,1)S(1)}, u32[]{:S(2)}, u32[]{:S(2)}) async-start(bf16[4,16,12,512]{3,1,2,0:T(8,128)(2,1)} %broadcast_in_dim.26), calls=%async_computation.2 | async-start | bytes 1572864 | tf_op jit(solution)/shard_map/all_to_all | solution.py:46
  77.9 6.4 %fusion.10 = (f32[1024,512]{1,0:T(8,128)}, f32[1024,512]{1,0:T(8,128)}) fusion(bf16[1024,1536]{1,0:T(8,128)(2,1)} %all-gather.4.cloned.1.call-done, bf16[1536,512]{1,0:T(8,128)(2,1)} %bitcast.65), kind=kOutput, calls=%fused_computation.20 | convolution fusion | flops 1614807040 | bytes 8912896 | tf_op jit(solution)/shard_map/dot_general | solution.py:106
  84.3 1.8 reduce_sum.120
  86.1 4.1 %all-to-all-done.2 = bf16[4,16,12,512]{3,1,2,0:T(8,128)(2,1)S(1)} async-done(((bf16[4,16,12,512]{3,1,2,0:T(8,128)(2,1)}), bf16[4,16,12,512]{3,1,2,0:T(8,128)(2,1)S(1)}, u32[]{:S(2)}, u32[]{:S(2)}) %all-to-all-start.2) | async-done | bytes 786464 | tf_op jit(solution)/shard_map/all_to_all | solution.py:46
  90.5 0.7 broadcast_in_dim.27
  91.2 5.0 %all-to-all-start.3 = ((f32[8,4,1536]{2,1,0:T(4,128)}), f32[8,4,1536]{2,1,0:T(4,128)S(1)}, u32[]{:S(2)}, u32[]{:S(2)}) async-start(f32[8,4,1536]{2,1,0:T(4,128)} %broadcast_in_dim.27), calls=%async_computation.3 | async-start | bytes 393216 | tf_op jit(solution)/shard_map/all_to_all | solution.py:47
  98.2 0.6 copy.47
  98.8 1.2 copy.48
  100.1 1.6 reshape.138
  102.9 1.0 broadcast_in_dim.31
  103.9 4.8 %all-to-all-start.4 = ((bf16[8,32,1536]{2,1,0:T(8,128)(2,1)}), bf16[8,32,1536]{2,1,0:T(8,128)(2,1)}, u32[]{:S(2)}, u32[]{:S(2)}) async-start(bf16[8,32,1536]{2,1,0:T(8,128)(2,1)} %broadcast_in_dim.31), calls=%async_computation.4 | async-start | bytes 1572864 | tf_op jit(solution)/shard_map/all_to_all | solution.py:47
  108.8 1.3 convolution_convert_fusion.2
  110.1 1.5 reshape.140
  111.6 6.4 %all-to-all-done.4 = bf16[8,32,1536]{2,1,0:T(8,128)(2,1)} async-done(((bf16[8,32,1536]{2,1,0:T(8,128)(2,1)}), bf16[8,32,1536]{2,1,0:T(8,128)(2,1)}, u32[]{:S(2)}, u32[]{:S(2)}) %all-to-all-start.4) | async-done | bytes 786464 | tf_op jit(solution)/shard_map/all_to_all | solution.py:47
  118.0 1.4 convert_reduce_fusion
  119.7 0.5 convolution_multiply_fusion.1
  120.3 1.3 fusion.17
  121.6 1.0 copy-done.6
  122.6 3.0 %convolution_convert_fusion.1 = bf16[1536,512]{1,0:T(8,128)(2,1)} fusion(bf16[1024,1536]{1,0:T(8,128)(2,1)S(1)} %copy-done.10, bf16[1024,512]{1,0:T(8,128)(2,1)S(1)} %fusion.17), kind=kOutput, calls=%fused_computation.6 | convolution fusion | flops 1611399168 | bytes 5767168 | tf_op jit(solution)/shard_map/rd,rf->df/dot_general | solution.py:144
  126.0 1.8 fusion.1
  127.8 9.3 %all_to_all.56 = bf16[2,4,8,40,512]{4,3,2,1,0:T(8,128)(2,1)S(1)} all-to-all(bf16[2,4,8,40,512]{4,3,2,1,0:T(8,128)(2,1)S(1)} %fusion.1), channel_id=1, replica_groups={{0,8},{16,24},{32,40},{48,56},{64,72},{80,88},{96,104},{112,120},{128,1..., dimensions={0} | all-to-all | bytes 5242880 | tf_op jit(solution)/shard_map/all_to_all | solution.py:46
  137.1 0.7 convert_element_type.104
  138.3 20.3 %all_to_all.57 = bf16[4,8,40,512]{3,2,1,0:T(8,128)(2,1)S(1)} all-to-all(bf16[4,8,40,512]{3,2,1,0:T(8,128)(2,1)S(1)} %fusion.18), channel_id=1, replica_groups={{0,16,256,272},{8,24,264,280},{32,48,288,304},{40,56,296,312},{64,80,32..., dimensions={0} | all-to-all | bytes 2621440 | tf_op jit(solution)/shard_map/all_to_all | solution.py:46
  159.2 1.2 copy-done.5
  160.6 3.5 %convolution_convert_fusion = bf16[1024,1536]{1,0:T(8,128)(2,1)} fusion(bf16[1024,512]{1,0:T(8,128)(2,1)S(1)} %copy-done.7, bf16[1536,512]{1,0:T(8,128)(2,1)S(1)} %bitcast.66), kind=kOutput, calls=%fused_computation.2 | convolution fusion | flops 1612185600 | bytes 5767168 | tf_op jit(solution)/shard_map/rf,df->rd/dot_general | solution.py:165
  164.2 24.2 %all_to_all.58 = bf16[8,40,512]{2,1,0:T(8,128)(2,1)S(1)} all-to-all(bf16[8,40,512]{2,1,0:T(8,128)(2,1)S(1)} %fusion.38), channel_id=1, replica_groups={{0,32,64,96,128,160,192,224},{8,40,72,104,136,168,200,232},{16,48,80,11..., dimensions={0} | all-to-all | bytes 655360 | tf_op jit(solution)/shard_map/all_to_all | solution.py:46
  188.5 25.4 %all_to_all.59 = bf16[8,32,512]{2,1,0:T(8,128)(2,1)S(1)} all-to-all(bf16[8,32,512]{2,1,0:T(8,128)(2,1)S(1)} %broadcast_in_dim.34), channel_id=1, replica_groups={{0,32,64,96,128,160,192,224},{8,40,72,104,136,168,200,232},{16,48,80,11..., dimensions={0} | all-to-all | bytes 524288 | tf_op jit(solution)/shard_map/all_to_all | solution.py:46
  213.9 1.1 broadcast_in_dim.35
  215.0 5.5 %all-to-all-start.9 = ((bf16[4,8,32,512]{3,2,1,0:T(8,128)(2,1)}), bf16[4,8,32,512]{3,2,1,0:T(8,128)(2,1)S(1)}, u32[]{:S(2)}, u32[]{:S(2)}) async-start(bf16[4,8,32,512]{3,2,1,0:T(8,128)(2,1)} %broadcast_in_dim.35), calls=%async_computation.10 | async-start | bytes 2097152 | tf_op jit(solution)/shard_map/all_to_all | solution.py:46
  220.5 0.7 slice.79
  221.6 0.7 fusion.47
  222.3 10.3 %all-to-all-done.9 = bf16[4,8,32,512]{3,2,1,0:T(8,128)(2,1)S(1)} async-done(((bf16[4,8,32,512]{3,2,1,0:T(8,128)(2,1)}), bf16[4,8,32,512]{3,2,1,0:T(8,128)(2,1)S(1)}, u32[]{:S(2)}, u32[]{:S(2)}) %all-to-all-start.9) | async-done | bytes 1048608 | tf_op jit(solution)/shard_map/all_to_all | solution.py:46
  232.9 9.0 %all_to_all.60 = bf16[2,4,8,32,512]{4,3,2,1,0:T(8,128)(2,1)S(1)} all-to-all(bf16[2,4,8,32,512]{4,3,2,1,0:T(8,128)(2,1)S(1)} %broadcast_in_dim.36), channel_id=1, replica_groups={{0,8},{16,24},{32,40},{48,56},{64,72},{80,88},{96,104},{112,120},{128,1..., dimensions={0} | all-to-all | bytes 4194304 | tf_op jit(solution)/shard_map/all_to_all | solution.py:46
  241.9 1.3 slice.76
  243.3 0.8 convolution_convert_fusion.3
  244.1 1.1 convert_element_type.111
  245.8 1.1 fusion.35
  (80 shorter events, 5.8 us)
Async XLA Ops:
  7.2 83.0 %copy-start = (bf16[512,1536]{1,0:T(8,128)(2,1)S(1)}, bf16[512,1536]{1,0:T(8,128)(2,1)}, u32[]{:S(2)}) copy-start(bf16[512,1536]{1,0:T(8,128)(2,1)} %param.10) | copy-start | bytes 4718596
  7.2 10.8 %copy-start.8 = (bf16[4,1536]{1,0:T(4,128)(2,1)S(1)}, bf16[4,1536]{1,0:T(4,128)(2,1)}, u32[]{:S(2)}) copy-start(bf16[4,1536]{1,0:T(4,128)(2,1)} %param.12) | copy-start | bytes 36868
  7.2 65.8 %all-gather.4.cloned.1.call-start = ((), (), s32[]{:S(2)}) async-start(), calls=%async_computation.12 | async-start | bytes 3538944 | tf_op jit(solution)/shard_map/all_gather | solution.py:87
  13.2 9.2 %all-to-all-start = ((bf16[2,24,512]{2,1,0:T(8,128)(2,1)}), bf16[2,24,512]{2,1,0:T(8,128)(2,1)S(1)}, u32[]{:S(2)}, u32[]{:S(2)}) async-start(bf16[2,24,512]{2,1,0:T(8,128)(2,1)} %broadcast_in_dim.24), calls=%async_computation | async-start | bytes 98304 | tf_op jit(solution)/shard_map/all_to_all | solution.py:46
  60.1 1.0 copy-start.2
  71.6 1.3 slice-start
  74.0 16.1 %all-to-all-start.2 = ((bf16[4,16,12,512]{3,1,2,0:T(8,128)(2,1)}), bf16[4,16,12,512]{3,1,2,0:T(8,128)(2,1)S(1)}, u32[]{:S(2)}, u32[]{:S(2)}) async-start(bf16[4,16,12,512]{3,1,2,0:T(8,128)(2,1)} %broadcast_in_dim.26), calls=%async_computation.2 | async-start | bytes 1572864 | tf_op jit(solution)/shard_map/all_to_all | solution.py:46
  84.3 11.9 %copy-start.9 = (bf16[28,1536]{1,0:T(8,128)(2,1)S(1)}, bf16[28,1536]{1,0:T(8,128)(2,1)}, u32[]{:S(2)}) copy-start(bf16[28,1536]{1,0:T(8,128)(2,1)} %param.11) | copy-start | bytes 258052
  91.2 10.8 %all-to-all-start.3 = ((f32[8,4,1536]{2,1,0:T(4,128)}), f32[8,4,1536]{2,1,0:T(4,128)S(1)}, u32[]{:S(2)}, u32[]{:S(2)}) async-start(f32[8,4,1536]{2,1,0:T(4,128)} %broadcast_in_dim.27), calls=%async_computation.3 | async-start | bytes 393216 | tf_op jit(solution)/shard_map/all_to_all | solution.py:47
  103.9 14.1 %all-to-all-start.4 = ((bf16[8,32,1536]{2,1,0:T(8,128)(2,1)}), bf16[8,32,1536]{2,1,0:T(8,128)(2,1)}, u32[]{:S(2)}, u32[]{:S(2)}) async-start(bf16[8,32,1536]{2,1,0:T(8,128)(2,1)} %broadcast_in_dim.31), calls=%async_computation.4 | async-start | bytes 1572864 | tf_op jit(solution)/shard_map/all_to_all | solution.py:47
  108.7 135.4 %reduce-scatter.2.cloned.1.call-start = ((), (), s32[]{:S(2)}) async-start(), calls=%async_computation.13 | async-start | bytes 3538944 | tf_op jit(solution)/shard_map/reduce_scatter | solution.py:169
  118.0 2.3 copy-start.4
  119.7 2.9 %copy-start.10 = (bf16[1024,1536]{1,0:T(8,128)(2,1)S(1)}, bf16[1024,1536]{1,0:T(8,128)(2,1)}, u32[]{:S(2)}) copy-start(bf16[1024,1536]{1,0:T(8,128)(2,1)} %all-gather.4.cloned.1.call-done) | copy-start | bytes 9437188
  121.6 1.0 copy-start.6
  158.9 1.4 copy-start.5
  158.9 1.7 copy-start.7
  215.0 17.6 %all-to-all-start.9 = ((bf16[4,8,32,512]{3,2,1,0:T(8,128)(2,1)}), bf16[4,8,32,512]{3,2,1,0:T(8,128)(2,1)S(1)}, u32[]{:S(2)}, u32[]{:S(2)}) async-start(bf16[4,8,32,512]{3,2,1,0:T(8,128)(2,1)} %broadcast_in_dim.35), calls=%async_computation.10 | async-start | bytes 2097152 | tf_op jit(solution)/shard_map/all_to_all | solution.py:46
  241.9 3.3 %copy-start.1 = (bf16[4,32,1536]{2,1,0:T(8,128)(2,1)S(1)}, bf16[4,32,1536]{2,1,0:T(8,128)(2,1)}, u32[]{:S(2)}) copy-start(bf16[4,32,1536]{2,1,0:T(8,128)(2,1)} %param.8) | copy-start | bytes 1179652
  244.1 1.5 copy-start.3
Sparse Core Ops, SparseCore 0:
  11.9 54.5 all-gather.3
  164.3 44.7 reduce-scatter.1

commit v3 on v2

--- a/solution.py
+++ b/solution.py
@@ -50,6 +50,13 @@
 def spread(block, axis):
     count = len(GROUPS[axis][0]) if axis in GROUPS else lax.axis_size(axis)
     return exchange(jnp.broadcast_to(block[None], (count,) + block.shape), axis)
+
+
+def pair(block, axis):
+    index = lax.axis_index("dp")
+    first = (index % 2 if axis == "core" else index // 32) == 0
+    other = lax.ppermute(block, "dp", [p for a, b in GROUPS[axis] for p in ((a, b), (b, a))])
+    return jnp.stack([jnp.where(first, block, other), jnp.where(first, other, block)])
 
 
 def sum_over(block, axis):
@@ -83,18 +90,18 @@
     inv_std = lax.rsqrt(jnp.mean(centered * centered, -1, keepdims=True) + epsilon)
     standard = centered * inv_std
     normed = standard.astype(jnp.bfloat16).reshape(-1, width_model)
-    in_weight, normed = lax.optimization_barrier((in_weight, normed))
-    flat = lax.all_gather(normed, "mp", axis=0, tiled=True)
     token_shape = (8, local_rows, local_patches, hidden_width)
 
     text_unit, text_inv = unit_rows(text_embed.astype(jnp.float32))
     text_low = text_unit.astype(jnp.bfloat16)
-    pair = spread(in_weight, "x_hi").reshape(2 * in_rows, hidden_width)
-    both = gather_z(jnp.concatenate([pair, text_low.reshape(text_rows, hidden_width)], 0))
-    full_in = spread(both[:, : 2 * in_rows], "core").reshape(2, 16, 2, in_rows, hidden_width)
+    in_weight, normed = lax.optimization_barrier((in_weight, normed))
+    near = pair(in_weight, "x_hi").reshape(2 * in_rows, hidden_width)
+    near = jnp.concatenate([near, text_low.reshape(text_rows, hidden_width)], 0)
+    flat = lax.all_gather(normed, "mp", axis=0, tiled=True)
+    both = gather_z(near)
+    full_in = pair(both[:, : 2 * in_rows], "core").reshape(2, 16, 2, in_rows, hidden_width)
     full_in = jnp.transpose(full_in, (2, 1, 0, 3, 4)).reshape(width_model, hidden_width)
-    flat, late = lax.optimization_barrier((flat, both[:, 2 * in_rows :]))
-    texts = spread(late, "core x_hi")
+    texts = spread(both[:, 2 * in_rows :], "core x_hi")
 
     first_row = lax.axis_index("mp") * text_count
     zero_index = jnp.zeros((), jnp.int32)
@@ -161,10 +168,10 @@
     for axis in ("core", "x_hi z_lo"):
         got = exchange(parts, axis).astype(jnp.float32)
         parts = sum(got[k] for k in range(got.shape[0])).astype(jnp.bfloat16)
-    hidden_grad, parts = lax.optimization_barrier((hidden_grad, parts))
     normed_part = jnp.einsum(
         "rf,df->rd", hidden_grad, full_in, preferred_element_type=jnp.float32
     ).astype(jnp.bfloat16)
+    normed_part, parts = lax.optimization_barrier((normed_part, parts))
     normed_grad = (
         lax.psum_scatter(normed_part, "mp", scatter_dimension=0, tiled=True)
         .astype(jnp.float32)
@@ -173,7 +180,15 @@
     got = exchange(parts, "z_hi")
     summed = jnp.sum(got[:, : in_rows + text_rows].astype(jnp.float32), 0)
     back = jnp.concatenate([summed[:in_rows].astype(jnp.bfloat16), act_mean], 0)
-    back = spread(spread(spread(pad_rows(back, 32), "z_hi"), "x_hi z_lo"), "core")
+    input_grad = inv_std * (
+        normed_grad
+        - jnp.mean(normed_grad, -1, keepdims=True)
+        - standard * jnp.mean(normed_grad * standard, -1, keepdims=True)
+    )
+    input_grad = (input_grad + pool_grad[:, None, :] / patches).astype(jnp.bfloat16)
+    back = spread(spread(pad_rows(back, 32), "z_hi"), "x_hi z_lo")
+    back, input_grad = lax.optimization_barrier((back, input_grad))
+    back = pair(back, "core")
     back = back.reshape(dp_count, 32, hidden_width)
     in_weight_grad = back[:, :in_rows].reshape(width_model, hidden_width)
     all_means = back[:, in_rows : in_rows + local_rows].reshape(-1, hidden_width)
@@ -191,12 +206,6 @@
     text_dir = scale_value * (text_acc - weight_coef * paired_images)
     text_grad = unit_backward(text_dir, text_unit, text_inv)
 
-    input_grad = inv_std * (
-        normed_grad
-        - jnp.mean(normed_grad, -1, keepdims=True)
-        - standard * jnp.mean(normed_grad * standard, -1, keepdims=True)
-    )
-    input_grad = (input_grad + pool_grad[:, None, :] / patches).astype(jnp.bfloat16)
     return (input_grad, in_weight_grad, out_weight_grad, rest_grad, text_grad)
 
 

time: 255 us -> 245 us (0.961)
  blocking collectives: 136 us -> 95.6 us
  starting transfers between devices: 24.1 us -> 42.2 us
  other arithmetic: 17.1 us -> 28.3 us
    all_to_all x6 -> x3, blocking collectives: 98.7 us -> 58.9 us  [exchange(): lax.all_to_all(blocks, 'dp', 0, 0, axis_index_groups=GROUPS[axis], tiled=...]
    ppermute x0 -> x3, starting transfers between devices: none -> 19.4 us  [pair(): lax.ppermute(block, 'dp', [p for a, b in GROUPS[axis] for p in ((a, b), (...]
    broadcast_in_dim x8 -> x5, local copies, waits for them, and re-layouts: 5.56 us -> 3.79 us  [spread(): return exchange(jnp.broadcast_to(block[None], (count,) + block.shape), axis)]
  transfers between devices with their start and end apart: 7 -> 10, of which waited for: 5 -> 5; matrix products, arithmetic and copies ran while one was open for 9% -> 16% of each run, Pallas kernels for 0% -> 0%
where the time goes in v3:
time: 245 us; the launch traced here: 244 us
  blocking collectives  95.6 us (39%)
  starting transfers between devices  42.2 us (17%)
  other arithmetic  28.3 us (12%)
  waiting for transfers between devices  24.9 us (10%)
  local copies, waits for them, and re-layouts  18.5 us (8%)
  matrix products  17.8 us (7%)
  between operations  16.5 us (7%)
    all_to_all x3, blocking collectives, exchange(): lax.all_to_all(blocks, 'dp', 0, 0, axis_index_groups=GROUPS[axis], tiled=...  58.9 us
    all_gather x1, blocking collectives, gather_z(): lax.all_gather(block, 'dp', axis=0, axis_index_groups=GROUPS['z'], tiled=...  36.7 us
    ppermute x3, starting transfers between devices, pair(): lax.ppermute(block, 'dp', [p for a, b in GROUPS[axis] for p in ((a, b), (...  19.4 us
    all_to_all x3, waiting for transfers between devices, exchange(): lax.all_to_all(blocks, 'dp', 0, 0, axis_index_groups=GROUPS[axis], tiled=...  17.9 us
    all_to_all x3, starting transfers between devices, exchange(): lax.all_to_all(blocks, 'dp', 0, 0, axis_index_groups=GROUPS[axis], tiled=...  13.1 us
    all_to_all x2, starting transfers between devices, exchange(): return lax.all_to_all(blocks, axis, 0, 0, tiled=True)  9.45 us
    all_to_all x2, waiting for transfers between devices, exchange(): return lax.all_to_all(blocks, axis, 0, 0, tiled=True)  6.92 us
    dot_general x1, matrix products, body(): hidden = jnp.dot(flat, full_in, preferred_element_type=jnp.float32)  6.39 us
  transfers between devices with their start and end apart: 10, of which 5 were waited for; matrix products, arithmetic and copies ran while one was open for 16% of the time, Pallas kernels for 0%

profile of v3, /device:TPU:1, one launch (start us, length us, event | category | flops | bytes accessed | tf_op | source)
XLA Modules:
  0.0 243.7 jit_solution(1387961794946491482)
XLA Ops:
  7.2 1.2 convert_reduce_fusion.2
  8.5 1.3 convert_reduce_fusion.1
  9.8 2.0 fusion.30
  11.8 5.5 %collective-permute-start = (bf16[24,512]{1,0:T(8,128)(2,1)}, bf16[24,512]{1,0:T(8,128)(2,1)S(1)}, u32[]{:S(2)}, u32[]{:S(2)}) collective-permute-start(bf16[24,512]{1,0:T(8,128)(2,1)} %param.9), channel_id=1, source_target_pairs={{0,256},{256,0},{8,264},{264,8},{16,272},{272,16},{24,280},{280,24... | collective-permute-start | bytes 73736 | tf_op jit(solution)/shard_map/ppermute | solution.py:58
  17.4 0.8 fusion.48
  19.7 36.7 %all-gather.1 = bf16[16,60,512]{2,1,0:T(8,128)(2,1)S(1)} all-gather(bf16[1,60,512]{2,1,0:T(8,128)(2,1)S(1)} %maximum_bitcast_fusion.1), channel_id=2, replica_groups={{0,16,32,48,64,80,96,112,128,144,160,176,192,208,224,240},{8,24,40,56,7..., dimensions={0}, use_global_device_ids=true | all-gather | bytes 1044480 | tf_op jit(solution)/shard_map/all_gather | solution.py:67
  56.4 0.9 slice.65
  57.3 8.1 %collective-permute-start.1 = (bf16[16,48,512]{2,1,0:T(8,128)(2,1)}, bf16[16,48,512]{2,1,0:T(8,128)(2,1)}, u32[]{:S(2)}, u32[]{:S(2)}) collective-permute-start(bf16[16,48,512]{2,1,0:T(8,128)(2,1)} %slice.65), channel_id=1, source_target_pairs={{0,8},{8,0},{16,24},{24,16},{32,40},{40,32},{48,56},{56,48},{64,72... | collective-permute-start | bytes 2359304 | tf_op jit(solution)/shard_map/ppermute | solution.py:58
  65.5 1.0 broadcast_in_dim.18
  66.5 4.5 %all-to-all-start = ((bf16[4,16,12,512]{3,1,2,0:T(8,128)(2,1)}), bf16[4,16,12,512]{3,1,2,0:T(8,128)(2,1)S(1)}, u32[]{:S(2)}, u32[]{:S(2)}) async-start(bf16[4,16,12,512]{3,1,2,0:T(8,128)(2,1)} %broadcast_in_dim.18), calls=%async_computation | async-start | bytes 1572864 | tf_op jit(solution)/shard_map/all_to_all | solution.py:46
  71.0 1.2 broadcast_select_fusion.1
  72.4 1.3 copy.44
  73.7 6.4 %fusion.10 = (f32[1024,512]{1,0:T(8,128)}, f32[1024,512]{1,0:T(8,128)}) fusion(bf16[1024,1536]{1,0:T(8,128)(2,1)} %all-gather.4.cloned.1.call-done, bf16[1536,512]{1,0:T(8,128)(2,1)} %bitcast.75), kind=kOutput, calls=%fused_computation.20 | convolution fusion | flops 1614807040 | bytes 8912896 | tf_op jit(solution)/shard_map/dot_general | solution.py:113
  80.1 1.8 reduce_sum.120
  81.9 1.3 all-to-all-done
  84.3 4.8 %all-to-all-start.1 = ((f32[8,4,1536]{2,1,0:T(4,128)}), f32[8,4,1536]{2,1,0:T(4,128)}, u32[]{:S(2)}, u32[]{:S(2)}) async-start(f32[8,4,1536]{2,1,0:T(4,128)} %broadcast_in_dim.19), calls=%async_computation.1 | async-start | bytes 393216 | tf_op jit(solution)/shard_map/all_to_all | solution.py:47
  91.7 1.2 copy.48
  92.9 1.6 reshape.136
  95.0 1.0 reduce_sum.122
  96.5 1.2 fusion.3
  97.7 1.0 broadcast_in_dim.23
  98.7 4.7 %all-to-all-start.2 = ((bf16[8,32,1536]{2,1,0:T(8,128)(2,1)}), bf16[8,32,1536]{2,1,0:T(8,128)(2,1)}, u32[]{:S(2)}, u32[]{:S(2)}) async-start(bf16[8,32,1536]{2,1,0:T(8,128)(2,1)} %broadcast_in_dim.23), calls=%async_computation.2 | async-start | bytes 1572864 | tf_op jit(solution)/shard_map/all_to_all | solution.py:47
  103.4 1.3 convolution_convert_fusion.2
  104.7 1.5 reshape.138
  106.2 6.5 %all-to-all-done.2 = bf16[8,32,1536]{2,1,0:T(8,128)(2,1)} async-done(((bf16[8,32,1536]{2,1,0:T(8,128)(2,1)}), bf16[8,32,1536]{2,1,0:T(8,128)(2,1)}, u32[]{:S(2)}, u32[]{:S(2)}) %all-to-all-start.2) | async-done | bytes 786464 | tf_op jit(solution)/shard_map/all_to_all | solution.py:47
  112.7 1.3 convert_reduce_fusion
  115.3 3.1 %fusion.17 = bf16[1024,512]{1,0:T(8,128)(2,1)S(1)} fusion(f32[1024,512]{1,0:T(8,128)} %get-tuple-element.32, f32[4,512]{1,0:T(4,128)S(1)} %convolution_multiply_fusion.1), kind=kLoop, calls=%fused_computation.27 | loop fusion | flops 9961472 | bytes 3153920 | tf_op jit(solution)/shard_map/convert_element_type | solution.py:146
  118.4 1.8 convolution_convert_fusion.1
  120.6 9.3 %all_to_all.40 = bf16[2,4,8,40,512]{4,3,2,1,0:T(8,128)(2,1)S(1)} all-to-all(bf16[2,4,8,40,512]{4,3,2,1,0:T(8,128)(2,1)S(1)} %fusion.1), channel_id=1, replica_groups={{0,8},{16,24},{32,40},{48,56},{64,72},{80,88},{96,104},{112,120},{128,1..., dimensions={0} | all-to-all | bytes 5242880 | tf_op jit(solution)/shard_map/all_to_all | solution.py:46
  130.6 1.5 fusion.18
  132.1 3.5 %all-to-all-start.4 = ((bf16[4,8,40,512]{3,2,1,0:T(8,128)(2,1)}), bf16[4,8,40,512]{3,2,1,0:T(8,128)(2,1)S(1)}, u32[]{:S(2)}, u32[]{:S(2)}) async-start(bf16[4,8,40,512]{3,2,1,0:T(8,128)(2,1)} %fusion.18), calls=%async_computation.4 | async-start | bytes 2621440 | tf_op jit(solution)/shard_map/all_to_all | solution.py:46
  135.9 5.2 %convolution_convert_fusion = bf16[1024,1536]{1,0:T(8,128)(2,1)} fusion(bf16[1024,512]{1,0:T(8,128)(2,1)} %copy-done.5, bf16[1536,512]{1,0:T(8,128)(2,1)} %bitcast.76), kind=kOutput, calls=%fused_computation.2 | convolution fusion | flops 1612185600 | bytes 5767168 | tf_op jit(solution)/shard_map/rf,df->rd/dot_general | solution.py:171
  141.1 12.0 %all-to-all-done.4 = bf16[4,8,40,512]{3,2,1,0:T(8,128)(2,1)S(1)} async-done(((bf16[4,8,40,512]{3,2,1,0:T(8,128)(2,1)}), bf16[4,8,40,512]{3,2,1,0:T(8,128)(2,1)S(1)}, u32[]{:S(2)}, u32[]{:S(2)}) %all-to-all-start.4) | async-done | bytes 1310752 | tf_op jit(solution)/shard_map/all_to_all | solution.py:46
  153.8 23.6 %all_to_all.41 = bf16[8,40,512]{2,1,0:T(8,128)(2,1)S(1)} all-to-all(bf16[8,40,512]{2,1,0:T(8,128)(2,1)S(1)} %fusion.38), channel_id=1, replica_groups={{0,32,64,96,128,160,192,224},{8,40,72,104,136,168,200,232},{16,48,80,11..., dimensions={0} | all-to-all | bytes 655360 | tf_op jit(solution)/shard_map/all_to_all | solution.py:46
  178.3 25.9 %all_to_all.42 = bf16[8,32,512]{2,1,0:T(8,128)(2,1)S(1)} all-to-all(bf16[8,32,512]{2,1,0:T(8,128)(2,1)S(1)} %broadcast_in_dim.26), channel_id=1, replica_groups={{0,32,64,96,128,160,192,224},{8,40,72,104,136,168,200,232},{16,48,80,11..., dimensions={0} | all-to-all | bytes 524288 | tf_op jit(solution)/shard_map/all_to_all | solution.py:46
  204.2 1.1 broadcast_in_dim.27
  205.3 5.1 %all-to-all-start.7 = ((bf16[4,8,32,512]{3,2,1,0:T(8,128)(2,1)}), bf16[4,8,32,512]{3,2,1,0:T(8,128)(2,1)S(1)}, u32[]{:S(2)}, u32[]{:S(2)}) async-start(bf16[4,8,32,512]{3,2,1,0:T(8,128)(2,1)} %broadcast_in_dim.27), calls=%async_computation.7 | async-start | bytes 2097152 | tf_op jit(solution)/shard_map/all_to_all | solution.py:46
  211.1 1.2 convert_reduce_fusion.4
  212.8 1.3 div.77
  214.1 1.1 convert_element_type.112
  215.2 1.0 fusion.31
  216.2 1.8 fusion.35
  218.0 4.5 %all-to-all-done.7 = bf16[4,8,32,512]{3,2,1,0:T(8,128)(2,1)S(1)} async-done(((bf16[4,8,32,512]{3,2,1,0:T(8,128)(2,1)}), bf16[4,8,32,512]{3,2,1,0:T(8,128)(2,1)S(1)}, u32[]{:S(2)}, u32[]{:S(2)}) %all-to-all-start.7) | async-done | bytes 1048608 | tf_op jit(solution)/shard_map/all_to_all | solution.py:46
  222.6 5.8 %collective-permute-start.2 = (bf16[4,8,32,512]{3,2,1,0:T(8,128)(2,1)S(1)}, bf16[4,8,32,512]{3,2,1,0:T(8,128)(2,1)}, u32[]{:S(2)}, u32[]{:S(2)}) collective-permute-start(bf16[4,8,32,512]{3,2,1,0:T(8,128)(2,1)S(1)} %all-to-all-done.7), channel_id=1, source_target_pairs={{0,8},{8,0},{16,24},{24,16},{32,40},{40,32},{48,56},{56,48},{64,72... | collective-permute-start | bytes 3145736 | tf_op jit(solution)/shard_map/ppermute | solution.py:58
  228.4 1.6 slice.79
  231.8 1.3 fusion.47
  233.1 1.4 select_bitcast_fusion.1
  234.8 1.3 slice.76
  (98 shorter events, 12.6 us)
Async XLA Ops:
  7.2 76.1 %copy-start = (bf16[512,1536]{1,0:T(8,128)(2,1)S(1)}, bf16[512,1536]{1,0:T(8,128)(2,1)}, u32[]{:S(2)}) copy-start(bf16[512,1536]{1,0:T(8,128)(2,1)} %param.10) | copy-start | bytes 4718596
  7.2 12.4 %copy-start.13 = (bf16[24,512]{1,0:T(8,128)(2,1)S(1)}, bf16[24,512]{1,0:T(8,128)(2,1)}, u32[]{:S(2)}) copy-start(bf16[24,512]{1,0:T(8,128)(2,1)} %param.9) | copy-start | bytes 73732
  7.2 11.7 %copy-start.7 = (bf16[4,1536]{1,0:T(4,128)(2,1)S(1)}, bf16[4,1536]{1,0:T(4,128)(2,1)}, u32[]{:S(2)}) copy-start(bf16[4,1536]{1,0:T(4,128)(2,1)} %param.12) | copy-start | bytes 36868
  7.2 66.5 %all-gather.4.cloned.1.call-start = ((), (), s32[]{:S(2)}) async-start(), calls=%async_computation.9 | async-start | bytes 3538944 | tf_op jit(solution)/shard_map/all_gather | solution.py:100
  9.8 47.5 %copy-start.12 = (f32[4,32]{1,0:T(4,128)}, f32[4,32]{1,0:T(4,128)S(1)}, u32[]{:S(2)}) copy-start(f32[4,32]{1,0:T(4,128)S(1)} %add_rsqrt_fusion) | copy-start | bytes 1540
  11.8 7.8 %collective-permute-start = (bf16[24,512]{1,0:T(8,128)(2,1)}, bf16[24,512]{1,0:T(8,128)(2,1)S(1)}, u32[]{:S(2)}, u32[]{:S(2)}) collective-permute-start(bf16[24,512]{1,0:T(8,128)(2,1)} %param.9), channel_id=1, source_target_pairs={{0,256},{256,0},{8,264},{264,8},{16,272},{272,16},{24,280},{280,24... | collective-permute-start | bytes 73736 | tf_op jit(solution)/shard_map/ppermute | solution.py:58
  18.2 47.3 %copy-start.15 = (f32[4]{0:T(128)}, f32[4]{0:T(128)S(1)}, u32[]{:S(2)}) copy-start(f32[4]{0:T(128)S(1)} %add_rsqrt_fusion.2) | copy-start | bytes 52
  57.3 13.7 %collective-permute-start.1 = (bf16[16,48,512]{2,1,0:T(8,128)(2,1)}, bf16[16,48,512]{2,1,0:T(8,128)(2,1)}, u32[]{:S(2)}, u32[]{:S(2)}) collective-permute-start(bf16[16,48,512]{2,1,0:T(8,128)(2,1)} %slice.65), channel_id=1, source_target_pairs={{0,8},{8,0},{16,24},{24,16},{32,40},{40,32},{48,56},{56,48},{64,72... | collective-permute-start | bytes 2359304 | tf_op jit(solution)/shard_map/ppermute | solution.py:58
  66.5 16.8 %all-to-all-start = ((bf16[4,16,12,512]{3,1,2,0:T(8,128)(2,1)}), bf16[4,16,12,512]{3,1,2,0:T(8,128)(2,1)S(1)}, u32[]{:S(2)}, u32[]{:S(2)}) async-start(bf16[4,16,12,512]{3,1,2,0:T(8,128)(2,1)} %broadcast_in_dim.18), calls=%async_computation | async-start | bytes 1572864 | tf_op jit(solution)/shard_map/all_to_all | solution.py:46
  80.1 8.9 %copy-start.8 = (bf16[28,1536]{1,0:T(8,128)(2,1)S(1)}, bf16[28,1536]{1,0:T(8,128)(2,1)}, u32[]{:S(2)}) copy-start(bf16[28,1536]{1,0:T(8,128)(2,1)} %param.11) | copy-start | bytes 258052
  81.9 11.0 %copy-start.10 = (bf16[4,512]{1,0:T(4,128)(2,1)}, bf16[4,512]{1,0:T(4,128)(2,1)S(1)}, u32[]{:S(2)}) copy-start(bf16[4,512]{1,0:T(4,128)(2,1)S(1)} %multiply_convert_fusion.1) | copy-start | bytes 12292
  84.3 10.7 %all-to-all-start.1 = ((f32[8,4,1536]{2,1,0:T(4,128)}), f32[8,4,1536]{2,1,0:T(4,128)}, u32[]{:S(2)}, u32[]{:S(2)}) async-start(f32[8,4,1536]{2,1,0:T(4,128)} %broadcast_in_dim.19), calls=%async_computation.1 | async-start | bytes 393216 | tf_op jit(solution)/shard_map/all_to_all | solution.py:47
  98.7 14.0 %all-to-all-start.2 = ((bf16[8,32,1536]{2,1,0:T(8,128)(2,1)}), bf16[8,32,1536]{2,1,0:T(8,128)(2,1)}, u32[]{:S(2)}, u32[]{:S(2)}) async-start(bf16[8,32,1536]{2,1,0:T(8,128)(2,1)} %broadcast_in_dim.23), calls=%async_computation.2 | async-start | bytes 1572864 | tf_op jit(solution)/shard_map/all_to_all | solution.py:47
  114.2 96.2 %copy-start.4 = (f32[32,1536]{1,0:T(8,128)}, f32[32,1536]{1,0:T(8,128)S(1)}, u32[]{:S(2)}) copy-start(f32[32,1536]{1,0:T(8,128)S(1)} %subtract_multiply_fusion) | copy-start | bytes 589828
  115.2 3.2 %copy-start.16 = (bf16[1024,1536]{1,0:T(8,128)(2,1)S(1)}, bf16[1024,1536]{1,0:T(8,128)(2,1)}, u32[]{:S(2)}) copy-start(bf16[1024,1536]{1,0:T(8,128)(2,1)} %all-gather.4.cloned.1.call-done) | copy-start | bytes 9437188
  118.3 1.8 copy-start.5
  132.1 21.0 %all-to-all-start.4 = ((bf16[4,8,40,512]{3,2,1,0:T(8,128)(2,1)}), bf16[4,8,40,512]{3,2,1,0:T(8,128)(2,1)S(1)}, u32[]{:S(2)}, u32[]{:S(2)}) async-start(bf16[4,8,40,512]{3,2,1,0:T(8,128)(2,1)} %fusion.18), calls=%async_computation.4 | async-start | bytes 2621440 | tf_op jit(solution)/shard_map/all_to_all | solution.py:46
  135.7 75.4 %reduce-scatter.2.cloned.1.call-start = ((), (), s32[]{:S(2)}) async-start(), calls=%async_computation.10 | async-start | bytes 3538944 | tf_op jit(solution)/shard_map/reduce_scatter | solution.py:176
  153.7 24.5 %copy-start.11 = (bf16[4,512]{1,0:T(4,128)(2,1)S(1)}, bf16[4,512]{1,0:T(4,128)(2,1)}, u32[]{:S(2)}) copy-start(bf16[4,512]{1,0:T(4,128)(2,1)} %copy-done.10) | copy-start | bytes 12292
  177.4 0.7 copy-start.3
  178.2 27.1 %copy-start.6 = (f32[36,512]{1,0:T(8,128)}, f32[36,512]{1,0:T(8,128)S(1)}, u32[]{:S(2)}) copy-start(f32[36,512]{1,0:T(8,128)S(1)} %convert_reduce_fusion.3) | copy-start | bytes 221188
  205.3 9.9 %copy-start.1 = (bf16[4,32,1536]{2,1,0:T(8,128)(2,1)S(1)}, bf16[4,32,1536]{2,1,0:T(8,128)(2,1)}, u32[]{:S(2)}) copy-start(bf16[4,32,1536]{2,1,0:T(8,128)(2,1)} %param.8) | copy-start | bytes 1179652
  205.3 17.2 %all-to-all-start.7 = ((bf16[4,8,32,512]{3,2,1,0:T(8,128)(2,1)}), bf16[4,8,32,512]{3,2,1,0:T(8,128)(2,1)S(1)}, u32[]{:S(2)}, u32[]{:S(2)}) async-start(bf16[4,8,32,512]{3,2,1,0:T(8,128)(2,1)} %broadcast_in_dim.27), calls=%async_computation.7 | async-start | bytes 2097152 | tf_op jit(solution)/shard_map/all_to_all | solution.py:46
  211.1 5.1 %copy-start.2 = (bf16[128,1536]{1,0:T(8,128)(2,1)S(1)}, bf16[128,1536]{1,0:T(8,128)(2,1)}, u32[]{:S(2)}) copy-start(bf16[128,1536]{1,0:T(8,128)(2,1)} %reduce-scatter.2.cloned.1.call-done) | copy-start | bytes 1179652
  212.3 17.8 %slice-start = ((f32[36,512]{1,0:T(8,128)}), f32[12,512]{1,0:T(8,128)S(1)}, s32[]{:S(2)}) async-start(f32[36,512]{1,0:T(8,128)} %copy-done.6), calls=%async_computation.11 | async-start | bytes 65536 | tf_op jit(solution)/shard_map/slice | solution.py:202
  214.1 2.1 copy-start.9
  214.1 2.1 copy-start.14
  222.6 10.5 %collective-permute-start.2 = (bf16[4,8,32,512]{3,2,1,0:T(8,128)(2,1)S(1)}, bf16[4,8,32,512]{3,2,1,0:T(8,128)(2,1)}, u32[]{:S(2)}, u32[]{:S(2)}) collective-permute-start(bf16[4,8,32,512]{3,2,1,0:T(8,128)(2,1)S(1)} %all-to-all-done.7), channel_id=1, source_target_pairs={{0,8},{8,0},{16,24},{24,16},{32,40},{40,32},{48,56},{56,48},{64,72... | collective-permute-start | bytes 3145736 | tf_op jit(solution)/shard_map/ppermute | solution.py:58
Sparse Core Ops, SparseCore 0:
  12.0 54.5 all-gather.3
  153.9 44.3 reduce-scatter.1

commit v4 on v3

--- a/solution.py
+++ b/solution.py
@@ -1,8 +1,11 @@
+import functools
 import math
 
 import jax
 import jax.numpy as jnp
 from jax import lax
+from jax.experimental import pallas as pl
+from jax.experimental.pallas import tpu as pltpu
 from jax.sharding import PartitionSpec as P
 
 epsilon = 1e-06
@@ -23,13 +26,91 @@
 }
 
 
-def gelu_slope(values):
+def norm_kernel(x_ref, normed_ref, total_ref):
+    values = x_ref[0].astype(jnp.float32)
+    centered = values - jnp.mean(values, -1, keepdims=True)
+    inv_std = lax.rsqrt(jnp.mean(centered * centered, -1, keepdims=True) + epsilon)
+    normed_ref[...] = (centered * inv_std).astype(jnp.bfloat16)
+    total_ref[0] = jnp.sum(values, 0, keepdims=True)
+
+
+def normalize(layer_input):
+    rows, patches, width = layer_input.shape
+    return pl.pallas_call(
+        norm_kernel,
+        grid=(rows,),
+        in_specs=[pl.BlockSpec((1, patches, width), lambda i: (i, 0, 0))],
+        out_specs=[
+            pl.BlockSpec((patches, width), lambda i: (i, 0)),
+            pl.BlockSpec((1, 1, width), lambda i: (i, 0, 0)),
+        ],
+        out_shape=[
+            jax.ShapeDtypeStruct((rows * patches, width), jnp.bfloat16),
+            jax.ShapeDtypeStruct((rows, 1, width), jnp.float32),
+        ],
+        compiler_params=pltpu.CompilerParams(vmem_limit_bytes=16 * 1024 * 1024),
+    )(layer_input)
+
+
+def hidden_kernel(
+    rows, patches, x_ref, in_ref, out_ref, total_ref, slope_ref, act_ref, part_ref, sum_ref
+):
+    step = pl.program_id(0)
+    hidden = jnp.dot(x_ref[...], in_ref[...], preferred_element_type=jnp.float32)
     root = math.sqrt(2.0 / math.pi)
-    inner = root * (values + 0.044715 * values * values * values)
-    tangent = jnp.tanh(inner)
-    return 0.5 * (1.0 + tangent) + 0.5 * values * (1.0 - tangent * tangent) * root * (
-        1.0 + 3.0 * 0.044715 * values * values
-    )
+    square = hidden * hidden
+    tangent = jnp.tanh(root * (hidden + 0.044715 * square * hidden))
+    half = 0.5 * (1.0 + tangent)
+    slope_ref[...] = half + 0.5 * hidden * (1.0 - tangent * tangent) * root * (
+        1.0 + 3.0 * 0.044715 * square
+    )
+    width = hidden.shape[1]
+    sums = jnp.sum((hidden * half).reshape(-1, rows, patches, width), (0, 2))
+
+    @pl.when(step == 0)
+    def _():
+        sum_ref[...] = sums
+
+    @pl.when(step > 0)
+    def _():
+        sum_ref[...] += sums
+
+    @pl.when(step == pl.num_programs(0) - 1)
+    def _():
+        act_mean = (sum_ref[...] * (1.0 / (8 * patches))).astype(jnp.bfloat16)
+        act_ref[...] = act_mean
+        part = jnp.dot(act_mean, out_ref[...], preferred_element_type=jnp.float32)
+        part = part + total_ref[:, 0] * (1.0 / (8 * patches))
+        part_ref[...] = jnp.broadcast_to(part[None], part_ref.shape)
+
+
+def hidden_layer(flat, full_in, out_weight, totals, patches):
+    tokens, width = flat.shape
+    units = full_in.shape[1]
+    rows = totals.shape[0]
+    block = 2 * rows * patches
+    return pl.pallas_call(
+        functools.partial(hidden_kernel, rows, patches),
+        grid=(tokens // block,),
+        in_specs=[
+            pl.BlockSpec((block, width), lambda i: (i, 0)),
+            pl.BlockSpec((width, units), lambda i: (0, 0)),
+            pl.BlockSpec((units, width), lambda i: (0, 0)),
+            pl.BlockSpec((rows, 1, width), lambda i: (0, 0, 0)),
+        ],
+        out_specs=[
+            pl.BlockSpec((block, units), lambda i: (i, 0)),
+            pl.BlockSpec((rows, units), lambda i: (0, 0)),
+            pl.BlockSpec((8, rows, width), lambda i: (0, 0, 0)),
+        ],
+        out_shape=[
+            jax.ShapeDtypeStruct((tokens, units), jnp.float32),
+            jax.ShapeDtypeStruct((rows, units), jnp.bfloat16),
+            jax.ShapeDtypeStruct((8, rows, width), jnp.float32),
+        ],
+        scratch_shapes=[pltpu.VMEM((rows, units), jnp.float32)],
+        compiler_params=pltpu.CompilerParams(vmem_limit_bytes=60 * 1024 * 1024),
+    )(flat, full_in, out_weight, totals)
 
 
 def unit_rows(values):
@@ -65,10 +146,6 @@
 
 def gather_z(block):
     return lax.all_gather(block, "dp", axis=0, axis_index_groups=GROUPS["z"], tiled=False)
-
-
-def pad_rows(block, rows):
-    return jnp.pad(block, [(0, 0)] * (block.ndim - 2) + [(0, rows - block.shape[-2]), (0, 0)])
 
 
 def body(
@@ -85,11 +162,7 @@
     image_count = local_rows + image_rest.shape[0]
     weight_coef = loss_scale[0] / (image_count * dp_count)
 
-    inputs_f = layer_input.astype(jnp.float32)
-    centered = inputs_f - jnp.mean(inputs_f, -1, keepdims=True)
-    inv_std = lax.rsqrt(jnp.mean(centered * centered, -1, keepdims=True) + epsilon)
-    standard = centered * inv_std
-    normed = standard.astype(jnp.bfloat16).reshape(-1, width_model)
+    normed, totals = normalize(layer_input)
     token_shape = (8, local_rows, local_patches, hidden_width)
 
     text_unit, text_inv = unit_rows(text_embed.astype(jnp.float32))
@@ -110,18 +183,11 @@
         text_low.astype(jnp.float32),
         (first_row, zero_index),
     )
-    hidden = jnp.dot(flat, full_in, preferred_element_type=jnp.float32)
-    act_mean = jnp.mean(
-        jax.nn.gelu(hidden, approximate=True).reshape(token_shape), (0, 2)
-    ).astype(jnp.bfloat16)
-    act_mean, texts = lax.optimization_barrier((act_mean, texts))
+    slope, act_mean, part_pool = hidden_layer(flat, full_in, out_weight, totals, local_patches)
+    part_pool, texts = lax.optimization_barrier((part_pool, texts))
     texts = jnp.transpose(texts.reshape(4, 8, 2, text_rows, hidden_width), (0, 2, 1, 3, 4))
     texts = texts.reshape(dp_count * text_count, width_model)
-    part_pool = (
-        jnp.dot(act_mean, out_weight, preferred_element_type=jnp.float32)
-        + jnp.sum(inputs_f, 1) / patches
-    )
-    pooled = sum_over(part_pool, "mp")
+    pooled = jnp.sum(exchange(part_pool, "mp"), 0)
     images = jnp.concatenate([pooled, image_rest.astype(jnp.float32)], 0)
     image_unit, image_inv = unit_rows(images)
     image_low = image_unit.astype(jnp.bfloat16)
@@ -142,7 +208,7 @@
         jnp.einsum("bd,fd->bf", pool_low, out_weight, preferred_element_type=jnp.float32) / patches
     )
     hidden_grad = (
-        (row_grad.reshape(1, local_rows, 1, hidden_width) * gelu_slope(hidden).reshape(token_shape))
+        (row_grad.reshape(1, local_rows, 1, hidden_width) * slope.reshape(token_shape))
         .astype(jnp.bfloat16)
         .reshape(-1, hidden_width)
     )
@@ -179,22 +245,27 @@
     )
     got = exchange(parts, "z_hi")
     summed = jnp.sum(got[:, : in_rows + text_rows].astype(jnp.float32), 0)
-    back = jnp.concatenate([summed[:in_rows].astype(jnp.bfloat16), act_mean], 0)
+    means = pair(act_mean, "core").reshape(2 * local_rows, hidden_width)
+    back = jnp.concatenate([summed[:in_rows].astype(jnp.bfloat16), means], 0)
+    normed_grad, again = lax.optimization_barrier((normed_grad, layer_input))
+    inputs_f = again.astype(jnp.float32)
+    centered = inputs_f - jnp.mean(inputs_f, -1, keepdims=True)
+    inv_std = lax.rsqrt(jnp.mean(centered * centered, -1, keepdims=True) + epsilon)
+    standard = centered * inv_std
     input_grad = inv_std * (
         normed_grad
         - jnp.mean(normed_grad, -1, keepdims=True)
         - standard * jnp.mean(normed_grad * standard, -1, keepdims=True)
     )
     input_grad = (input_grad + pool_grad[:, None, :] / patches).astype(jnp.bfloat16)
-    back = spread(spread(pad_rows(back, 32), "z_hi"), "x_hi z_lo")
+    back = spread(spread(back, "z_hi"), "x_hi z_lo")
     back, input_grad = lax.optimization_barrier((back, input_grad))
-    back = pair(back, "core")
-    back = back.reshape(dp_count, 32, hidden_width)
-    in_weight_grad = back[:, :in_rows].reshape(width_model, hidden_width)
-    all_means = back[:, in_rows : in_rows + local_rows].reshape(-1, hidden_width)
+    back = back.reshape(dp_count // 2, -1, hidden_width)
+    in_weight_grad = pair(back[:, :in_rows], "core").reshape(width_model, hidden_width)
+    all_means = back[:, in_rows:].reshape(-1, hidden_width)
     columns = got[:, in_rows + text_rows :, : 8 * column_width]
-    columns = columns.reshape(8, local_rows, 8, column_width)
-    columns = jnp.transpose(columns, (2, 0, 1, 3)).reshape(-1, column_width)
+    columns = columns.reshape(8, local_rows, 2, 4, column_width)
+    columns = jnp.transpose(columns, (3, 0, 2, 1, 4)).reshape(-1, column_width)
     out_weight_grad = jnp.einsum(
         "bf,bc->fc", all_means, columns, preferred_element_type=jnp.float32
     ).astype(jnp.bfloat16)

time: 245 us -> 235 us (0.959)
  blocking collectives: 95.6 us -> 72.4 us
  waiting for transfers between devices: 24.9 us -> 47.2 us
  other arithmetic: 28.3 us -> 16.8 us
  Pallas kernels: 0 us -> 9.27 us
  starting transfers between devices: 42.2 us -> 50.8 us
  matrix products: 17.8 us -> 9.7 us
  local copies, waits for them, and re-layouts: 18.5 us -> 10.9 us
    all_to_all x3 -> x2, blocking collectives: 58.9 us -> 36.1 us  [exchange(): lax.all_to_all(blocks, 'dp', 0, 0, axis_index_groups=GROUPS[axis], tiled=...]
    all_to_all x3 -> x4, waiting for transfers between devices: 17.9 us -> 37.9 us  [exchange(): lax.all_to_all(blocks, 'dp', 0, 0, axis_index_groups=GROUPS[axis], tiled=...]
    pallas_call x0 -> x2, Pallas kernels: none -> 9.27 us  [the longest x1 7.36 us: hidden_layer(): pl.pallas_call(functools.partial(hidden_kernel, rows, patches), grid=(tok...]
    all_to_all x3 -> x4, starting transfers between devices: 13.1 us -> 20.1 us  [exchange(): lax.all_to_all(blocks, 'dp', 0, 0, axis_index_groups=GROUPS[axis], tiled=...]
    dot_general x2 -> x0, matrix products: 6.7 us -> none  [the longest x1 6.39 us: body(): hidden = jnp.dot(flat, full_in, preferred_element_type=jnp.float32)]
    convert_element_type x4 -> x1, other arithmetic: 6.13 us -> 2.01 us  [body(): hidden_grad = (row_grad.reshape(1, local_rows, 1, hidden_width) * slope.r...]
    reduce_sum x3 -> x2, other arithmetic: 4.11 us -> 0.29 us  [the longest x1 0.25 us: body(): jnp.mean(centered * centered, -1, keepdims=True) + epsilon]
    ppermute x3 -> x4, starting transfers between devices: 19.4 us -> 21.6 us  [pair(): lax.ppermute(block, 'dp', [p for a, b in GROUPS[axis] for p in ((a, b), (...]
  transfers between devices with their start and end apart: 10 -> 12, of which waited for: 5 -> 8; matrix products, arithmetic and copies ran while one was open for 16% -> 9% of each run, Pallas kernels for 0% -> 3%
where the time goes in v4:
time: 235 us; the launch traced here: 234 us
  blocking collectives  72.4 us (31%)
  starting transfers between devices  50.8 us (22%)
  waiting for transfers between devices  47.2 us (20%)
  other arithmetic  16.8 us (7%)
  between operations  16.6 us (7%)
  local copies, waits for them, and re-layouts  10.9 us (5%)
  matrix products  9.7 us (4%)
  Pallas kernels  9.27 us (4%)
    all_to_all x4, waiting for transfers between devices, exchange(): lax.all_to_all(blocks, 'dp', 0, 0, axis_index_groups=GROUPS[axis], tiled=...  37.9 us
    all_gather x1, blocking collectives, gather_z(): lax.all_gather(block, 'dp', axis=0, axis_index_groups=GROUPS['z'], tiled=...  36.3 us
    all_to_all x2, blocking collectives, exchange(): lax.all_to_all(blocks, 'dp', 0, 0, axis_index_groups=GROUPS[axis], tiled=...  36.1 us
    ppermute x4, starting transfers between devices, pair(): lax.ppermute(block, 'dp', [p for a, b in GROUPS[axis] for p in ((a, b), (...  21.6 us
    all_to_all x4, starting transfers between devices, exchange(): lax.all_to_all(blocks, 'dp', 0, 0, axis_index_groups=GROUPS[axis], tiled=...  20.1 us
    all_to_all x2, starting transfers between devices, exchange(): return lax.all_to_all(blocks, axis, 0, 0, tiled=True)  8.96 us
    all_to_all x2, waiting for transfers between devices, exchange(): return lax.all_to_all(blocks, axis, 0, 0, tiled=True)  8.24 us
    pallas_call x1, Pallas kernels, hidden_layer(): pl.pallas_call(functools.partial(hidden_kernel, rows, patches), grid=(tok...  7.36 us
  transfers between devices with their start and end apart: 12, of which 8 were waited for; matrix products, arithmetic and copies ran while one was open for 9% of the time, Pallas kernels for 3%

profile of v4, /device:TPU:1, one launch (start us, length us, event | category | flops | bytes accessed | tf_op | source)
XLA Modules:
  0.0 233.6 jit_solution(6124376412616202358)
XLA Ops:
  7.2 1.0 copy-done
  8.2 1.9 shard_map.119
  10.1 0.6 copy-done.2
  10.7 5.5 %collective-permute-start = (bf16[24,512]{1,0:T(8,128)(2,1)}, bf16[24,512]{1,0:T(8,128)(2,1)S(1)}, u32[]{:S(2)}, u32[]{:S(2)}) collective-permute-start(bf16[24,512]{1,0:T(8,128)(2,1)} %param.9), channel_id=1, source_target_pairs={{0,256},{256,0},{8,264},{264,8},{16,272},{272,16},{24,280},{280,24... | collective-permute-start | bytes 73736 | tf_op jit(solution)/shard_map/ppermute | solution.py:139
  16.3 0.8 fusion.31
  17.1 0.8 convert_dynamic-update-slice_fusion
  18.0 0.7 select_bitcast_fusion.3
  18.8 36.3 %all-gather.1 = bf16[16,60,512]{2,1,0:T(8,128)(2,1)S(1)} all-gather(bf16[1,60,512]{2,1,0:T(8,128)(2,1)S(1)} %maximum_bitcast_fusion.1), channel_id=2, replica_groups={{0,16,32,48,64,80,96,112,128,144,160,176,192,208,224,240},{8,24,40,56,7..., dimensions={0}, use_global_device_ids=true | all-gather | bytes 1044480 | tf_op jit(solution)/shard_map/all_gather | solution.py:148
  55.1 9.0 %collective-permute-start.1 = (bf16[16,48,512]{2,1,0:T(8,128)(2,1)S(1)}, bf16[16,48,512]{2,1,0:T(8,128)(2,1)}, u32[]{:S(2)}, u32[]{:S(2)}) collective-permute-start(bf16[16,48,512]{2,1,0:T(8,128)(2,1)S(1)} %slice.65), channel_id=1, source_target_pairs={{0,8},{8,0},{16,24},{24,16},{32,40},{40,32},{48,56},{56,48},{64,72... | collective-permute-start | bytes 2359304 | tf_op jit(solution)/shard_map/ppermute | solution.py:139
  64.2 1.0 broadcast_in_dim.18
  65.3 4.5 %all-to-all-start = ((bf16[4,16,12,512]{3,1,2,0:T(8,128)(2,1)}), bf16[4,16,12,512]{3,1,2,0:T(8,128)(2,1)S(1)}, u32[]{:S(2)}, u32[]{:S(2)}) async-start(bf16[4,16,12,512]{3,1,2,0:T(8,128)(2,1)} %broadcast_in_dim.18), calls=%async_computation | async-start | bytes 1572864 | tf_op jit(solution)/shard_map/all_to_all | solution.py:127
  69.8 1.2 broadcast_select_fusion.1
  71.2 1.3 copy.37
  72.5 7.4 %shard_map.120 = (f32[1024,512]{1,0:T(8,128)}, bf16[4,512]{1,0:T(4,128)(2,1)}, f32[8,4,1536]{2,1,0:T(4,128)}) custom-call(bf16[1024,1536]{1,0:T(8,128)(2,1)} %all-gather.4.cloned.1.call-done.x_ref, bf16[1536,512]{1,0:T(8,128)(2,1)} %bitcast.65, bf16[512,1536]{1,0:T(8,128)(2,1)} %out_ref.1, f32[4,1,1536]{2,1,0:T(1,128)} %copy-done.2), custom_call_target="tpu_custom_call" | custom-call | tf_op jit(solution)/shard_map/pallas_call | solution.py:92
  79.9 2.2 all-to-all-done
  82.0 4.8 %all-to-all-start.1 = ((f32[8,4,1536]{2,1,0:T(4,128)}), f32[8,4,1536]{2,1,0:T(4,128)S(1)}, u32[]{:S(2)}, u32[]{:S(2)}) async-start(f32[8,4,1536]{2,1,0:T(4,128)} %get-tuple-element.25), calls=%async_computation.1 | async-start | bytes 393216 | tf_op jit(solution)/shard_map/all_to_all | solution.py:128
  88.8 0.6 copy.39
  90.1 2.5 %all-to-all-done.1 = f32[8,4,1536]{2,1,0:T(4,128)S(1)} async-done(((f32[8,4,1536]{2,1,0:T(4,128)}), f32[8,4,1536]{2,1,0:T(4,128)S(1)}, u32[]{:S(2)}, u32[]{:S(2)}) %all-to-all-start.1) | async-done | bytes 196640 | tf_op jit(solution)/shard_map/all_to_all | solution.py:128
  93.5 1.0 broadcast_in_dim.20
  94.5 4.2 %all-to-all-start.2 = ((bf16[8,32,1536]{2,1,0:T(8,128)(2,1)}), bf16[8,32,1536]{2,1,0:T(8,128)(2,1)}, u32[]{:S(2)}, u32[]{:S(2)}) async-start(bf16[8,32,1536]{2,1,0:T(8,128)(2,1)} %broadcast_in_dim.20), calls=%async_computation.2 | async-start | bytes 1572864 | tf_op jit(solution)/shard_map/all_to_all | solution.py:128
  98.7 1.3 convolution_convert_fusion.2
  100.0 1.5 reshape.129
  101.6 5.8 %all-to-all-done.2 = bf16[8,32,1536]{2,1,0:T(8,128)(2,1)} async-done(((bf16[8,32,1536]{2,1,0:T(8,128)(2,1)}), bf16[8,32,1536]{2,1,0:T(8,128)(2,1)}, u32[]{:S(2)}, u32[]{:S(2)}) %all-to-all-start.2) | async-done | bytes 786464 | tf_op jit(solution)/shard_map/all_to_all | solution.py:128
  107.3 1.3 convert_reduce_fusion
  109.9 2.0 fusion.4
  112.3 1.8 convolution_convert_fusion.1
  114.5 10.1 %all_to_all.40 = bf16[2,4,8,40,512]{4,3,2,1,0:T(8,128)(2,1)S(1)} all-to-all(bf16[2,4,8,40,512]{4,3,2,1,0:T(8,128)(2,1)S(1)} %fusion.1), channel_id=1, replica_groups={{0,8},{16,24},{32,40},{48,56},{64,72},{80,88},{96,104},{112,120},{128,1..., dimensions={0} | all-to-all | bytes 5242880 | tf_op jit(solution)/shard_map/all_to_all | solution.py:127
  124.6 0.7 convert_element_type.92
  125.4 1.5 fusion.5
  126.9 3.7 %all-to-all-start.4 = ((bf16[4,8,40,512]{3,2,1,0:T(8,128)(2,1)}), bf16[4,8,40,512]{3,2,1,0:T(8,128)(2,1)S(1)}, u32[]{:S(2)}, u32[]{:S(2)}) async-start(bf16[4,8,40,512]{3,2,1,0:T(8,128)(2,1)} %fusion.5), calls=%async_computation.4 | async-start | bytes 2621440 | tf_op jit(solution)/shard_map/all_to_all | solution.py:127
  130.6 4.7 %convolution_convert_fusion = bf16[1024,1536]{1,0:T(8,128)(2,1)} fusion(bf16[1024,512]{1,0:T(8,128)(2,1)} %copy-done.6, bf16[1536,512]{1,0:T(8,128)(2,1)S(1)} %bitcast.66), kind=kOutput, calls=%fused_computation.2 | convolution fusion | flops 1612185600 | bytes 5767168 | tf_op jit(solution)/shard_map/rf,df->rd/dot_general | solution.py:237
  135.3 12.9 %all-to-all-done.4 = bf16[4,8,40,512]{3,2,1,0:T(8,128)(2,1)S(1)} async-done(((bf16[4,8,40,512]{3,2,1,0:T(8,128)(2,1)}), bf16[4,8,40,512]{3,2,1,0:T(8,128)(2,1)S(1)}, u32[]{:S(2)}, u32[]{:S(2)}) %all-to-all-start.4) | async-done | bytes 1310752 | tf_op jit(solution)/shard_map/all_to_all | solution.py:127
  148.5 1.0 fusion.24
  149.5 6.2 %all-to-all-start.5 = ((bf16[8,40,512]{2,1,0:T(8,128)(2,1)}), bf16[8,40,512]{2,1,0:T(8,128)(2,1)S(1)}, u32[]{:S(2)}, u32[]{:S(2)}) async-start(bf16[8,40,512]{2,1,0:T(8,128)(2,1)} %fusion.24), calls=%async_computation.5 | async-start | bytes 655360 | tf_op jit(solution)/shard_map/all_to_all | solution.py:127
  155.8 3.4 %collective-permute-start.2 = (bf16[4,512]{1,0:T(4,128)(2,1)S(1)}, bf16[4,512]{1,0:T(4,128)(2,1)S(1)}, u32[]{:S(2)}, u32[]{:S(2)}) collective-permute-start(bf16[4,512]{1,0:T(4,128)(2,1)S(1)} %copy-done.9), channel_id=1, source_target_pairs={{0,8},{8,0},{16,24},{24,16},{32,40},{40,32},{48,56},{56,48},{64,72... | collective-permute-start | bytes 12296 | tf_op jit(solution)/shard_map/ppermute | solution.py:139
  159.2 0.8 collective-permute-done.2
  160.0 12.5 %all-to-all-done.5 = bf16[8,40,512]{2,1,0:T(8,128)(2,1)S(1)} async-done(((bf16[8,40,512]{2,1,0:T(8,128)(2,1)}), bf16[8,40,512]{2,1,0:T(8,128)(2,1)S(1)}, u32[]{:S(2)}, u32[]{:S(2)}) %all-to-all-start.5) | async-done | bytes 327712 | tf_op jit(solution)/shard_map/all_to_all | solution.py:127
  172.7 26.0 %all_to_all.41 = bf16[8,32,512]{2,1,0:T(8,128)(2,1)S(1)} all-to-all(bf16[8,32,512]{2,1,0:T(8,128)(2,1)S(1)} %broadcast_in_dim.23), channel_id=1, replica_groups={{0,32,64,96,128,160,192,224},{8,40,72,104,136,168,200,232},{16,48,80,11..., dimensions={0} | all-to-all | bytes 524288 | tf_op jit(solution)/shard_map/all_to_all | solution.py:127
  198.6 1.1 broadcast_in_dim.24
  199.7 5.7 %all-to-all-start.7 = ((bf16[4,8,32,512]{3,2,1,0:T(8,128)(2,1)}), bf16[4,8,32,512]{3,2,1,0:T(8,128)(2,1)S(1)}, u32[]{:S(2)}, u32[]{:S(2)}) async-start(bf16[4,8,32,512]{3,2,1,0:T(8,128)(2,1)} %broadcast_in_dim.24), calls=%async_computation.7 | async-start | bytes 2097152 | tf_op jit(solution)/shard_map/all_to_all | solution.py:127
  205.4 0.7 slice.79
  206.4 1.1 convert.5
  208.2 1.1 fusion.21
  209.3 10.3 %all-to-all-done.7 = bf16[4,8,32,512]{3,2,1,0:T(8,128)(2,1)S(1)} async-done(((bf16[4,8,32,512]{3,2,1,0:T(8,128)(2,1)}), bf16[4,8,32,512]{3,2,1,0:T(8,128)(2,1)S(1)}, u32[]{:S(2)}, u32[]{:S(2)}) %all-to-all-start.7) | async-done | bytes 1048608 | tf_op jit(solution)/shard_map/all_to_all | solution.py:127
  219.7 3.8 %collective-permute-start.3 = (bf16[32,24,512]{2,1,0:T(8,128)(2,1)S(1)}, bf16[32,24,512]{2,1,0:T(8,128)(2,1)S(1)}, u32[]{:S(2)}, u32[]{:S(2)}) collective-permute-start(bf16[32,24,512]{2,1,0:T(8,128)(2,1)S(1)} %slice.76), channel_id=1, source_target_pairs={{0,8},{8,0},{16,24},{24,16},{32,40},{40,32},{48,56},{56,48},{64,72... | collective-permute-start | bytes 2359304 | tf_op jit(solution)/shard_map/ppermute | solution.py:139
  223.6 0.7 fusion.30
  224.3 0.8 convolution_convert_fusion.3
  225.4 1.3 pad_maximum_fusion
  (80 shorter events, 6.1 us)
Async XLA Ops:
  7.2 65.3 %all-gather.4.cloned.1.call-start = ((), (), s32[]{:S(2)}) async-start(), calls=%async_computation.9 | async-start | bytes 3538944 | tf_op jit(solution)/shard_map/all_gather | solution.py:173
  7.2 1.0 copy-start
  10.1 0.6 copy-start.2
  10.7 7.2 %collective-permute-start = (bf16[24,512]{1,0:T(8,128)(2,1)}, bf16[24,512]{1,0:T(8,128)(2,1)S(1)}, u32[]{:S(2)}, u32[]{:S(2)}) collective-permute-start(bf16[24,512]{1,0:T(8,128)(2,1)} %param.9), channel_id=1, source_target_pairs={{0,256},{256,0},{8,264},{264,8},{16,272},{272,16},{24,280},{280,24... | collective-permute-start | bytes 73736 | tf_op jit(solution)/shard_map/ppermute | solution.py:139
  55.1 14.6 %collective-permute-start.1 = (bf16[16,48,512]{2,1,0:T(8,128)(2,1)S(1)}, bf16[16,48,512]{2,1,0:T(8,128)(2,1)}, u32[]{:S(2)}, u32[]{:S(2)}) collective-permute-start(bf16[16,48,512]{2,1,0:T(8,128)(2,1)S(1)} %slice.65), channel_id=1, source_target_pairs={{0,8},{8,0},{16,24},{24,16},{32,40},{40,32},{48,56},{56,48},{64,72... | collective-permute-start | bytes 2359304 | tf_op jit(solution)/shard_map/ppermute | solution.py:139
  65.3 16.8 %all-to-all-start = ((bf16[4,16,12,512]{3,1,2,0:T(8,128)(2,1)}), bf16[4,16,12,512]{3,1,2,0:T(8,128)(2,1)S(1)}, u32[]{:S(2)}, u32[]{:S(2)}) async-start(bf16[4,16,12,512]{3,1,2,0:T(8,128)(2,1)} %broadcast_in_dim.18), calls=%async_computation | async-start | bytes 1572864 | tf_op jit(solution)/shard_map/all_to_all | solution.py:127
  72.5 14.3 %copy-start.8 = (bf16[28,1536]{1,0:T(8,128)(2,1)S(1)}, bf16[28,1536]{1,0:T(8,128)(2,1)}, u32[]{:S(2)}) copy-start(bf16[28,1536]{1,0:T(8,128)(2,1)} %param.11) | copy-start | bytes 258052
  82.0 10.6 %all-to-all-start.1 = ((f32[8,4,1536]{2,1,0:T(4,128)}), f32[8,4,1536]{2,1,0:T(4,128)S(1)}, u32[]{:S(2)}, u32[]{:S(2)}) async-start(f32[8,4,1536]{2,1,0:T(4,128)} %get-tuple-element.25), calls=%async_computation.1 | async-start | bytes 393216 | tf_op jit(solution)/shard_map/all_to_all | solution.py:128
  94.5 12.9 %all-to-all-start.2 = ((bf16[8,32,1536]{2,1,0:T(8,128)(2,1)}), bf16[8,32,1536]{2,1,0:T(8,128)(2,1)}, u32[]{:S(2)}, u32[]{:S(2)}) async-start(bf16[8,32,1536]{2,1,0:T(8,128)(2,1)} %broadcast_in_dim.20), calls=%async_computation.2 | async-start | bytes 1572864 | tf_op jit(solution)/shard_map/all_to_all | solution.py:128
  98.7 10.2 %copy-start.3 = (bf16[512,1536]{1,0:T(8,128)(2,1)S(1)}, bf16[512,1536]{1,0:T(8,128)(2,1)}, u32[]{:S(2)}) copy-start(bf16[512,1536]{1,0:T(8,128)(2,1)} %out_ref.1) | copy-start | bytes 4718596
  109.8 2.5 %copy-start.5 = (bf16[1024,1536]{1,0:T(8,128)(2,1)S(1)}, bf16[1024,1536]{1,0:T(8,128)(2,1)}, u32[]{:S(2)}) copy-start(bf16[1024,1536]{1,0:T(8,128)(2,1)} %all-gather.4.cloned.1.call-done.x_ref) | copy-start | bytes 9437188
  112.3 1.8 copy-start.6
  126.9 3.7 %copy-start.4 = (bf16[2,16,2,24,512]{4,3,2,1,0:T(8,128)(2,1)S(1)}, bf16[2,16,2,24,512]{4,3,2,1,0:T(8,128)(2,1)}, u32[]{:S(2)}) copy-start(bf16[2,16,2,24,512]{4,3,2,1,0:T(8,128)(2,1)} %copy.37) | copy-start | bytes 4718596
  126.9 21.3 %all-to-all-start.4 = ((bf16[4,8,40,512]{3,2,1,0:T(8,128)(2,1)}), bf16[4,8,40,512]{3,2,1,0:T(8,128)(2,1)S(1)}, u32[]{:S(2)}, u32[]{:S(2)}) async-start(bf16[4,8,40,512]{3,2,1,0:T(8,128)(2,1)} %fusion.5), calls=%async_computation.4 | async-start | bytes 2621440 | tf_op jit(solution)/shard_map/all_to_all | solution.py:127
  130.6 75.8 %reduce-scatter.2.cloned.1.call-start = ((), (), s32[]{:S(2)}) async-start(), calls=%async_computation.10 | async-start | bytes 3538944 | tf_op jit(solution)/shard_map/reduce_scatter | solution.py:242
  149.5 6.3 %copy-start.9 = (bf16[4,512]{1,0:T(4,128)(2,1)S(1)}, bf16[4,512]{1,0:T(4,128)(2,1)}, u32[]{:S(2)}) copy-start(bf16[4,512]{1,0:T(4,128)(2,1)} %get-tuple-element.29) | copy-start | bytes 12292
  149.5 23.0 %all-to-all-start.5 = ((bf16[8,40,512]{2,1,0:T(8,128)(2,1)}), bf16[8,40,512]{2,1,0:T(8,128)(2,1)S(1)}, u32[]{:S(2)}, u32[]{:S(2)}) async-start(bf16[8,40,512]{2,1,0:T(8,128)(2,1)} %fusion.24), calls=%async_computation.5 | async-start | bytes 655360 | tf_op jit(solution)/shard_map/all_to_all | solution.py:127
  155.8 4.2 %collective-permute-start.2 = (bf16[4,512]{1,0:T(4,128)(2,1)S(1)}, bf16[4,512]{1,0:T(4,128)(2,1)S(1)}, u32[]{:S(2)}, u32[]{:S(2)}) collective-permute-start(bf16[4,512]{1,0:T(4,128)(2,1)S(1)} %copy-done.9), channel_id=1, source_target_pairs={{0,8},{8,0},{16,24},{24,16},{32,40},{40,32},{48,56},{56,48},{64,72... | collective-permute-start | bytes 12296 | tf_op jit(solution)/shard_map/ppermute | solution.py:139
  198.6 8.8 %copy-start.1 = (bf16[4,32,1536]{2,1,0:T(8,128)(2,1)S(1)}, bf16[4,32,1536]{2,1,0:T(8,128)(2,1)}, u32[]{:S(2)}) copy-start(bf16[4,32,1536]{2,1,0:T(8,128)(2,1)} %x_ref.1) | copy-start | bytes 1179652
  199.7 19.9 %all-to-all-start.7 = ((bf16[4,8,32,512]{3,2,1,0:T(8,128)(2,1)}), bf16[4,8,32,512]{3,2,1,0:T(8,128)(2,1)S(1)}, u32[]{:S(2)}, u32[]{:S(2)}) async-start(bf16[4,8,32,512]{3,2,1,0:T(8,128)(2,1)} %broadcast_in_dim.24), calls=%async_computation.7 | async-start | bytes 2097152 | tf_op jit(solution)/shard_map/all_to_all | solution.py:127
  207.4 16.0 %copy-start.7 = (bf16[4,1536]{1,0:T(4,128)(2,1)S(1)}, bf16[4,1536]{1,0:T(4,128)(2,1)}, u32[]{:S(2)}) copy-start(bf16[4,1536]{1,0:T(4,128)(2,1)} %param.12) | copy-start | bytes 36868
  219.7 5.7 %collective-permute-start.3 = (bf16[32,24,512]{2,1,0:T(8,128)(2,1)S(1)}, bf16[32,24,512]{2,1,0:T(8,128)(2,1)S(1)}, u32[]{:S(2)}, u32[]{:S(2)}) collective-permute-start(bf16[32,24,512]{2,1,0:T(8,128)(2,1)S(1)} %slice.76), channel_id=1, source_target_pairs={{0,8},{8,0},{16,24},{24,16},{32,40},{40,32},{48,56},{56,48},{64,72... | collective-permute-start | bytes 2359304 | tf_op jit(solution)/shard_map/ppermute | solution.py:139
Sparse Core Ops, SparseCore 0:
  10.9 54.5 all-gather.3
  149.6 43.5 reduce-scatter.1

commit v5 on v4

--- a/solution.py
+++ b/solution.py
@@ -27,22 +27,22 @@
 
 
 def norm_kernel(x_ref, normed_ref, total_ref):
-    values = x_ref[0].astype(jnp.float32)
+    values = x_ref[...].astype(jnp.float32)
     centered = values - jnp.mean(values, -1, keepdims=True)
     inv_std = lax.rsqrt(jnp.mean(centered * centered, -1, keepdims=True) + epsilon)
-    normed_ref[...] = (centered * inv_std).astype(jnp.bfloat16)
-    total_ref[0] = jnp.sum(values, 0, keepdims=True)
+    normed_ref[...] = (centered * inv_std).astype(jnp.bfloat16).reshape(normed_ref.shape)
+    total_ref[...] = jnp.sum(values, 1, keepdims=True)
 
 
 def normalize(layer_input):
     rows, patches, width = layer_input.shape
     return pl.pallas_call(
         norm_kernel,
-        grid=(rows,),
-        in_specs=[pl.BlockSpec((1, patches, width), lambda i: (i, 0, 0))],
+        grid=(2,),
+        in_specs=[pl.BlockSpec((rows // 2, patches, width), lambda i: (i, 0, 0))],
         out_specs=[
-            pl.BlockSpec((patches, width), lambda i: (i, 0)),
-            pl.BlockSpec((1, 1, width), lambda i: (i, 0, 0)),
+            pl.BlockSpec((rows // 2 * patches, width), lambda i: (i, 0)),
+            pl.BlockSpec((rows // 2, 1, width), lambda i: (i, 0, 0)),
         ],
         out_shape=[
             jax.ShapeDtypeStruct((rows * patches, width), jnp.bfloat16),
@@ -232,8 +232,8 @@
         3,
     )
     for axis in ("core", "x_hi z_lo"):
-        got = exchange(parts, axis).astype(jnp.float32)
-        parts = sum(got[k] for k in range(got.shape[0])).astype(jnp.bfloat16)
+        got = exchange(parts, axis)
+        parts = sum(got[k].astype(jnp.float32) for k in range(got.shape[0])).astype(jnp.bfloat16)
     normed_part = jnp.einsum(
         "rf,df->rd", hidden_grad, full_in, preferred_element_type=jnp.float32
     ).astype(jnp.bfloat16)

time: 235 us -> 233 us (level)
  no operation moved by 1% of the time
where the time goes in v5:
time: 233 us; the launch traced here: 232 us
  blocking collectives  72.3 us (31%)
  starting transfers between devices  50.9 us (22%)
  waiting for transfers between devices  47.1 us (20%)
  between operations  16.5 us (7%)
  other arithmetic  15.6 us (7%)
  local copies, waits for them, and re-layouts  11 us (5%)
  matrix products  9.7 us (4%)
  Pallas kernels  8.53 us (4%)
    all_to_all x4, waiting for transfers between devices, exchange(): lax.all_to_all(blocks, 'dp', 0, 0, axis_index_groups=GROUPS[axis], tiled=...  37.9 us
    all_gather x1, blocking collectives, gather_z(): lax.all_gather(block, 'dp', axis=0, axis_index_groups=GROUPS['z'], tiled=...  36.3 us
    all_to_all x2, blocking collectives, exchange(): lax.all_to_all(blocks, 'dp', 0, 0, axis_index_groups=GROUPS[axis], tiled=...  36.1 us
    ppermute x4, starting transfers between devices, pair(): lax.ppermute(block, 'dp', [p for a, b in GROUPS[axis] for p in ((a, b), (...  21.7 us
    all_to_all x4, starting transfers between devices, exchange(): lax.all_to_all(blocks, 'dp', 0, 0, axis_index_groups=GROUPS[axis], tiled=...  20.2 us
    all_to_all x2, starting transfers between devices, exchange(): return lax.all_to_all(blocks, axis, 0, 0, tiled=True)  8.96 us
    all_to_all x2, waiting for transfers between devices, exchange(): return lax.all_to_all(blocks, axis, 0, 0, tiled=True)  8.12 us
    pallas_call x1, Pallas kernels, hidden_layer(): pl.pallas_call(functools.partial(hidden_kernel, rows, patches), grid=(tok...  7.36 us
  transfers between devices with their start and end apart: 12, of which 8 were waited for; matrix products, arithmetic and copies ran while one was open for 9% of the time, Pallas kernels for 3%

profile of v5, /device:TPU:1, one launch (start us, length us, event | category | flops | bytes accessed | tf_op | source)
XLA Modules:
  0.0 231.8 jit_solution(11332383900866176252)
XLA Ops:
  7.2 1.0 copy-done
  8.2 1.2 shard_map.119
  9.4 0.6 copy-done.2
  10.0 5.5 %collective-permute-start = (bf16[24,512]{1,0:T(8,128)(2,1)}, bf16[24,512]{1,0:T(8,128)(2,1)S(1)}, u32[]{:S(2)}, u32[]{:S(2)}) collective-permute-start(bf16[24,512]{1,0:T(8,128)(2,1)} %param.9), channel_id=1, source_target_pairs={{0,256},{256,0},{8,264},{264,8},{16,272},{272,16},{24,280},{280,24... | collective-permute-start | bytes 73736 | tf_op jit(solution)/shard_map/ppermute | solution.py:139
  15.5 0.8 fusion.29
  16.4 0.8 convert_dynamic-update-slice_fusion
  17.2 0.7 select_bitcast_fusion.3
  18.0 36.3 %all-gather.1 = bf16[16,60,512]{2,1,0:T(8,128)(2,1)S(1)} all-gather(bf16[1,60,512]{2,1,0:T(8,128)(2,1)S(1)} %maximum_bitcast_fusion.1), channel_id=2, replica_groups={{0,16,32,48,64,80,96,112,128,144,160,176,192,208,224,240},{8,24,40,56,7..., dimensions={0}, use_global_device_ids=true | all-gather | bytes 1044480 | tf_op jit(solution)/shard_map/all_gather | solution.py:148
  54.4 9.0 %collective-permute-start.1 = (bf16[16,48,512]{2,1,0:T(8,128)(2,1)S(1)}, bf16[16,48,512]{2,1,0:T(8,128)(2,1)}, u32[]{:S(2)}, u32[]{:S(2)}) collective-permute-start(bf16[16,48,512]{2,1,0:T(8,128)(2,1)S(1)} %slice.65), channel_id=1, source_target_pairs={{0,8},{8,0},{16,24},{24,16},{32,40},{40,32},{48,56},{56,48},{64,72... | collective-permute-start | bytes 2359304 | tf_op jit(solution)/shard_map/ppermute | solution.py:139
  63.5 1.0 broadcast_in_dim.18
  64.5 4.5 %all-to-all-start = ((bf16[4,16,12,512]{3,1,2,0:T(8,128)(2,1)}), bf16[4,16,12,512]{3,1,2,0:T(8,128)(2,1)S(1)}, u32[]{:S(2)}, u32[]{:S(2)}) async-start(bf16[4,16,12,512]{3,1,2,0:T(8,128)(2,1)} %broadcast_in_dim.18), calls=%async_computation | async-start | bytes 1572864 | tf_op jit(solution)/shard_map/all_to_all | solution.py:127
  69.0 1.2 broadcast_select_fusion.1
  70.4 1.3 copy.37
  71.7 7.4 %shard_map.120 = (f32[1024,512]{1,0:T(8,128)}, bf16[4,512]{1,0:T(4,128)(2,1)}, f32[8,4,1536]{2,1,0:T(4,128)}) custom-call(bf16[1024,1536]{1,0:T(8,128)(2,1)} %all-gather.4.cloned.1.call-done.x_ref, bf16[1536,512]{1,0:T(8,128)(2,1)} %bitcast.65, bf16[512,1536]{1,0:T(8,128)(2,1)} %out_ref.1, f32[4,1,1536]{2,1,0:T(1,128)} %copy-done.2), custom_call_target="tpu_custom_call" | custom-call | tf_op jit(solution)/shard_map/pallas_call | solution.py:92
  79.1 2.2 all-to-all-done
  81.3 4.8 %all-to-all-start.1 = ((f32[8,4,1536]{2,1,0:T(4,128)}), f32[8,4,1536]{2,1,0:T(4,128)S(1)}, u32[]{:S(2)}, u32[]{:S(2)}) async-start(f32[8,4,1536]{2,1,0:T(4,128)} %get-tuple-element.25), calls=%async_computation.1 | async-start | bytes 393216 | tf_op jit(solution)/shard_map/all_to_all | solution.py:128
  88.1 0.6 copy.39
  89.4 2.5 %all-to-all-done.1 = f32[8,4,1536]{2,1,0:T(4,128)S(1)} async-done(((f32[8,4,1536]{2,1,0:T(4,128)}), f32[8,4,1536]{2,1,0:T(4,128)S(1)}, u32[]{:S(2)}, u32[]{:S(2)}) %all-to-all-start.1) | async-done | bytes 196640 | tf_op jit(solution)/shard_map/all_to_all | solution.py:128
  92.7 1.0 broadcast_in_dim.20
  93.7 4.2 %all-to-all-start.2 = ((bf16[8,32,1536]{2,1,0:T(8,128)(2,1)}), bf16[8,32,1536]{2,1,0:T(8,128)(2,1)}, u32[]{:S(2)}, u32[]{:S(2)}) async-start(bf16[8,32,1536]{2,1,0:T(8,128)(2,1)} %broadcast_in_dim.20), calls=%async_computation.2 | async-start | bytes 1572864 | tf_op jit(solution)/shard_map/all_to_all | solution.py:128
  98.0 1.3 convolution_convert_fusion.2
  99.3 1.7 reshape.135
  100.9 5.7 %all-to-all-done.2 = bf16[8,32,1536]{2,1,0:T(8,128)(2,1)} async-done(((bf16[8,32,1536]{2,1,0:T(8,128)(2,1)}), bf16[8,32,1536]{2,1,0:T(8,128)(2,1)}, u32[]{:S(2)}, u32[]{:S(2)}) %all-to-all-start.2) | async-done | bytes 786464 | tf_op jit(solution)/shard_map/all_to_all | solution.py:128
  106.6 1.3 convert_reduce_fusion
  108.2 0.5 convolution_multiply_fusion.1
  109.2 2.0 fusion.3
  111.6 1.8 convolution_convert_fusion.1
  113.8 10.1 %all_to_all.40 = bf16[2,4,8,40,512]{4,3,2,1,0:T(8,128)(2,1)S(1)} all-to-all(bf16[2,4,8,40,512]{4,3,2,1,0:T(8,128)(2,1)S(1)} %fusion.1), channel_id=1, replica_groups={{0,8},{16,24},{32,40},{48,56},{64,72},{80,88},{96,104},{112,120},{128,1..., dimensions={0} | all-to-all | bytes 5242880 | tf_op jit(solution)/shard_map/all_to_all | solution.py:127
  123.9 1.4 fusion.4
  125.4 3.7 %all-to-all-start.4 = ((bf16[4,8,40,512]{3,2,1,0:T(8,128)(2,1)}), bf16[4,8,40,512]{3,2,1,0:T(8,128)(2,1)S(1)}, u32[]{:S(2)}, u32[]{:S(2)}) async-start(bf16[4,8,40,512]{3,2,1,0:T(8,128)(2,1)} %fusion.4), calls=%async_computation.4 | async-start | bytes 2621440 | tf_op jit(solution)/shard_map/all_to_all | solution.py:127
  129.1 4.7 %convolution_convert_fusion = bf16[1024,1536]{1,0:T(8,128)(2,1)} fusion(bf16[1024,512]{1,0:T(8,128)(2,1)} %copy-done.6, bf16[1536,512]{1,0:T(8,128)(2,1)S(1)} %bitcast.66), kind=kOutput, calls=%fused_computation.2 | convolution fusion | flops 1612185600 | bytes 5767168 | tf_op jit(solution)/shard_map/rf,df->rd/dot_general | solution.py:237
  133.8 12.9 %all-to-all-done.4 = bf16[4,8,40,512]{3,2,1,0:T(8,128)(2,1)S(1)} async-done(((bf16[4,8,40,512]{3,2,1,0:T(8,128)(2,1)}), bf16[4,8,40,512]{3,2,1,0:T(8,128)(2,1)S(1)}, u32[]{:S(2)}, u32[]{:S(2)}) %all-to-all-start.4) | async-done | bytes 1310752 | tf_op jit(solution)/shard_map/all_to_all | solution.py:127
  146.7 0.9 fusion.22
  147.6 6.2 %all-to-all-start.5 = ((bf16[8,40,512]{2,1,0:T(8,128)(2,1)}), bf16[8,40,512]{2,1,0:T(8,128)(2,1)S(1)}, u32[]{:S(2)}, u32[]{:S(2)}) async-start(bf16[8,40,512]{2,1,0:T(8,128)(2,1)} %fusion.22), calls=%async_computation.5 | async-start | bytes 655360 | tf_op jit(solution)/shard_map/all_to_all | solution.py:127
  153.8 3.4 %collective-permute-start.2 = (bf16[4,512]{1,0:T(4,128)(2,1)S(1)}, bf16[4,512]{1,0:T(4,128)(2,1)S(1)}, u32[]{:S(2)}, u32[]{:S(2)}) collective-permute-start(bf16[4,512]{1,0:T(4,128)(2,1)S(1)} %copy-done.9), channel_id=1, source_target_pairs={{0,8},{8,0},{16,24},{24,16},{32,40},{40,32},{48,56},{56,48},{64,72... | collective-permute-start | bytes 12296 | tf_op jit(solution)/shard_map/ppermute | solution.py:139
  157.2 0.8 collective-permute-done.2
  158.1 12.5 %all-to-all-done.5 = bf16[8,40,512]{2,1,0:T(8,128)(2,1)S(1)} async-done(((bf16[8,40,512]{2,1,0:T(8,128)(2,1)}), bf16[8,40,512]{2,1,0:T(8,128)(2,1)S(1)}, u32[]{:S(2)}, u32[]{:S(2)}) %all-to-all-start.5) | async-done | bytes 327712 | tf_op jit(solution)/shard_map/all_to_all | solution.py:127
  170.7 26.0 %all_to_all.41 = bf16[8,32,512]{2,1,0:T(8,128)(2,1)S(1)} all-to-all(bf16[8,32,512]{2,1,0:T(8,128)(2,1)S(1)} %broadcast_in_dim.23), channel_id=1, replica_groups={{0,32,64,96,128,160,192,224},{8,40,72,104,136,168,200,232},{16,48,80,11..., dimensions={0} | all-to-all | bytes 524288 | tf_op jit(solution)/shard_map/all_to_all | solution.py:127
  196.7 1.1 broadcast_in_dim.24
  197.8 5.8 %all-to-all-start.7 = ((bf16[4,8,32,512]{3,2,1,0:T(8,128)(2,1)}), bf16[4,8,32,512]{3,2,1,0:T(8,128)(2,1)S(1)}, u32[]{:S(2)}, u32[]{:S(2)}) async-start(bf16[4,8,32,512]{3,2,1,0:T(8,128)(2,1)} %broadcast_in_dim.24), calls=%async_computation.7 | async-start | bytes 2097152 | tf_op jit(solution)/shard_map/all_to_all | solution.py:127
  203.6 0.7 slice.79
  204.6 1.1 convert.9
  206.4 1.1 fusion.20
  207.5 10.3 %all-to-all-done.7 = bf16[4,8,32,512]{3,2,1,0:T(8,128)(2,1)S(1)} async-done(((bf16[4,8,32,512]{3,2,1,0:T(8,128)(2,1)}), bf16[4,8,32,512]{3,2,1,0:T(8,128)(2,1)S(1)}, u32[]{:S(2)}, u32[]{:S(2)}) %all-to-all-start.7) | async-done | bytes 1048608 | tf_op jit(solution)/shard_map/all_to_all | solution.py:127
  217.8 3.8 %collective-permute-start.3 = (bf16[32,24,512]{2,1,0:T(8,128)(2,1)S(1)}, bf16[32,24,512]{2,1,0:T(8,128)(2,1)S(1)}, u32[]{:S(2)}, u32[]{:S(2)}) collective-permute-start(bf16[32,24,512]{2,1,0:T(8,128)(2,1)S(1)} %slice.76), channel_id=1, source_target_pairs={{0,8},{8,0},{16,24},{24,16},{32,40},{40,32},{48,56},{56,48},{64,72... | collective-permute-start | bytes 2359304 | tf_op jit(solution)/shard_map/ppermute | solution.py:139
  221.8 0.7 fusion.28
  222.5 0.8 convolution_convert_fusion.3
  223.6 1.3 pad_maximum_fusion
  (78 shorter events, 5.3 us)
Async XLA Ops:
  7.2 64.6 %all-gather.4.cloned.1.call-start = ((), (), s32[]{:S(2)}) async-start(), calls=%async_computation.9 | async-start | bytes 3538944 | tf_op jit(solution)/shard_map/all_gather | solution.py:173
  7.2 1.0 copy-start
  9.4 0.6 copy-start.2
  10.0 7.2 %collective-permute-start = (bf16[24,512]{1,0:T(8,128)(2,1)}, bf16[24,512]{1,0:T(8,128)(2,1)S(1)}, u32[]{:S(2)}, u32[]{:S(2)}) collective-permute-start(bf16[24,512]{1,0:T(8,128)(2,1)} %param.9), channel_id=1, source_target_pairs={{0,256},{256,0},{8,264},{264,8},{16,272},{272,16},{24,280},{280,24... | collective-permute-start | bytes 73736 | tf_op jit(solution)/shard_map/ppermute | solution.py:139
  54.4 14.6 %collective-permute-start.1 = (bf16[16,48,512]{2,1,0:T(8,128)(2,1)S(1)}, bf16[16,48,512]{2,1,0:T(8,128)(2,1)}, u32[]{:S(2)}, u32[]{:S(2)}) collective-permute-start(bf16[16,48,512]{2,1,0:T(8,128)(2,1)S(1)} %slice.65), channel_id=1, source_target_pairs={{0,8},{8,0},{16,24},{24,16},{32,40},{40,32},{48,56},{56,48},{64,72... | collective-permute-start | bytes 2359304 | tf_op jit(solution)/shard_map/ppermute | solution.py:139
  64.5 16.8 %all-to-all-start = ((bf16[4,16,12,512]{3,1,2,0:T(8,128)(2,1)}), bf16[4,16,12,512]{3,1,2,0:T(8,128)(2,1)S(1)}, u32[]{:S(2)}, u32[]{:S(2)}) async-start(bf16[4,16,12,512]{3,1,2,0:T(8,128)(2,1)} %broadcast_in_dim.18), calls=%async_computation | async-start | bytes 1572864 | tf_op jit(solution)/shard_map/all_to_all | solution.py:127
  71.7 16.3 %copy-start.8 = (bf16[28,1536]{1,0:T(8,128)(2,1)S(1)}, bf16[28,1536]{1,0:T(8,128)(2,1)}, u32[]{:S(2)}) copy-start(bf16[28,1536]{1,0:T(8,128)(2,1)} %param.11) | copy-start | bytes 258052
  81.3 10.6 %all-to-all-start.1 = ((f32[8,4,1536]{2,1,0:T(4,128)}), f32[8,4,1536]{2,1,0:T(4,128)S(1)}, u32[]{:S(2)}, u32[]{:S(2)}) async-start(f32[8,4,1536]{2,1,0:T(4,128)} %get-tuple-element.25), calls=%async_computation.1 | async-start | bytes 393216 | tf_op jit(solution)/shard_map/all_to_all | solution.py:128
  93.7 12.9 %all-to-all-start.2 = ((bf16[8,32,1536]{2,1,0:T(8,128)(2,1)}), bf16[8,32,1536]{2,1,0:T(8,128)(2,1)}, u32[]{:S(2)}, u32[]{:S(2)}) async-start(bf16[8,32,1536]{2,1,0:T(8,128)(2,1)} %broadcast_in_dim.20), calls=%async_computation.2 | async-start | bytes 1572864 | tf_op jit(solution)/shard_map/all_to_all | solution.py:128
  99.3 8.9 %copy-start.3 = (bf16[512,1536]{1,0:T(8,128)(2,1)S(1)}, bf16[512,1536]{1,0:T(8,128)(2,1)}, u32[]{:S(2)}) copy-start(bf16[512,1536]{1,0:T(8,128)(2,1)} %out_ref.1) | copy-start | bytes 4718596
  109.1 2.5 %copy-start.5 = (bf16[1024,1536]{1,0:T(8,128)(2,1)S(1)}, bf16[1024,1536]{1,0:T(8,128)(2,1)}, u32[]{:S(2)}) copy-start(bf16[1024,1536]{1,0:T(8,128)(2,1)} %all-gather.4.cloned.1.call-done.x_ref) | copy-start | bytes 9437188
  111.6 1.8 copy-start.6
  125.4 3.7 %copy-start.4 = (bf16[2,16,2,24,512]{4,3,2,1,0:T(8,128)(2,1)S(1)}, bf16[2,16,2,24,512]{4,3,2,1,0:T(8,128)(2,1)}, u32[]{:S(2)}) copy-start(bf16[2,16,2,24,512]{4,3,2,1,0:T(8,128)(2,1)} %copy.37) | copy-start | bytes 4718596
  125.4 21.3 %all-to-all-start.4 = ((bf16[4,8,40,512]{3,2,1,0:T(8,128)(2,1)}), bf16[4,8,40,512]{3,2,1,0:T(8,128)(2,1)S(1)}, u32[]{:S(2)}, u32[]{:S(2)}) async-start(bf16[4,8,40,512]{3,2,1,0:T(8,128)(2,1)} %fusion.4), calls=%async_computation.4 | async-start | bytes 2621440 | tf_op jit(solution)/shard_map/all_to_all | solution.py:127
  129.0 75.5 %reduce-scatter.2.cloned.1.call-start = ((), (), s32[]{:S(2)}) async-start(), calls=%async_computation.10 | async-start | bytes 3538944 | tf_op jit(solution)/shard_map/reduce_scatter | solution.py:242
  147.6 6.3 %copy-start.9 = (bf16[4,512]{1,0:T(4,128)(2,1)S(1)}, bf16[4,512]{1,0:T(4,128)(2,1)}, u32[]{:S(2)}) copy-start(bf16[4,512]{1,0:T(4,128)(2,1)} %get-tuple-element.29) | copy-start | bytes 12292
  147.6 23.0 %all-to-all-start.5 = ((bf16[8,40,512]{2,1,0:T(8,128)(2,1)}), bf16[8,40,512]{2,1,0:T(8,128)(2,1)S(1)}, u32[]{:S(2)}, u32[]{:S(2)}) async-start(bf16[8,40,512]{2,1,0:T(8,128)(2,1)} %fusion.22), calls=%async_computation.5 | async-start | bytes 655360 | tf_op jit(solution)/shard_map/all_to_all | solution.py:127
  153.8 4.2 %collective-permute-start.2 = (bf16[4,512]{1,0:T(4,128)(2,1)S(1)}, bf16[4,512]{1,0:T(4,128)(2,1)S(1)}, u32[]{:S(2)}, u32[]{:S(2)}) collective-permute-start(bf16[4,512]{1,0:T(4,128)(2,1)S(1)} %copy-done.9), channel_id=1, source_target_pairs={{0,8},{8,0},{16,24},{24,16},{32,40},{40,32},{48,56},{56,48},{64,72... | collective-permute-start | bytes 12296 | tf_op jit(solution)/shard_map/ppermute | solution.py:139
  197.8 7.8 %copy-start.1 = (bf16[4,32,1536]{2,1,0:T(8,128)(2,1)S(1)}, bf16[4,32,1536]{2,1,0:T(8,128)(2,1)}, u32[]{:S(2)}) copy-start(bf16[4,32,1536]{2,1,0:T(8,128)(2,1)} %x_ref.1) | copy-start | bytes 1179652
  197.8 20.0 %all-to-all-start.7 = ((bf16[4,8,32,512]{3,2,1,0:T(8,128)(2,1)}), bf16[4,8,32,512]{3,2,1,0:T(8,128)(2,1)S(1)}, u32[]{:S(2)}, u32[]{:S(2)}) async-start(bf16[4,8,32,512]{3,2,1,0:T(8,128)(2,1)} %broadcast_in_dim.24), calls=%async_computation.7 | async-start | bytes 2097152 | tf_op jit(solution)/shard_map/all_to_all | solution.py:127
  206.0 15.6 %copy-start.7 = (bf16[4,1536]{1,0:T(4,128)(2,1)S(1)}, bf16[4,1536]{1,0:T(4,128)(2,1)}, u32[]{:S(2)}) copy-start(bf16[4,1536]{1,0:T(4,128)(2,1)} %param.12) | copy-start | bytes 36868
  217.8 5.7 %collective-permute-start.3 = (bf16[32,24,512]{2,1,0:T(8,128)(2,1)S(1)}, bf16[32,24,512]{2,1,0:T(8,128)(2,1)S(1)}, u32[]{:S(2)}, u32[]{:S(2)}) collective-permute-start(bf16[32,24,512]{2,1,0:T(8,128)(2,1)S(1)} %slice.76), channel_id=1, source_target_pairs={{0,8},{8,0},{16,24},{24,16},{32,40},{40,32},{48,56},{56,48},{64,72... | collective-permute-start | bytes 2359304 | tf_op jit(solution)/shard_map/ppermute | solution.py:139
Sparse Core Ops, SparseCore 0:
  10.7 54.5 all-gather.3
  147.7 43.7 reduce-scatter.1

commit v6 on v5

--- a/solution.py
+++ b/solution.py
@@ -81,14 +81,14 @@
         act_ref[...] = act_mean
         part = jnp.dot(act_mean, out_ref[...], preferred_element_type=jnp.float32)
         part = part + total_ref[:, 0] * (1.0 / (8 * patches))
-        part_ref[...] = jnp.broadcast_to(part[None], part_ref.shape)
+        part_ref[...] = jnp.broadcast_to(part.astype(jnp.bfloat16)[None], part_ref.shape)
 
 
 def hidden_layer(flat, full_in, out_weight, totals, patches):
     tokens, width = flat.shape
     units = full_in.shape[1]
     rows = totals.shape[0]
-    block = 2 * rows * patches
+    block = 4 * rows * patches
     return pl.pallas_call(
         functools.partial(hidden_kernel, rows, patches),
         grid=(tokens // block,),
@@ -106,7 +106,7 @@
         out_shape=[
             jax.ShapeDtypeStruct((tokens, units), jnp.float32),
             jax.ShapeDtypeStruct((rows, units), jnp.bfloat16),
-            jax.ShapeDtypeStruct((8, rows, width), jnp.float32),
+            jax.ShapeDtypeStruct((8, rows, width), jnp.bfloat16),
         ],
         scratch_shapes=[pltpu.VMEM((rows, units), jnp.float32)],
         compiler_params=pltpu.CompilerParams(vmem_limit_bytes=60 * 1024 * 1024),
@@ -187,7 +187,7 @@
     part_pool, texts = lax.optimization_barrier((part_pool, texts))
     texts = jnp.transpose(texts.reshape(4, 8, 2, text_rows, hidden_width), (0, 2, 1, 3, 4))
     texts = texts.reshape(dp_count * text_count, width_model)
-    pooled = jnp.sum(exchange(part_pool, "mp"), 0)
+    pooled = jnp.sum(exchange(part_pool, "mp").astype(jnp.float32), 0)
     images = jnp.concatenate([pooled, image_rest.astype(jnp.float32)], 0)
     image_unit, image_inv = unit_rows(images)
     image_low = image_unit.astype(jnp.bfloat16)

time: 233 us -> 232 us (level)
  transfers between devices with their start and end apart: 12 -> 12, of which waited for: 8 -> 8; matrix products, arithmetic and copies ran while one was open for 9% -> 10% of each run, Pallas kernels for 3% -> 3%
where the time goes in v6:
time: 232 us; the launch traced here: 231 us
  blocking collectives  72.4 us (31%)
  starting transfers between devices  50.9 us (22%)
  waiting for transfers between devices  47.1 us (20%)
  between operations  16.5 us (7%)
  other arithmetic  15.7 us (7%)
  local copies, waits for them, and re-layouts  11 us (5%)
  matrix products  9.7 us (4%)
  Pallas kernels  7.95 us (3%)
    all_to_all x4, waiting for transfers between devices, exchange(): lax.all_to_all(blocks, 'dp', 0, 0, axis_index_groups=GROUPS[axis], tiled=...  38.5 us
    all_gather x1, blocking collectives, gather_z(): lax.all_gather(block, 'dp', axis=0, axis_index_groups=GROUPS['z'], tiled=...  36.3 us
    all_to_all x2, blocking collectives, exchange(): lax.all_to_all(blocks, 'dp', 0, 0, axis_index_groups=GROUPS[axis], tiled=...  36.1 us
    ppermute x4, starting transfers between devices, pair(): lax.ppermute(block, 'dp', [p for a, b in GROUPS[axis] for p in ((a, b), (...  21.7 us
    all_to_all x4, starting transfers between devices, exchange(): lax.all_to_all(blocks, 'dp', 0, 0, axis_index_groups=GROUPS[axis], tiled=...  20.2 us
    all_to_all x2, starting transfers between devices, exchange(): return lax.all_to_all(blocks, axis, 0, 0, tiled=True)  8.96 us
    all_to_all x2, waiting for transfers between devices, exchange(): return lax.all_to_all(blocks, axis, 0, 0, tiled=True)  7.56 us
    pallas_call x1, Pallas kernels, hidden_layer(): pl.pallas_call(functools.partial(hidden_kernel, rows, patches), grid=(tok...  6.79 us
  transfers between devices with their start and end apart: 12, of which 8 were waited for; matrix products, arithmetic and copies ran while one was open for 10% of the time, Pallas kernels for 3%

profile of v6, /device:TPU:1, one launch (start us, length us, event | category | flops | bytes accessed | tf_op | source)
XLA Modules:
  0.0 231.2 jit_solution(10461219219727445812)
XLA Ops:
  7.2 1.0 copy-done
  8.2 1.2 shard_map.119
  9.4 0.6 copy-done.2
  10.0 5.5 %collective-permute-start = (bf16[24,512]{1,0:T(8,128)(2,1)}, bf16[24,512]{1,0:T(8,128)(2,1)S(1)}, u32[]{:S(2)}, u32[]{:S(2)}) collective-permute-start(bf16[24,512]{1,0:T(8,128)(2,1)} %param.9), channel_id=1, source_target_pairs={{0,256},{256,0},{8,264},{264,8},{16,272},{272,16},{24,280},{280,24... | collective-permute-start | bytes 73736 | tf_op jit(solution)/shard_map/ppermute | solution.py:139
  15.5 0.8 fusion.29
  16.4 0.8 convert_dynamic-update-slice_fusion
  17.2 0.7 select_bitcast_fusion.3
  18.0 36.3 %all-gather.1 = bf16[16,60,512]{2,1,0:T(8,128)(2,1)S(1)} all-gather(bf16[1,60,512]{2,1,0:T(8,128)(2,1)S(1)} %maximum_bitcast_fusion.1), channel_id=2, replica_groups={{0,16,32,48,64,80,96,112,128,144,160,176,192,208,224,240},{8,24,40,56,7..., dimensions={0}, use_global_device_ids=true | all-gather | bytes 1044480 | tf_op jit(solution)/shard_map/all_gather | solution.py:148
  54.4 9.0 %collective-permute-start.1 = (bf16[16,48,512]{2,1,0:T(8,128)(2,1)S(1)}, bf16[16,48,512]{2,1,0:T(8,128)(2,1)}, u32[]{:S(2)}, u32[]{:S(2)}) collective-permute-start(bf16[16,48,512]{2,1,0:T(8,128)(2,1)S(1)} %slice.65), channel_id=1, source_target_pairs={{0,8},{8,0},{16,24},{24,16},{32,40},{40,32},{48,56},{56,48},{64,72... | collective-permute-start | bytes 2359304 | tf_op jit(solution)/shard_map/ppermute | solution.py:139
  63.5 1.0 broadcast_in_dim.18
  64.5 4.5 %all-to-all-start = ((bf16[4,16,12,512]{3,1,2,0:T(8,128)(2,1)}), bf16[4,16,12,512]{3,1,2,0:T(8,128)(2,1)S(1)}, u32[]{:S(2)}, u32[]{:S(2)}) async-start(bf16[4,16,12,512]{3,1,2,0:T(8,128)(2,1)} %broadcast_in_dim.18), calls=%async_computation | async-start | bytes 1572864 | tf_op jit(solution)/shard_map/all_to_all | solution.py:127
  69.0 1.2 broadcast_select_fusion.1
  70.4 1.3 copy.37
  71.7 6.8 %shard_map.120 = (f32[1024,512]{1,0:T(8,128)}, bf16[4,512]{1,0:T(4,128)(2,1)}, bf16[8,4,1536]{2,1,0:T(4,128)(2,1)}) custom-call(bf16[1024,1536]{1,0:T(8,128)(2,1)} %all-gather.4.cloned.1.call-done.x_ref, bf16[1536,512]{1,0:T(8,128)(2,1)} %bitcast.65, bf16[512,1536]{1,0:T(8,128)(2,1)} %out_ref.1, f32[4,1,1536]{2,1,0:T(1,128)} %copy-done.2), custom_call_target="tpu_custom_call" | custom-call | tf_op jit(solution)/shard_map/pallas_call | solution.py:92
  78.5 2.8 %all-to-all-done = bf16[4,16,12,512]{3,1,2,0:T(8,128)(2,1)S(1)} async-done(((bf16[4,16,12,512]{3,1,2,0:T(8,128)(2,1)}), bf16[4,16,12,512]{3,1,2,0:T(8,128)(2,1)S(1)}, u32[]{:S(2)}, u32[]{:S(2)}) %all-to-all-start) | async-done | bytes 786464 | tf_op jit(solution)/shard_map/all_to_all | solution.py:127
  81.3 4.8 %all-to-all-start.1 = ((bf16[8,4,1536]{2,1,0:T(4,128)(2,1)}), bf16[8,4,1536]{2,1,0:T(4,128)(2,1)S(1)}, u32[]{:S(2)}, u32[]{:S(2)}) async-start(bf16[8,4,1536]{2,1,0:T(4,128)(2,1)} %get-tuple-element.25), calls=%async_computation.1 | async-start | bytes 196608 | tf_op jit(solution)/shard_map/all_to_all | solution.py:128
  88.1 0.6 copy.39
  89.4 1.9 all-to-all-done.1
  92.2 1.0 broadcast_in_dim.20
  93.2 4.2 %all-to-all-start.2 = ((bf16[8,32,1536]{2,1,0:T(8,128)(2,1)}), bf16[8,32,1536]{2,1,0:T(8,128)(2,1)}, u32[]{:S(2)}, u32[]{:S(2)}) async-start(bf16[8,32,1536]{2,1,0:T(8,128)(2,1)} %broadcast_in_dim.20), calls=%async_computation.2 | async-start | bytes 1572864 | tf_op jit(solution)/shard_map/all_to_all | solution.py:128
  97.5 1.3 convolution_convert_fusion.2
  98.7 1.7 reshape.135
  100.4 5.6 %all-to-all-done.2 = bf16[8,32,1536]{2,1,0:T(8,128)(2,1)} async-done(((bf16[8,32,1536]{2,1,0:T(8,128)(2,1)}), bf16[8,32,1536]{2,1,0:T(8,128)(2,1)}, u32[]{:S(2)}, u32[]{:S(2)}) %all-to-all-start.2) | async-done | bytes 786464 | tf_op jit(solution)/shard_map/all_to_all | solution.py:128
  106.0 1.3 convert_reduce_fusion
  107.6 0.5 convolution_multiply_fusion.1
  108.6 2.0 fusion.3
  111.0 1.8 convolution_convert_fusion.1
  113.3 10.1 %all_to_all.40 = bf16[2,4,8,40,512]{4,3,2,1,0:T(8,128)(2,1)S(1)} all-to-all(bf16[2,4,8,40,512]{4,3,2,1,0:T(8,128)(2,1)S(1)} %fusion.1), channel_id=1, replica_groups={{0,8},{16,24},{32,40},{48,56},{64,72},{80,88},{96,104},{112,120},{128,1..., dimensions={0} | all-to-all | bytes 5242880 | tf_op jit(solution)/shard_map/all_to_all | solution.py:127
  123.4 1.4 fusion.4
  124.8 3.7 %all-to-all-start.4 = ((bf16[4,8,40,512]{3,2,1,0:T(8,128)(2,1)}), bf16[4,8,40,512]{3,2,1,0:T(8,128)(2,1)S(1)}, u32[]{:S(2)}, u32[]{:S(2)}) async-start(bf16[4,8,40,512]{3,2,1,0:T(8,128)(2,1)} %fusion.4), calls=%async_computation.4 | async-start | bytes 2621440 | tf_op jit(solution)/shard_map/all_to_all | solution.py:127
  128.6 4.7 %convolution_convert_fusion = bf16[1024,1536]{1,0:T(8,128)(2,1)} fusion(bf16[1024,512]{1,0:T(8,128)(2,1)} %copy-done.6, bf16[1536,512]{1,0:T(8,128)(2,1)S(1)} %bitcast.66), kind=kOutput, calls=%fused_computation.2 | convolution fusion | flops 1612185600 | bytes 5767168 | tf_op jit(solution)/shard_map/rf,df->rd/dot_general | solution.py:237
  133.3 12.9 %all-to-all-done.4 = bf16[4,8,40,512]{3,2,1,0:T(8,128)(2,1)S(1)} async-done(((bf16[4,8,40,512]{3,2,1,0:T(8,128)(2,1)}), bf16[4,8,40,512]{3,2,1,0:T(8,128)(2,1)S(1)}, u32[]{:S(2)}, u32[]{:S(2)}) %all-to-all-start.4) | async-done | bytes 1310752 | tf_op jit(solution)/shard_map/all_to_all | solution.py:127
  146.1 0.9 fusion.22
  147.1 6.2 %all-to-all-start.5 = ((bf16[8,40,512]{2,1,0:T(8,128)(2,1)}), bf16[8,40,512]{2,1,0:T(8,128)(2,1)S(1)}, u32[]{:S(2)}, u32[]{:S(2)}) async-start(bf16[8,40,512]{2,1,0:T(8,128)(2,1)} %fusion.22), calls=%async_computation.5 | async-start | bytes 655360 | tf_op jit(solution)/shard_map/all_to_all | solution.py:127
  153.3 3.4 %collective-permute-start.2 = (bf16[4,512]{1,0:T(4,128)(2,1)S(1)}, bf16[4,512]{1,0:T(4,128)(2,1)S(1)}, u32[]{:S(2)}, u32[]{:S(2)}) collective-permute-start(bf16[4,512]{1,0:T(4,128)(2,1)S(1)} %copy-done.9), channel_id=1, source_target_pairs={{0,8},{8,0},{16,24},{24,16},{32,40},{40,32},{48,56},{56,48},{64,72... | collective-permute-start | bytes 12296 | tf_op jit(solution)/shard_map/ppermute | solution.py:139
  156.7 0.8 collective-permute-done.2
  157.6 12.5 %all-to-all-done.5 = bf16[8,40,512]{2,1,0:T(8,128)(2,1)S(1)} async-done(((bf16[8,40,512]{2,1,0:T(8,128)(2,1)}), bf16[8,40,512]{2,1,0:T(8,128)(2,1)S(1)}, u32[]{:S(2)}, u32[]{:S(2)}) %all-to-all-start.5) | async-done | bytes 327712 | tf_op jit(solution)/shard_map/all_to_all | solution.py:127
  170.2 26.0 %all_to_all.41 = bf16[8,32,512]{2,1,0:T(8,128)(2,1)S(1)} all-to-all(bf16[8,32,512]{2,1,0:T(8,128)(2,1)S(1)} %broadcast_in_dim.23), channel_id=1, replica_groups={{0,32,64,96,128,160,192,224},{8,40,72,104,136,168,200,232},{16,48,80,11..., dimensions={0} | all-to-all | bytes 524288 | tf_op jit(solution)/shard_map/all_to_all | solution.py:127
  196.2 1.1 broadcast_in_dim.24
  197.3 5.8 %all-to-all-start.7 = ((bf16[4,8,32,512]{3,2,1,0:T(8,128)(2,1)}), bf16[4,8,32,512]{3,2,1,0:T(8,128)(2,1)S(1)}, u32[]{:S(2)}, u32[]{:S(2)}) async-start(bf16[4,8,32,512]{3,2,1,0:T(8,128)(2,1)} %broadcast_in_dim.24), calls=%async_computation.7 | async-start | bytes 2097152 | tf_op jit(solution)/shard_map/all_to_all | solution.py:127
  203.1 0.7 slice.79
  204.0 1.1 convert.9
  205.9 1.1 fusion.20
  207.0 10.3 %all-to-all-done.7 = bf16[4,8,32,512]{3,2,1,0:T(8,128)(2,1)S(1)} async-done(((bf16[4,8,32,512]{3,2,1,0:T(8,128)(2,1)}), bf16[4,8,32,512]{3,2,1,0:T(8,128)(2,1)S(1)}, u32[]{:S(2)}, u32[]{:S(2)}) %all-to-all-start.7) | async-done | bytes 1048608 | tf_op jit(solution)/shard_map/all_to_all | solution.py:127
  217.3 3.8 %collective-permute-start.3 = (bf16[32,24,512]{2,1,0:T(8,128)(2,1)S(1)}, bf16[32,24,512]{2,1,0:T(8,128)(2,1)S(1)}, u32[]{:S(2)}, u32[]{:S(2)}) collective-permute-start(bf16[32,24,512]{2,1,0:T(8,128)(2,1)S(1)} %slice.76), channel_id=1, source_target_pairs={{0,8},{8,0},{16,24},{24,16},{32,40},{40,32},{48,56},{56,48},{64,72... | collective-permute-start | bytes 2359304 | tf_op jit(solution)/shard_map/ppermute | solution.py:139
  221.3 0.7 fusion.28
  222.0 0.8 convolution_convert_fusion.3
  223.1 1.3 pad_maximum_fusion
  (78 shorter events, 5.3 us)
Async XLA Ops:
  7.2 64.6 %all-gather.4.cloned.1.call-start = ((), (), s32[]{:S(2)}) async-start(), calls=%async_computation.9 | async-start | bytes 3538944 | tf_op jit(solution)/shard_map/all_gather | solution.py:173
  7.2 1.0 copy-start
  9.4 0.6 copy-start.2
  10.0 7.2 %collective-permute-start = (bf16[24,512]{1,0:T(8,128)(2,1)}, bf16[24,512]{1,0:T(8,128)(2,1)S(1)}, u32[]{:S(2)}, u32[]{:S(2)}) collective-permute-start(bf16[24,512]{1,0:T(8,128)(2,1)} %param.9), channel_id=1, source_target_pairs={{0,256},{256,0},{8,264},{264,8},{16,272},{272,16},{24,280},{280,24... | collective-permute-start | bytes 73736 | tf_op jit(solution)/shard_map/ppermute | solution.py:139
  54.4 14.6 %collective-permute-start.1 = (bf16[16,48,512]{2,1,0:T(8,128)(2,1)S(1)}, bf16[16,48,512]{2,1,0:T(8,128)(2,1)}, u32[]{:S(2)}, u32[]{:S(2)}) collective-permute-start(bf16[16,48,512]{2,1,0:T(8,128)(2,1)S(1)} %slice.65), channel_id=1, source_target_pairs={{0,8},{8,0},{16,24},{24,16},{32,40},{40,32},{48,56},{56,48},{64,72... | collective-permute-start | bytes 2359304 | tf_op jit(solution)/shard_map/ppermute | solution.py:139
  64.5 16.8 %all-to-all-start = ((bf16[4,16,12,512]{3,1,2,0:T(8,128)(2,1)}), bf16[4,16,12,512]{3,1,2,0:T(8,128)(2,1)S(1)}, u32[]{:S(2)}, u32[]{:S(2)}) async-start(bf16[4,16,12,512]{3,1,2,0:T(8,128)(2,1)} %broadcast_in_dim.18), calls=%async_computation | async-start | bytes 1572864 | tf_op jit(solution)/shard_map/all_to_all | solution.py:127
  71.7 16.3 %copy-start.8 = (bf16[28,1536]{1,0:T(8,128)(2,1)S(1)}, bf16[28,1536]{1,0:T(8,128)(2,1)}, u32[]{:S(2)}) copy-start(bf16[28,1536]{1,0:T(8,128)(2,1)} %param.11) | copy-start | bytes 258052
  81.3 10.0 %all-to-all-start.1 = ((bf16[8,4,1536]{2,1,0:T(4,128)(2,1)}), bf16[8,4,1536]{2,1,0:T(4,128)(2,1)S(1)}, u32[]{:S(2)}, u32[]{:S(2)}) async-start(bf16[8,4,1536]{2,1,0:T(4,128)(2,1)} %get-tuple-element.25), calls=%async_computation.1 | async-start | bytes 196608 | tf_op jit(solution)/shard_map/all_to_all | solution.py:128
  93.2 12.8 %all-to-all-start.2 = ((bf16[8,32,1536]{2,1,0:T(8,128)(2,1)}), bf16[8,32,1536]{2,1,0:T(8,128)(2,1)}, u32[]{:S(2)}, u32[]{:S(2)}) async-start(bf16[8,32,1536]{2,1,0:T(8,128)(2,1)} %broadcast_in_dim.20), calls=%async_computation.2 | async-start | bytes 1572864 | tf_op jit(solution)/shard_map/all_to_all | solution.py:128
  98.7 8.9 %copy-start.3 = (bf16[512,1536]{1,0:T(8,128)(2,1)S(1)}, bf16[512,1536]{1,0:T(8,128)(2,1)}, u32[]{:S(2)}) copy-start(bf16[512,1536]{1,0:T(8,128)(2,1)} %out_ref.1) | copy-start | bytes 4718596
  108.5 2.5 %copy-start.5 = (bf16[1024,1536]{1,0:T(8,128)(2,1)S(1)}, bf16[1024,1536]{1,0:T(8,128)(2,1)}, u32[]{:S(2)}) copy-start(bf16[1024,1536]{1,0:T(8,128)(2,1)} %all-gather.4.cloned.1.call-done.x_ref) | copy-start | bytes 9437188
  111.0 1.8 copy-start.6
  124.8 3.7 %copy-start.4 = (bf16[2,16,2,24,512]{4,3,2,1,0:T(8,128)(2,1)S(1)}, bf16[2,16,2,24,512]{4,3,2,1,0:T(8,128)(2,1)}, u32[]{:S(2)}) copy-start(bf16[2,16,2,24,512]{4,3,2,1,0:T(8,128)(2,1)} %copy.37) | copy-start | bytes 4718596
  124.8 21.3 %all-to-all-start.4 = ((bf16[4,8,40,512]{3,2,1,0:T(8,128)(2,1)}), bf16[4,8,40,512]{3,2,1,0:T(8,128)(2,1)S(1)}, u32[]{:S(2)}, u32[]{:S(2)}) async-start(bf16[4,8,40,512]{3,2,1,0:T(8,128)(2,1)} %fusion.4), calls=%async_computation.4 | async-start | bytes 2621440 | tf_op jit(solution)/shard_map/all_to_all | solution.py:127
  128.5 75.5 %reduce-scatter.2.cloned.1.call-start = ((), (), s32[]{:S(2)}) async-start(), calls=%async_computation.10 | async-start | bytes 3538944 | tf_op jit(solution)/shard_map/reduce_scatter | solution.py:242
  147.0 6.3 %copy-start.9 = (bf16[4,512]{1,0:T(4,128)(2,1)S(1)}, bf16[4,512]{1,0:T(4,128)(2,1)}, u32[]{:S(2)}) copy-start(bf16[4,512]{1,0:T(4,128)(2,1)} %get-tuple-element.29) | copy-start | bytes 12292
  147.1 23.0 %all-to-all-start.5 = ((bf16[8,40,512]{2,1,0:T(8,128)(2,1)}), bf16[8,40,512]{2,1,0:T(8,128)(2,1)S(1)}, u32[]{:S(2)}, u32[]{:S(2)}) async-start(bf16[8,40,512]{2,1,0:T(8,128)(2,1)} %fusion.22), calls=%async_computation.5 | async-start | bytes 655360 | tf_op jit(solution)/shard_map/all_to_all | solution.py:127
  153.3 4.2 %collective-permute-start.2 = (bf16[4,512]{1,0:T(4,128)(2,1)S(1)}, bf16[4,512]{1,0:T(4,128)(2,1)S(1)}, u32[]{:S(2)}, u32[]{:S(2)}) collective-permute-start(bf16[4,512]{1,0:T(4,128)(2,1)S(1)} %copy-done.9), channel_id=1, source_target_pairs={{0,8},{8,0},{16,24},{24,16},{32,40},{40,32},{48,56},{56,48},{64,72... | collective-permute-start | bytes 12296 | tf_op jit(solution)/shard_map/ppermute | solution.py:139
  197.3 7.8 %copy-start.1 = (bf16[4,32,1536]{2,1,0:T(8,128)(2,1)S(1)}, bf16[4,32,1536]{2,1,0:T(8,128)(2,1)}, u32[]{:S(2)}) copy-start(bf16[4,32,1536]{2,1,0:T(8,128)(2,1)} %x_ref.1) | copy-start | bytes 1179652
  197.3 20.0 %all-to-all-start.7 = ((bf16[4,8,32,512]{3,2,1,0:T(8,128)(2,1)}), bf16[4,8,32,512]{3,2,1,0:T(8,128)(2,1)S(1)}, u32[]{:S(2)}, u32[]{:S(2)}) async-start(bf16[4,8,32,512]{3,2,1,0:T(8,128)(2,1)} %broadcast_in_dim.24), calls=%async_computation.7 | async-start | bytes 2097152 | tf_op jit(solution)/shard_map/all_to_all | solution.py:127
  205.5 15.6 %copy-start.7 = (bf16[4,1536]{1,0:T(4,128)(2,1)S(1)}, bf16[4,1536]{1,0:T(4,128)(2,1)}, u32[]{:S(2)}) copy-start(bf16[4,1536]{1,0:T(4,128)(2,1)} %param.12) | copy-start | bytes 36868
  217.3 5.7 %collective-permute-start.3 = (bf16[32,24,512]{2,1,0:T(8,128)(2,1)S(1)}, bf16[32,24,512]{2,1,0:T(8,128)(2,1)S(1)}, u32[]{:S(2)}, u32[]{:S(2)}) collective-permute-start(bf16[32,24,512]{2,1,0:T(8,128)(2,1)S(1)} %slice.76), channel_id=1, source_target_pairs={{0,8},{8,0},{16,24},{24,16},{32,40},{40,32},{48,56},{56,48},{64,72... | collective-permute-start | bytes 2359304 | tf_op jit(solution)/shard_map/ppermute | solution.py:139
Sparse Core Ops, SparseCore 0:
  10.7 54.5 all-gather.3
  147.2 43.4 reduce-scatter.1

commit v7 on v6

--- a/solution.py
+++ b/solution.py
@@ -174,7 +174,7 @@
     both = gather_z(near)
     full_in = pair(both[:, : 2 * in_rows], "core").reshape(2, 16, 2, in_rows, hidden_width)
     full_in = jnp.transpose(full_in, (2, 1, 0, 3, 4)).reshape(width_model, hidden_width)
-    texts = spread(both[:, 2 * in_rows :], "core x_hi")
+    texts = spread(both[:, 2 * in_rows :], "x_hi")
 
     first_row = lax.axis_index("mp") * text_count
     zero_index = jnp.zeros((), jnp.int32)
@@ -185,6 +185,7 @@
     )
     slope, act_mean, part_pool = hidden_layer(flat, full_in, out_weight, totals, local_patches)
     part_pool, texts = lax.optimization_barrier((part_pool, texts))
+    texts = pair(texts, "core")
     texts = jnp.transpose(texts.reshape(4, 8, 2, text_rows, hidden_width), (0, 2, 1, 3, 4))
     texts = texts.reshape(dp_count * text_count, width_model)
     pooled = jnp.sum(exchange(part_pool, "mp").astype(jnp.float32), 0)

time: 232 us -> 234 us (level)
  starting transfers between devices: 50.9 us -> 58.2 us
  blocking collectives: 72.4 us -> 68.8 us
    all_to_all x2, blocking collectives: 36.1 us -> 32.6 us  [exchange(): lax.all_to_all(blocks, 'dp', 0, 0, axis_index_groups=GROUPS[axis], tiled=...]
    all_to_all x4, starting transfers between devices: 20.2 us -> 23.1 us  [exchange(): lax.all_to_all(blocks, 'dp', 0, 0, axis_index_groups=GROUPS[axis], tiled=...]
    all_to_all x4, waiting for transfers between devices: 38.5 us -> 35.6 us  [exchange(): lax.all_to_all(blocks, 'dp', 0, 0, axis_index_groups=GROUPS[axis], tiled=...]
    ppermute x4 -> x5, starting transfers between devices: 21.7 us -> 24.4 us  [pair(): lax.ppermute(block, 'dp', [p for a, b in GROUPS[axis] for p in ((a, b), (...]
  transfers between devices with their start and end apart: 12 -> 13, of which waited for: 8 -> 8; matrix products, arithmetic and copies ran while one was open for 10% -> 8% of each run, Pallas kernels for 3% -> 3%
where the time goes in v7:
time: 234 us; the launch traced here: 233 us
  blocking collectives  68.8 us (29%)
  starting transfers between devices  58.2 us (25%)
  waiting for transfers between devices  46.6 us (20%)
  between operations  16.5 us (7%)
  other arithmetic  14.6 us (6%)
  local copies, waits for them, and re-layouts  10.8 us (5%)
  matrix products  9.68 us (4%)
  Pallas kernels  7.95 us (3%)
    all_gather x1, blocking collectives, gather_z(): lax.all_gather(block, 'dp', axis=0, axis_index_groups=GROUPS['z'], tiled=...  36.3 us
    all_to_all x4, waiting for transfers between devices, exchange(): lax.all_to_all(blocks, 'dp', 0, 0, axis_index_groups=GROUPS[axis], tiled=...  35.6 us
    all_to_all x2, blocking collectives, exchange(): lax.all_to_all(blocks, 'dp', 0, 0, axis_index_groups=GROUPS[axis], tiled=...  32.6 us
    ppermute x5, starting transfers between devices, pair(): lax.ppermute(block, 'dp', [p for a, b in GROUPS[axis] for p in ((a, b), (...  24.4 us
    all_to_all x4, starting transfers between devices, exchange(): lax.all_to_all(blocks, 'dp', 0, 0, axis_index_groups=GROUPS[axis], tiled=...  23.1 us
    all_to_all x2, starting transfers between devices, exchange(): return lax.all_to_all(blocks, axis, 0, 0, tiled=True)  10.6 us
    all_to_all x2, waiting for transfers between devices, exchange(): return lax.all_to_all(blocks, axis, 0, 0, tiled=True)  9.47 us
    pallas_call x1, Pallas kernels, hidden_layer(): pl.pallas_call(functools.partial(hidden_kernel, rows, patches), grid=(tok...  6.79 us
  transfers between devices with their start and end apart: 13, of which 8 were waited for; matrix products, arithmetic and copies ran while one was open for 8% of the time, Pallas kernels for 3%

profile of v7, /device:TPU:1, one launch (start us, length us, event | category | flops | bytes accessed | tf_op | source)
XLA Modules:
  0.0 233.2 jit_solution(8458203788173874217)
XLA Ops:
  7.2 1.0 copy-done
  8.2 1.2 shard_map.119
  9.4 0.6 copy-done.2
  10.0 5.5 %collective-permute-start = (bf16[24,512]{1,0:T(8,128)(2,1)}, bf16[24,512]{1,0:T(8,128)(2,1)S(1)}, u32[]{:S(2)}, u32[]{:S(2)}) collective-permute-start(bf16[24,512]{1,0:T(8,128)(2,1)} %param.9), channel_id=1, source_target_pairs={{0,256},{256,0},{8,264},{264,8},{16,272},{272,16},{24,280},{280,24... | collective-permute-start | bytes 73736 | tf_op jit(solution)/shard_map/ppermute | solution.py:139
  15.5 0.8 fusion.29
  16.4 0.8 convert_dynamic-update-slice_fusion
  17.2 0.7 select_bitcast_fusion.5
  18.0 36.3 %all-gather.1 = bf16[16,60,512]{2,1,0:T(8,128)(2,1)S(1)} all-gather(bf16[1,60,512]{2,1,0:T(8,128)(2,1)S(1)} %maximum_bitcast_fusion.1), channel_id=2, replica_groups={{0,16,32,48,64,80,96,112,128,144,160,176,192,208,224,240},{8,24,40,56,7..., dimensions={0}, use_global_device_ids=true | all-gather | bytes 1044480 | tf_op jit(solution)/shard_map/all_gather | solution.py:148
  54.4 9.0 %collective-permute-start.1 = (bf16[16,48,512]{2,1,0:T(8,128)(2,1)S(1)}, bf16[16,48,512]{2,1,0:T(8,128)(2,1)S(1)}, u32[]{:S(2)}, u32[]{:S(2)}) collective-permute-start(bf16[16,48,512]{2,1,0:T(8,128)(2,1)S(1)} %slice.65), channel_id=1, source_target_pairs={{0,8},{8,0},{16,24},{24,16},{32,40},{40,32},{48,56},{56,48},{64,72... | collective-permute-start | bytes 2359304 | tf_op jit(solution)/shard_map/ppermute | solution.py:139
  63.5 0.8 broadcast_in_dim.18
  64.3 4.1 %all-to-all-start = ((bf16[2,16,12,512]{3,1,2,0:T(8,128)(2,1)}), bf16[2,16,12,512]{3,1,2,0:T(8,128)(2,1)S(1)}, u32[]{:S(2)}, u32[]{:S(2)}) async-start(bf16[2,16,12,512]{3,1,2,0:T(8,128)(2,1)} %broadcast_in_dim.18), calls=%async_computation | async-start | bytes 786432 | tf_op jit(solution)/shard_map/all_to_all | solution.py:127
  68.7 1.3 copy.30
  70.0 6.8 %shard_map.120 = (f32[1024,512]{1,0:T(8,128)}, bf16[4,512]{1,0:T(4,128)(2,1)}, bf16[8,4,1536]{2,1,0:T(4,128)(2,1)}) custom-call(bf16[1024,1536]{1,0:T(8,128)(2,1)} %all-gather.4.cloned.1.call-done.x_ref, bf16[1536,512]{1,0:T(8,128)(2,1)} %bitcast.71, bf16[512,1536]{1,0:T(8,128)(2,1)} %out_ref.1, f32[4,1,1536]{2,1,0:T(1,128)} %copy-done.2), custom_call_target="tpu_custom_call" | custom-call | tf_op jit(solution)/shard_map/pallas_call | solution.py:92
  76.8 5.1 %all-to-all-start.1 = ((bf16[8,4,1536]{2,1,0:T(4,128)(2,1)}), bf16[8,4,1536]{2,1,0:T(4,128)(2,1)S(1)}, u32[]{:S(2)}, u32[]{:S(2)}) async-start(bf16[8,4,1536]{2,1,0:T(4,128)(2,1)} %get-tuple-element.25), calls=%async_computation.1 | async-start | bytes 196608 | tf_op jit(solution)/shard_map/all_to_all | solution.py:128
  84.0 2.8 %collective-permute-start.2 = (bf16[2,16,12,512]{3,1,2,0:T(8,128)(2,1)S(1)}, bf16[2,16,12,512]{3,1,2,0:T(8,128)(2,1)S(1)}, u32[]{:S(2)}, u32[]{:S(2)}) collective-permute-start(bf16[2,16,12,512]{3,1,2,0:T(8,128)(2,1)S(1)} %all-to-all-done), channel_id=1, source_target_pairs={{0,8},{8,0},{16,24},{24,16},{32,40},{40,32},{48,56},{56,48},{64,72... | collective-permute-start | bytes 1179656 | tf_op jit(solution)/shard_map/ppermute | solution.py:139
  86.8 0.5 all-to-all-done.1
  87.6 0.5 collective-permute-done.2
  89.0 0.5 reshape.133
  90.1 1.0 broadcast_in_dim.20
  91.1 5.4 %all-to-all-start.2 = ((bf16[8,32,1536]{2,1,0:T(8,128)(2,1)}), bf16[8,32,1536]{2,1,0:T(8,128)(2,1)}, u32[]{:S(2)}, u32[]{:S(2)}) async-start(bf16[8,32,1536]{2,1,0:T(8,128)(2,1)} %broadcast_in_dim.20), calls=%async_computation.2 | async-start | bytes 1572864 | tf_op jit(solution)/shard_map/all_to_all | solution.py:128
  96.5 1.3 convolution_convert_fusion.2
  97.8 1.7 reshape.135
  99.4 9.0 %all-to-all-done.2 = bf16[8,32,1536]{2,1,0:T(8,128)(2,1)} async-done(((bf16[8,32,1536]{2,1,0:T(8,128)(2,1)}), bf16[8,32,1536]{2,1,0:T(8,128)(2,1)}, u32[]{:S(2)}, u32[]{:S(2)}) %all-to-all-start.2) | async-done | bytes 786464 | tf_op jit(solution)/shard_map/all_to_all | solution.py:128
  108.4 1.3 convert_reduce_fusion
  110.0 0.5 convolution_multiply_fusion.1
  111.0 2.0 fusion.3
  113.4 1.8 convolution_convert_fusion.1
  115.7 6.6 %all_to_all.40 = bf16[2,4,8,40,512]{4,3,2,1,0:T(8,128)(2,1)S(1)} all-to-all(bf16[2,4,8,40,512]{4,3,2,1,0:T(8,128)(2,1)S(1)} %fusion.1), channel_id=1, replica_groups={{0,8},{16,24},{32,40},{48,56},{64,72},{80,88},{96,104},{112,120},{128,1..., dimensions={0} | all-to-all | bytes 5242880 | tf_op jit(solution)/shard_map/all_to_all | solution.py:127
  122.2 1.4 fusion.4
  123.7 4.6 %all-to-all-start.4 = ((bf16[4,8,40,512]{3,2,1,0:T(8,128)(2,1)}), bf16[4,8,40,512]{3,2,1,0:T(8,128)(2,1)S(1)}, u32[]{:S(2)}, u32[]{:S(2)}) async-start(bf16[4,8,40,512]{3,2,1,0:T(8,128)(2,1)} %fusion.4), calls=%async_computation.4 | async-start | bytes 2621440 | tf_op jit(solution)/shard_map/all_to_all | solution.py:127
  128.3 4.7 %convolution_convert_fusion = bf16[1024,1536]{1,0:T(8,128)(2,1)} fusion(bf16[1024,512]{1,0:T(8,128)(2,1)} %copy-done.6, bf16[1536,512]{1,0:T(8,128)(2,1)S(1)} %bitcast.72), kind=kOutput, calls=%fused_computation.2 | convolution fusion | flops 1612185600 | bytes 5767168 | tf_op jit(solution)/shard_map/rf,df->rd/dot_general | solution.py:238
  133.0 12.8 %all-to-all-done.4 = bf16[4,8,40,512]{3,2,1,0:T(8,128)(2,1)S(1)} async-done(((bf16[4,8,40,512]{3,2,1,0:T(8,128)(2,1)}), bf16[4,8,40,512]{3,2,1,0:T(8,128)(2,1)S(1)}, u32[]{:S(2)}, u32[]{:S(2)}) %all-to-all-start.4) | async-done | bytes 1310752 | tf_op jit(solution)/shard_map/all_to_all | solution.py:127
  145.8 0.9 fusion.22
  146.7 8.6 %all-to-all-start.5 = ((bf16[8,40,512]{2,1,0:T(8,128)(2,1)}), bf16[8,40,512]{2,1,0:T(8,128)(2,1)S(1)}, u32[]{:S(2)}, u32[]{:S(2)}) async-start(bf16[8,40,512]{2,1,0:T(8,128)(2,1)} %fusion.22), calls=%async_computation.5 | async-start | bytes 655360 | tf_op jit(solution)/shard_map/all_to_all | solution.py:127
  155.3 3.4 %collective-permute-start.3 = (bf16[4,512]{1,0:T(4,128)(2,1)S(1)}, bf16[4,512]{1,0:T(4,128)(2,1)S(1)}, u32[]{:S(2)}, u32[]{:S(2)}) collective-permute-start(bf16[4,512]{1,0:T(4,128)(2,1)S(1)} %copy-done.9), channel_id=1, source_target_pairs={{0,8},{8,0},{16,24},{24,16},{32,40},{40,32},{48,56},{56,48},{64,72... | collective-permute-start | bytes 12296 | tf_op jit(solution)/shard_map/ppermute | solution.py:139
  158.7 0.8 collective-permute-done.3
  159.5 12.5 %all-to-all-done.5 = bf16[8,40,512]{2,1,0:T(8,128)(2,1)S(1)} async-done(((bf16[8,40,512]{2,1,0:T(8,128)(2,1)}), bf16[8,40,512]{2,1,0:T(8,128)(2,1)S(1)}, u32[]{:S(2)}, u32[]{:S(2)}) %all-to-all-start.5) | async-done | bytes 327712 | tf_op jit(solution)/shard_map/all_to_all | solution.py:127
  172.2 26.0 %all_to_all.41 = bf16[8,32,512]{2,1,0:T(8,128)(2,1)S(1)} all-to-all(bf16[8,32,512]{2,1,0:T(8,128)(2,1)S(1)} %broadcast_in_dim.23), channel_id=1, replica_groups={{0,32,64,96,128,160,192,224},{8,40,72,104,136,168,200,232},{16,48,80,11..., dimensions={0} | all-to-all | bytes 524288 | tf_op jit(solution)/shard_map/all_to_all | solution.py:127
  198.2 1.1 broadcast_in_dim.24
  199.3 5.8 %all-to-all-start.7 = ((bf16[4,8,32,512]{3,2,1,0:T(8,128)(2,1)}), bf16[4,8,32,512]{3,2,1,0:T(8,128)(2,1)S(1)}, u32[]{:S(2)}, u32[]{:S(2)}) async-start(bf16[4,8,32,512]{3,2,1,0:T(8,128)(2,1)} %broadcast_in_dim.24), calls=%async_computation.7 | async-start | bytes 2097152 | tf_op jit(solution)/shard_map/all_to_all | solution.py:127
  205.1 0.7 slice.79
  206.0 1.1 convert.9
  207.8 1.1 fusion.20
  209.0 10.3 %all-to-all-done.7 = bf16[4,8,32,512]{3,2,1,0:T(8,128)(2,1)S(1)} async-done(((bf16[4,8,32,512]{3,2,1,0:T(8,128)(2,1)}), bf16[4,8,32,512]{3,2,1,0:T(8,128)(2,1)S(1)}, u32[]{:S(2)}, u32[]{:S(2)}) %all-to-all-start.7) | async-done | bytes 1048608 | tf_op jit(solution)/shard_map/all_to_all | solution.py:127
  219.3 3.8 %collective-permute-start.4 = (bf16[32,24,512]{2,1,0:T(8,128)(2,1)S(1)}, bf16[32,24,512]{2,1,0:T(8,128)(2,1)S(1)}, u32[]{:S(2)}, u32[]{:S(2)}) collective-permute-start(bf16[32,24,512]{2,1,0:T(8,128)(2,1)S(1)} %slice.76), channel_id=1, source_target_pairs={{0,8},{8,0},{16,24},{24,16},{32,40},{40,32},{48,56},{56,48},{64,72... | collective-permute-start | bytes 2359304 | tf_op jit(solution)/shard_map/ppermute | solution.py:139
  223.3 0.7 fusion.28
  224.0 0.8 convolution_convert_fusion.3
  225.1 1.3 pad_maximum_fusion
  (82 shorter events, 5.5 us)
Async XLA Ops:
  7.2 62.9 %all-gather.4.cloned.1.call-start = ((), (), s32[]{:S(2)}) async-start(), calls=%async_computation.9 | async-start | bytes 3538944 | tf_op jit(solution)/shard_map/all_gather | solution.py:173
  7.2 1.0 copy-start
  9.4 0.6 copy-start.2
  10.0 7.2 %collective-permute-start = (bf16[24,512]{1,0:T(8,128)(2,1)}, bf16[24,512]{1,0:T(8,128)(2,1)S(1)}, u32[]{:S(2)}, u32[]{:S(2)}) collective-permute-start(bf16[24,512]{1,0:T(8,128)(2,1)} %param.9), channel_id=1, source_target_pairs={{0,256},{256,0},{8,264},{264,8},{16,272},{272,16},{24,280},{280,24... | collective-permute-start | bytes 73736 | tf_op jit(solution)/shard_map/ppermute | solution.py:139
  54.4 14.1 %collective-permute-start.1 = (bf16[16,48,512]{2,1,0:T(8,128)(2,1)S(1)}, bf16[16,48,512]{2,1,0:T(8,128)(2,1)S(1)}, u32[]{:S(2)}, u32[]{:S(2)}) collective-permute-start(bf16[16,48,512]{2,1,0:T(8,128)(2,1)S(1)} %slice.65), channel_id=1, source_target_pairs={{0,8},{8,0},{16,24},{24,16},{32,40},{40,32},{48,56},{56,48},{64,72... | collective-permute-start | bytes 2359304 | tf_op jit(solution)/shard_map/ppermute | solution.py:139
  64.3 12.5 %all-to-all-start = ((bf16[2,16,12,512]{3,1,2,0:T(8,128)(2,1)}), bf16[2,16,12,512]{3,1,2,0:T(8,128)(2,1)S(1)}, u32[]{:S(2)}, u32[]{:S(2)}) async-start(bf16[2,16,12,512]{3,1,2,0:T(8,128)(2,1)} %broadcast_in_dim.18), calls=%async_computation | async-start | bytes 786432 | tf_op jit(solution)/shard_map/all_to_all | solution.py:127
  70.0 13.9 %copy-start.8 = (bf16[28,1536]{1,0:T(8,128)(2,1)S(1)}, bf16[28,1536]{1,0:T(8,128)(2,1)}, u32[]{:S(2)}) copy-start(bf16[28,1536]{1,0:T(8,128)(2,1)} %param.11) | copy-start | bytes 258052
  76.8 10.4 %all-to-all-start.1 = ((bf16[8,4,1536]{2,1,0:T(4,128)(2,1)}), bf16[8,4,1536]{2,1,0:T(4,128)(2,1)S(1)}, u32[]{:S(2)}, u32[]{:S(2)}) async-start(bf16[8,4,1536]{2,1,0:T(4,128)(2,1)} %get-tuple-element.25), calls=%async_computation.1 | async-start | bytes 196608 | tf_op jit(solution)/shard_map/all_to_all | solution.py:128
  84.0 4.1 %collective-permute-start.2 = (bf16[2,16,12,512]{3,1,2,0:T(8,128)(2,1)S(1)}, bf16[2,16,12,512]{3,1,2,0:T(8,128)(2,1)S(1)}, u32[]{:S(2)}, u32[]{:S(2)}) collective-permute-start(bf16[2,16,12,512]{3,1,2,0:T(8,128)(2,1)S(1)} %all-to-all-done), channel_id=1, source_target_pairs={{0,8},{8,0},{16,24},{24,16},{32,40},{40,32},{48,56},{56,48},{64,72... | collective-permute-start | bytes 1179656 | tf_op jit(solution)/shard_map/ppermute | solution.py:139
  91.1 17.3 %all-to-all-start.2 = ((bf16[8,32,1536]{2,1,0:T(8,128)(2,1)}), bf16[8,32,1536]{2,1,0:T(8,128)(2,1)}, u32[]{:S(2)}, u32[]{:S(2)}) async-start(bf16[8,32,1536]{2,1,0:T(8,128)(2,1)} %broadcast_in_dim.20), calls=%async_computation.2 | async-start | bytes 1572864 | tf_op jit(solution)/shard_map/all_to_all | solution.py:128
  97.8 12.2 %copy-start.3 = (bf16[512,1536]{1,0:T(8,128)(2,1)S(1)}, bf16[512,1536]{1,0:T(8,128)(2,1)}, u32[]{:S(2)}) copy-start(bf16[512,1536]{1,0:T(8,128)(2,1)} %out_ref.1) | copy-start | bytes 4718596
  110.9 2.5 %copy-start.5 = (bf16[1024,1536]{1,0:T(8,128)(2,1)S(1)}, bf16[1024,1536]{1,0:T(8,128)(2,1)}, u32[]{:S(2)}) copy-start(bf16[1024,1536]{1,0:T(8,128)(2,1)} %all-gather.4.cloned.1.call-done.x_ref) | copy-start | bytes 9437188
  113.4 1.8 copy-start.6
  123.7 4.7 %copy-start.4 = (bf16[2,16,2,24,512]{4,3,2,1,0:T(8,128)(2,1)S(1)}, bf16[2,16,2,24,512]{4,3,2,1,0:T(8,128)(2,1)}, u32[]{:S(2)}) copy-start(bf16[2,16,2,24,512]{4,3,2,1,0:T(8,128)(2,1)} %copy.30) | copy-start | bytes 4718596
  123.7 22.1 %all-to-all-start.4 = ((bf16[4,8,40,512]{3,2,1,0:T(8,128)(2,1)}), bf16[4,8,40,512]{3,2,1,0:T(8,128)(2,1)S(1)}, u32[]{:S(2)}, u32[]{:S(2)}) async-start(bf16[4,8,40,512]{3,2,1,0:T(8,128)(2,1)} %fusion.4), calls=%async_computation.4 | async-start | bytes 2621440 | tf_op jit(solution)/shard_map/all_to_all | solution.py:127
  128.3 77.7 %reduce-scatter.2.cloned.1.call-start = ((), (), s32[]{:S(2)}) async-start(), calls=%async_computation.10 | async-start | bytes 3538944 | tf_op jit(solution)/shard_map/reduce_scatter | solution.py:243
  146.7 8.6 %copy-start.9 = (bf16[4,512]{1,0:T(4,128)(2,1)S(1)}, bf16[4,512]{1,0:T(4,128)(2,1)}, u32[]{:S(2)}) copy-start(bf16[4,512]{1,0:T(4,128)(2,1)} %get-tuple-element.29) | copy-start | bytes 12292
  146.7 25.4 %all-to-all-start.5 = ((bf16[8,40,512]{2,1,0:T(8,128)(2,1)}), bf16[8,40,512]{2,1,0:T(8,128)(2,1)S(1)}, u32[]{:S(2)}, u32[]{:S(2)}) async-start(bf16[8,40,512]{2,1,0:T(8,128)(2,1)} %fusion.22), calls=%async_computation.5 | async-start | bytes 655360 | tf_op jit(solution)/shard_map/all_to_all | solution.py:127
  155.3 4.2 %collective-permute-start.3 = (bf16[4,512]{1,0:T(4,128)(2,1)S(1)}, bf16[4,512]{1,0:T(4,128)(2,1)S(1)}, u32[]{:S(2)}, u32[]{:S(2)}) collective-permute-start(bf16[4,512]{1,0:T(4,128)(2,1)S(1)} %copy-done.9), channel_id=1, source_target_pairs={{0,8},{8,0},{16,24},{24,16},{32,40},{40,32},{48,56},{56,48},{64,72... | collective-permute-start | bytes 12296 | tf_op jit(solution)/shard_map/ppermute | solution.py:139
  199.3 7.8 %copy-start.1 = (bf16[4,32,1536]{2,1,0:T(8,128)(2,1)S(1)}, bf16[4,32,1536]{2,1,0:T(8,128)(2,1)}, u32[]{:S(2)}) copy-start(bf16[4,32,1536]{2,1,0:T(8,128)(2,1)} %x_ref.1) | copy-start | bytes 1179652
  199.3 20.0 %all-to-all-start.7 = ((bf16[4,8,32,512]{3,2,1,0:T(8,128)(2,1)}), bf16[4,8,32,512]{3,2,1,0:T(8,128)(2,1)S(1)}, u32[]{:S(2)}, u32[]{:S(2)}) async-start(bf16[4,8,32,512]{3,2,1,0:T(8,128)(2,1)} %broadcast_in_dim.24), calls=%async_computation.7 | async-start | bytes 2097152 | tf_op jit(solution)/shard_map/all_to_all | solution.py:127
  207.5 15.6 %copy-start.7 = (bf16[4,1536]{1,0:T(4,128)(2,1)S(1)}, bf16[4,1536]{1,0:T(4,128)(2,1)}, u32[]{:S(2)}) copy-start(bf16[4,1536]{1,0:T(4,128)(2,1)} %param.12) | copy-start | bytes 36868
  219.3 5.7 %collective-permute-start.4 = (bf16[32,24,512]{2,1,0:T(8,128)(2,1)S(1)}, bf16[32,24,512]{2,1,0:T(8,128)(2,1)S(1)}, u32[]{:S(2)}, u32[]{:S(2)}) collective-permute-start(bf16[32,24,512]{2,1,0:T(8,128)(2,1)S(1)} %slice.76), channel_id=1, source_target_pairs={{0,8},{8,0},{16,24},{24,16},{32,40},{40,32},{48,56},{56,48},{64,72... | collective-permute-start | bytes 2359304 | tf_op jit(solution)/shard_map/ppermute | solution.py:139
Sparse Core Ops, SparseCore 0:
  10.7 54.5 all-gather.3
  146.8 46.4 reduce-scatter.1

commit v8 on v6

--- a/solution.py
+++ b/solution.py
@@ -184,10 +184,10 @@
         (first_row, zero_index),
     )
     slope, act_mean, part_pool = hidden_layer(flat, full_in, out_weight, totals, local_patches)
-    part_pool, texts = lax.optimization_barrier((part_pool, texts))
     texts = jnp.transpose(texts.reshape(4, 8, 2, text_rows, hidden_width), (0, 2, 1, 3, 4))
     texts = texts.reshape(dp_count * text_count, width_model)
-    pooled = jnp.sum(exchange(part_pool, "mp").astype(jnp.float32), 0)
+    pooled_parts, texts = lax.optimization_barrier((exchange(part_pool, "mp"), texts))
+    pooled = jnp.sum(pooled_parts.astype(jnp.float32), 0)
     images = jnp.concatenate([pooled, image_rest.astype(jnp.float32)], 0)
     image_unit, image_inv = unit_rows(images)
     image_low = image_unit.astype(jnp.bfloat16)

time: 232 us -> 232 us (level)
  no operation moved by 1% of the time
where the time goes in v8:
time: 232 us; the launch traced here: 231 us
  blocking collectives  72.4 us (31%)
  starting transfers between devices  50.9 us (22%)
  waiting for transfers between devices  47.1 us (20%)
  between operations  16.5 us (7%)
  other arithmetic  15.7 us (7%)
  local copies, waits for them, and re-layouts  11 us (5%)
  matrix products  9.7 us (4%)
  Pallas kernels  7.95 us (3%)
    all_to_all x4, waiting for transfers between devices, exchange(): lax.all_to_all(blocks, 'dp', 0, 0, axis_index_groups=GROUPS[axis], tiled=...  38.5 us
    all_gather x1, blocking collectives, gather_z(): lax.all_gather(block, 'dp', axis=0, axis_index_groups=GROUPS['z'], tiled=...  36.3 us
    all_to_all x2, blocking collectives, exchange(): lax.all_to_all(blocks, 'dp', 0, 0, axis_index_groups=GROUPS[axis], tiled=...  36.1 us
    ppermute x4, starting transfers between devices, pair(): lax.ppermute(block, 'dp', [p for a, b in GROUPS[axis] for p in ((a, b), (...  21.7 us
    all_to_all x4, starting transfers between devices, exchange(): lax.all_to_all(blocks, 'dp', 0, 0, axis_index_groups=GROUPS[axis], tiled=...  20.2 us
    all_to_all x2, starting transfers between devices, exchange(): return lax.all_to_all(blocks, axis, 0, 0, tiled=True)  8.96 us
    all_to_all x2, waiting for transfers between devices, exchange(): return lax.all_to_all(blocks, axis, 0, 0, tiled=True)  7.56 us
    pallas_call x1, Pallas kernels, hidden_layer(): pl.pallas_call(functools.partial(hidden_kernel, rows, patches), grid=(tok...  6.79 us
  transfers between devices with their start and end apart: 12, of which 8 were waited for; matrix products, arithmetic and copies ran while one was open for 10% of the time, Pallas kernels for 3%

profile of v8, /device:TPU:1, one launch (start us, length us, event | category | flops | bytes accessed | tf_op | source)
XLA Modules:
  0.0 231.2 jit_solution(10461219219727445812)
XLA Ops:
  7.2 1.0 copy-done
  8.2 1.2 shard_map.119
  9.4 0.6 copy-done.2
  10.0 5.5 %collective-permute-start = (bf16[24,512]{1,0:T(8,128)(2,1)}, bf16[24,512]{1,0:T(8,128)(2,1)S(1)}, u32[]{:S(2)}, u32[]{:S(2)}) collective-permute-start(bf16[24,512]{1,0:T(8,128)(2,1)} %param.9), channel_id=1, source_target_pairs={{0,256},{256,0},{8,264},{264,8},{16,272},{272,16},{24,280},{280,24... | collective-permute-start | bytes 73736 | tf_op jit(solution)/shard_map/ppermute | solution.py:139
  15.5 0.8 fusion.29
  16.4 0.8 convert_dynamic-update-slice_fusion
  17.2 0.7 select_bitcast_fusion.3
  18.0 36.3 %all-gather.1 = bf16[16,60,512]{2,1,0:T(8,128)(2,1)S(1)} all-gather(bf16[1,60,512]{2,1,0:T(8,128)(2,1)S(1)} %maximum_bitcast_fusion.1), channel_id=2, replica_groups={{0,16,32,48,64,80,96,112,128,144,160,176,192,208,224,240},{8,24,40,56,7..., dimensions={0}, use_global_device_ids=true | all-gather | bytes 1044480 | tf_op jit(solution)/shard_map/all_gather | solution.py:148
  54.4 9.0 %collective-permute-start.1 = (bf16[16,48,512]{2,1,0:T(8,128)(2,1)S(1)}, bf16[16,48,512]{2,1,0:T(8,128)(2,1)}, u32[]{:S(2)}, u32[]{:S(2)}) collective-permute-start(bf16[16,48,512]{2,1,0:T(8,128)(2,1)S(1)} %slice.65), channel_id=1, source_target_pairs={{0,8},{8,0},{16,24},{24,16},{32,40},{40,32},{48,56},{56,48},{64,72... | collective-permute-start | bytes 2359304 | tf_op jit(solution)/shard_map/ppermute | solution.py:139
  63.5 1.0 broadcast_in_dim.18
  64.5 4.5 %all-to-all-start.1 = ((bf16[4,16,12,512]{3,1,2,0:T(8,128)(2,1)}), bf16[4,16,12,512]{3,1,2,0:T(8,128)(2,1)S(1)}, u32[]{:S(2)}, u32[]{:S(2)}) async-start(bf16[4,16,12,512]{3,1,2,0:T(8,128)(2,1)} %broadcast_in_dim.18), calls=%async_computation.1 | async-start | bytes 1572864 | tf_op jit(solution)/shard_map/all_to_all | solution.py:127
  69.0 1.2 broadcast_select_fusion.1
  70.4 1.3 copy.37
  71.7 6.8 %shard_map.120 = (f32[1024,512]{1,0:T(8,128)}, bf16[4,512]{1,0:T(4,128)(2,1)}, bf16[8,4,1536]{2,1,0:T(4,128)(2,1)}) custom-call(bf16[1024,1536]{1,0:T(8,128)(2,1)} %all-gather.4.cloned.1.call-done.x_ref, bf16[1536,512]{1,0:T(8,128)(2,1)} %bitcast.65, bf16[512,1536]{1,0:T(8,128)(2,1)} %out_ref.1, f32[4,1,1536]{2,1,0:T(1,128)} %copy-done.2), custom_call_target="tpu_custom_call" | custom-call | tf_op jit(solution)/shard_map/pallas_call | solution.py:92
  78.5 2.8 %all-to-all-done.1 = bf16[4,16,12,512]{3,1,2,0:T(8,128)(2,1)S(1)} async-done(((bf16[4,16,12,512]{3,1,2,0:T(8,128)(2,1)}), bf16[4,16,12,512]{3,1,2,0:T(8,128)(2,1)S(1)}, u32[]{:S(2)}, u32[]{:S(2)}) %all-to-all-start.1) | async-done | bytes 786464 | tf_op jit(solution)/shard_map/all_to_all | solution.py:127
  81.3 4.8 %all-to-all-start = ((bf16[8,4,1536]{2,1,0:T(4,128)(2,1)}), bf16[8,4,1536]{2,1,0:T(4,128)(2,1)S(1)}, u32[]{:S(2)}, u32[]{:S(2)}) async-start(bf16[8,4,1536]{2,1,0:T(4,128)(2,1)} %get-tuple-element.24), calls=%async_computation | async-start | bytes 196608 | tf_op jit(solution)/shard_map/all_to_all | solution.py:128
  88.1 0.6 copy.39
  89.4 1.9 all-to-all-done
  92.2 1.0 broadcast_in_dim.20
  93.2 4.2 %all-to-all-start.2 = ((bf16[8,32,1536]{2,1,0:T(8,128)(2,1)}), bf16[8,32,1536]{2,1,0:T(8,128)(2,1)}, u32[]{:S(2)}, u32[]{:S(2)}) async-start(bf16[8,32,1536]{2,1,0:T(8,128)(2,1)} %broadcast_in_dim.20), calls=%async_computation.2 | async-start | bytes 1572864 | tf_op jit(solution)/shard_map/all_to_all | solution.py:128
  97.5 1.3 convolution_convert_fusion.2
  98.7 1.7 reshape.135
  100.4 5.6 %all-to-all-done.2 = bf16[8,32,1536]{2,1,0:T(8,128)(2,1)} async-done(((bf16[8,32,1536]{2,1,0:T(8,128)(2,1)}), bf16[8,32,1536]{2,1,0:T(8,128)(2,1)}, u32[]{:S(2)}, u32[]{:S(2)}) %all-to-all-start.2) | async-done | bytes 786464 | tf_op jit(solution)/shard_map/all_to_all | solution.py:128
  106.0 1.3 convert_reduce_fusion
  107.6 0.5 convolution_multiply_fusion.1
  108.6 2.0 fusion.3
  111.0 1.8 convolution_convert_fusion.1
  113.3 10.1 %all_to_all.40 = bf16[2,4,8,40,512]{4,3,2,1,0:T(8,128)(2,1)S(1)} all-to-all(bf16[2,4,8,40,512]{4,3,2,1,0:T(8,128)(2,1)S(1)} %fusion.1), channel_id=1, replica_groups={{0,8},{16,24},{32,40},{48,56},{64,72},{80,88},{96,104},{112,120},{128,1..., dimensions={0} | all-to-all | bytes 5242880 | tf_op jit(solution)/shard_map/all_to_all | solution.py:127
  123.4 1.4 fusion.4
  124.8 3.7 %all-to-all-start.4 = ((bf16[4,8,40,512]{3,2,1,0:T(8,128)(2,1)}), bf16[4,8,40,512]{3,2,1,0:T(8,128)(2,1)S(1)}, u32[]{:S(2)}, u32[]{:S(2)}) async-start(bf16[4,8,40,512]{3,2,1,0:T(8,128)(2,1)} %fusion.4), calls=%async_computation.4 | async-start | bytes 2621440 | tf_op jit(solution)/shard_map/all_to_all | solution.py:127
  128.6 4.7 %convolution_convert_fusion = bf16[1024,1536]{1,0:T(8,128)(2,1)} fusion(bf16[1024,512]{1,0:T(8,128)(2,1)} %copy-done.6, bf16[1536,512]{1,0:T(8,128)(2,1)S(1)} %bitcast.66), kind=kOutput, calls=%fused_computation.2 | convolution fusion | flops 1612185600 | bytes 5767168 | tf_op jit(solution)/shard_map/rf,df->rd/dot_general | solution.py:237
  133.3 12.9 %all-to-all-done.4 = bf16[4,8,40,512]{3,2,1,0:T(8,128)(2,1)S(1)} async-done(((bf16[4,8,40,512]{3,2,1,0:T(8,128)(2,1)}), bf16[4,8,40,512]{3,2,1,0:T(8,128)(2,1)S(1)}, u32[]{:S(2)}, u32[]{:S(2)}) %all-to-all-start.4) | async-done | bytes 1310752 | tf_op jit(solution)/shard_map/all_to_all | solution.py:127
  146.1 0.9 fusion.22
  147.1 6.2 %all-to-all-start.5 = ((bf16[8,40,512]{2,1,0:T(8,128)(2,1)}), bf16[8,40,512]{2,1,0:T(8,128)(2,1)S(1)}, u32[]{:S(2)}, u32[]{:S(2)}) async-start(bf16[8,40,512]{2,1,0:T(8,128)(2,1)} %fusion.22), calls=%async_computation.5 | async-start | bytes 655360 | tf_op jit(solution)/shard_map/all_to_all | solution.py:127
  153.3 3.4 %collective-permute-start.2 = (bf16[4,512]{1,0:T(4,128)(2,1)S(1)}, bf16[4,512]{1,0:T(4,128)(2,1)S(1)}, u32[]{:S(2)}, u32[]{:S(2)}) collective-permute-start(bf16[4,512]{1,0:T(4,128)(2,1)S(1)} %copy-done.9), channel_id=1, source_target_pairs={{0,8},{8,0},{16,24},{24,16},{32,40},{40,32},{48,56},{56,48},{64,72... | collective-permute-start | bytes 12296 | tf_op jit(solution)/shard_map/ppermute | solution.py:139
  156.7 0.8 collective-permute-done.2
  157.6 12.5 %all-to-all-done.5 = bf16[8,40,512]{2,1,0:T(8,128)(2,1)S(1)} async-done(((bf16[8,40,512]{2,1,0:T(8,128)(2,1)}), bf16[8,40,512]{2,1,0:T(8,128)(2,1)S(1)}, u32[]{:S(2)}, u32[]{:S(2)}) %all-to-all-start.5) | async-done | bytes 327712 | tf_op jit(solution)/shard_map/all_to_all | solution.py:127
  170.2 26.0 %all_to_all.41 = bf16[8,32,512]{2,1,0:T(8,128)(2,1)S(1)} all-to-all(bf16[8,32,512]{2,1,0:T(8,128)(2,1)S(1)} %broadcast_in_dim.23), channel_id=1, replica_groups={{0,32,64,96,128,160,192,224},{8,40,72,104,136,168,200,232},{16,48,80,11..., dimensions={0} | all-to-all | bytes 524288 | tf_op jit(solution)/shard_map/all_to_all | solution.py:127
  196.2 1.1 broadcast_in_dim.24
  197.3 5.8 %all-to-all-start.7 = ((bf16[4,8,32,512]{3,2,1,0:T(8,128)(2,1)}), bf16[4,8,32,512]{3,2,1,0:T(8,128)(2,1)S(1)}, u32[]{:S(2)}, u32[]{:S(2)}) async-start(bf16[4,8,32,512]{3,2,1,0:T(8,128)(2,1)} %broadcast_in_dim.24), calls=%async_computation.7 | async-start | bytes 2097152 | tf_op jit(solution)/shard_map/all_to_all | solution.py:127
  203.1 0.7 slice.79
  204.0 1.1 convert.9
  205.9 1.1 fusion.20
  207.0 10.3 %all-to-all-done.7 = bf16[4,8,32,512]{3,2,1,0:T(8,128)(2,1)S(1)} async-done(((bf16[4,8,32,512]{3,2,1,0:T(8,128)(2,1)}), bf16[4,8,32,512]{3,2,1,0:T(8,128)(2,1)S(1)}, u32[]{:S(2)}, u32[]{:S(2)}) %all-to-all-start.7) | async-done | bytes 1048608 | tf_op jit(solution)/shard_map/all_to_all | solution.py:127
  217.3 3.8 %collective-permute-start.3 = (bf16[32,24,512]{2,1,0:T(8,128)(2,1)S(1)}, bf16[32,24,512]{2,1,0:T(8,128)(2,1)S(1)}, u32[]{:S(2)}, u32[]{:S(2)}) collective-permute-start(bf16[32,24,512]{2,1,0:T(8,128)(2,1)S(1)} %slice.76), channel_id=1, source_target_pairs={{0,8},{8,0},{16,24},{24,16},{32,40},{40,32},{48,56},{56,48},{64,72... | collective-permute-start | bytes 2359304 | tf_op jit(solution)/shard_map/ppermute | solution.py:139
  221.3 0.7 fusion.28
  222.0 0.8 convolution_convert_fusion.3
  223.1 1.3 pad_maximum_fusion
  (78 shorter events, 5.3 us)
Async XLA Ops:
  7.2 64.6 %all-gather.4.cloned.1.call-start = ((), (), s32[]{:S(2)}) async-start(), calls=%async_computation.9 | async-start | bytes 3538944 | tf_op jit(solution)/shard_map/all_gather | solution.py:173
  7.2 1.0 copy-start
  9.4 0.6 copy-start.2
  10.0 7.2 %collective-permute-start = (bf16[24,512]{1,0:T(8,128)(2,1)}, bf16[24,512]{1,0:T(8,128)(2,1)S(1)}, u32[]{:S(2)}, u32[]{:S(2)}) collective-permute-start(bf16[24,512]{1,0:T(8,128)(2,1)} %param.9), channel_id=1, source_target_pairs={{0,256},{256,0},{8,264},{264,8},{16,272},{272,16},{24,280},{280,24... | collective-permute-start | bytes 73736 | tf_op jit(solution)/shard_map/ppermute | solution.py:139
  54.4 14.6 %collective-permute-start.1 = (bf16[16,48,512]{2,1,0:T(8,128)(2,1)S(1)}, bf16[16,48,512]{2,1,0:T(8,128)(2,1)}, u32[]{:S(2)}, u32[]{:S(2)}) collective-permute-start(bf16[16,48,512]{2,1,0:T(8,128)(2,1)S(1)} %slice.65), channel_id=1, source_target_pairs={{0,8},{8,0},{16,24},{24,16},{32,40},{40,32},{48,56},{56,48},{64,72... | collective-permute-start | bytes 2359304 | tf_op jit(solution)/shard_map/ppermute | solution.py:139
  64.5 16.8 %all-to-all-start.1 = ((bf16[4,16,12,512]{3,1,2,0:T(8,128)(2,1)}), bf16[4,16,12,512]{3,1,2,0:T(8,128)(2,1)S(1)}, u32[]{:S(2)}, u32[]{:S(2)}) async-start(bf16[4,16,12,512]{3,1,2,0:T(8,128)(2,1)} %broadcast_in_dim.18), calls=%async_computation.1 | async-start | bytes 1572864 | tf_op jit(solution)/shard_map/all_to_all | solution.py:127
  71.7 16.3 %copy-start.8 = (bf16[28,1536]{1,0:T(8,128)(2,1)S(1)}, bf16[28,1536]{1,0:T(8,128)(2,1)}, u32[]{:S(2)}) copy-start(bf16[28,1536]{1,0:T(8,128)(2,1)} %param.11) | copy-start | bytes 258052
  81.3 10.0 %all-to-all-start = ((bf16[8,4,1536]{2,1,0:T(4,128)(2,1)}), bf16[8,4,1536]{2,1,0:T(4,128)(2,1)S(1)}, u32[]{:S(2)}, u32[]{:S(2)}) async-start(bf16[8,4,1536]{2,1,0:T(4,128)(2,1)} %get-tuple-element.24), calls=%async_computation | async-start | bytes 196608 | tf_op jit(solution)/shard_map/all_to_all | solution.py:128
  93.2 12.8 %all-to-all-start.2 = ((bf16[8,32,1536]{2,1,0:T(8,128)(2,1)}), bf16[8,32,1536]{2,1,0:T(8,128)(2,1)}, u32[]{:S(2)}, u32[]{:S(2)}) async-start(bf16[8,32,1536]{2,1,0:T(8,128)(2,1)} %broadcast_in_dim.20), calls=%async_computation.2 | async-start | bytes 1572864 | tf_op jit(solution)/shard_map/all_to_all | solution.py:128
  98.7 8.9 %copy-start.3 = (bf16[512,1536]{1,0:T(8,128)(2,1)S(1)}, bf16[512,1536]{1,0:T(8,128)(2,1)}, u32[]{:S(2)}) copy-start(bf16[512,1536]{1,0:T(8,128)(2,1)} %out_ref.1) | copy-start | bytes 4718596
  108.5 2.5 %copy-start.5 = (bf16[1024,1536]{1,0:T(8,128)(2,1)S(1)}, bf16[1024,1536]{1,0:T(8,128)(2,1)}, u32[]{:S(2)}) copy-start(bf16[1024,1536]{1,0:T(8,128)(2,1)} %all-gather.4.cloned.1.call-done.x_ref) | copy-start | bytes 9437188
  111.0 1.8 copy-start.6
  124.8 3.7 %copy-start.4 = (bf16[2,16,2,24,512]{4,3,2,1,0:T(8,128)(2,1)S(1)}, bf16[2,16,2,24,512]{4,3,2,1,0:T(8,128)(2,1)}, u32[]{:S(2)}) copy-start(bf16[2,16,2,24,512]{4,3,2,1,0:T(8,128)(2,1)} %copy.37) | copy-start | bytes 4718596
  124.8 21.3 %all-to-all-start.4 = ((bf16[4,8,40,512]{3,2,1,0:T(8,128)(2,1)}), bf16[4,8,40,512]{3,2,1,0:T(8,128)(2,1)S(1)}, u32[]{:S(2)}, u32[]{:S(2)}) async-start(bf16[4,8,40,512]{3,2,1,0:T(8,128)(2,1)} %fusion.4), calls=%async_computation.4 | async-start | bytes 2621440 | tf_op jit(solution)/shard_map/all_to_all | solution.py:127
  128.5 75.5 %reduce-scatter.2.cloned.1.call-start = ((), (), s32[]{:S(2)}) async-start(), calls=%async_computation.10 | async-start | bytes 3538944 | tf_op jit(solution)/shard_map/reduce_scatter | solution.py:242
  147.0 6.3 %copy-start.9 = (bf16[4,512]{1,0:T(4,128)(2,1)S(1)}, bf16[4,512]{1,0:T(4,128)(2,1)}, u32[]{:S(2)}) copy-start(bf16[4,512]{1,0:T(4,128)(2,1)} %get-tuple-element.29) | copy-start | bytes 12292
  147.1 23.0 %all-to-all-start.5 = ((bf16[8,40,512]{2,1,0:T(8,128)(2,1)}), bf16[8,40,512]{2,1,0:T(8,128)(2,1)S(1)}, u32[]{:S(2)}, u32[]{:S(2)}) async-start(bf16[8,40,512]{2,1,0:T(8,128)(2,1)} %fusion.22), calls=%async_computation.5 | async-start | bytes 655360 | tf_op jit(solution)/shard_map/all_to_all | solution.py:127
  153.3 4.2 %collective-permute-start.2 = (bf16[4,512]{1,0:T(4,128)(2,1)S(1)}, bf16[4,512]{1,0:T(4,128)(2,1)S(1)}, u32[]{:S(2)}, u32[]{:S(2)}) collective-permute-start(bf16[4,512]{1,0:T(4,128)(2,1)S(1)} %copy-done.9), channel_id=1, source_target_pairs={{0,8},{8,0},{16,24},{24,16},{32,40},{40,32},{48,56},{56,48},{64,72... | collective-permute-start | bytes 12296 | tf_op jit(solution)/shard_map/ppermute | solution.py:139
  197.3 7.8 %copy-start.1 = (bf16[4,32,1536]{2,1,0:T(8,128)(2,1)S(1)}, bf16[4,32,1536]{2,1,0:T(8,128)(2,1)}, u32[]{:S(2)}) copy-start(bf16[4,32,1536]{2,1,0:T(8,128)(2,1)} %x_ref.1) | copy-start | bytes 1179652
  197.3 20.0 %all-to-all-start.7 = ((bf16[4,8,32,512]{3,2,1,0:T(8,128)(2,1)}), bf16[4,8,32,512]{3,2,1,0:T(8,128)(2,1)S(1)}, u32[]{:S(2)}, u32[]{:S(2)}) async-start(bf16[4,8,32,512]{3,2,1,0:T(8,128)(2,1)} %broadcast_in_dim.24), calls=%async_computation.7 | async-start | bytes 2097152 | tf_op jit(solution)/shard_map/all_to_all | solution.py:127
  205.5 15.6 %copy-start.7 = (bf16[4,1536]{1,0:T(4,128)(2,1)S(1)}, bf16[4,1536]{1,0:T(4,128)(2,1)}, u32[]{:S(2)}) copy-start(bf16[4,1536]{1,0:T(4,128)(2,1)} %param.12) | copy-start | bytes 36868
  217.3 5.7 %collective-permute-start.3 = (bf16[32,24,512]{2,1,0:T(8,128)(2,1)S(1)}, bf16[32,24,512]{2,1,0:T(8,128)(2,1)S(1)}, u32[]{:S(2)}, u32[]{:S(2)}) collective-permute-start(bf16[32,24,512]{2,1,0:T(8,128)(2,1)S(1)} %slice.76), channel_id=1, source_target_pairs={{0,8},{8,0},{16,24},{24,16},{32,40},{40,32},{48,56},{56,48},{64,72... | collective-permute-start | bytes 2359304 | tf_op jit(solution)/shard_map/ppermute | solution.py:139
Sparse Core Ops, SparseCore 0:
  10.7 54.5 all-gather.3
  147.2 43.4 reduce-scatter.1
